TPU v7x, 256 devices: a whole 4x4x8 slice. The times are simulated.
256 devices in a mesh: row: 16 (over x, z_lo, core), col: 16 (over z_hi, y).
Axes of the slice: x: 4, y: 4, z: 8 (z_hi: 4, z_lo: 2; z = z_hi * 2 + z_lo), core: 2. Of those that a mesh axis runs over, the one named last changes fastest.
Arguments:
- amps: bfloat16 [16, 16, 16, 4096], P('row', 'col'), may hold values from -6 to 6
- source: bfloat16 [16, 16, 16, 4096], P('row', 'col'), may hold values from -6 to 6
- factors: bfloat16 [16, 1024, 1024], P(None, ('row', 'col')), may hold values from -0.09375 to 0.09375
- screen: int32 [16, 8, 8], replicated, may hold values from 0 to 1, as said below
- occ_energy: float32 [4], replicated, may hold values from -1.5 to -0.3
- vir_energy: float32 [1024], replicated, may hold values from 0.2 to 2.5
Outputs:
- new_amps: bfloat16 [16, 16, 16, 4096], P('row', 'col')
Inputs may be any that keep to these rules, and one draw needn't show every extreme that they name: screen[i * 4 + j, A, B] equals screen[j * 4 + i, B, A].
All inputs are finite; a program needn't handle non-finite values.
Results may differ from a plain program's by a relative error of at most 0.012.
Values may be sent and summed in bfloat16 or wider, within the bound.
No kernel may reach another device: no remote copies, remote signals or barrier semaphores. Data moves between devices by JAX's collectives and lax.ppermute only.
A program may use at most 192 MiB of HBM per device.

v0:
```python
import jax
import jax.numpy as jnp
from jax import lax
from jax.sharding import PartitionSpec as P


def to_col_major(array, dim, row_count, col_count):
    old_shape = array.shape
    group_len = old_shape[dim] // (row_count * col_count)
    divided = array.reshape(
        old_shape[:dim] + (row_count, col_count, group_len) + old_shape[dim + 1 :]
    )
    return jnp.swapaxes(divided, dim, dim + 1).reshape(old_shape)


def ladder_over_aux(running, segment, left_part, right_factor):

    def step(total, factor_pair):
        left_one, right_one = factor_pair
        inner_part = jnp.einsum(
            "pcd,bd->pcb", segment, right_one, preferred_element_type=jnp.float32
        ).astype(jnp.bfloat16)
        return (
            total
            + jnp.einsum("ac,pcb->pab", left_one, inner_part, preferred_element_type=jnp.float32),
            None,
        )

    result, unused = lax.scan(step, running, (left_part, right_factor))
    return result


def shards(amps, source, factors, screen, occ_energy, vir_energy):
    row_count = lax.axis_size("row")
    col_count = lax.axis_size("col")
    row_id = lax.axis_index("row")
    col_id = lax.axis_index("col")
    pair_count = amps.shape[2]
    aux_count, group_size, virt_count = factors.shape
    a_local = col_count * group_size
    b_local = row_count * group_size
    occ_count = occ_energy.shape[0]
    block_count = screen.shape[1]
    block_size = virt_count // block_count
    a_index = row_id * a_local + jnp.arange(a_local)
    b_position = jnp.arange(b_local)
    b_index = b_position // group_size * a_local + col_id * group_size + b_position % group_size
    block_ids = jnp.arange(block_count)
    select_rows = (a_index[:, None] // block_size == block_ids[None, :]).astype(jnp.float32)
    select_cols = (b_index[:, None] // block_size == block_ids[None, :]).astype(jnp.float32)
    mask_tile = jnp.einsum("pxy,ax,by->pab", screen.astype(jnp.float32), select_rows, select_cols)
    amp_tile = amps.reshape(pair_count, a_local, b_local)
    masked = (amp_tile * mask_tile).astype(jnp.bfloat16)
    share_rows = lax.all_to_all(factors, "row", split_axis=0, concat_axis=1, tiled=True)
    col_ordered = lax.all_gather(share_rows, "col", axis=1, tiled=True)
    left_factor = to_col_major(col_ordered, 1, col_count, row_count)
    right_factor = to_col_major(col_ordered, 2, row_count, col_count)
    mine = lax.all_to_all(masked, "col", split_axis=0, concat_axis=2, tiled=True)
    initial = jnp.zeros((mine.shape[0], virt_count, virt_count), jnp.float32)
    ladder_sum = ladder_over_aux(
        initial, lax.all_gather(mine, "row", axis=1, tiled=True), left_factor, right_factor
    )
    reduced = lax.psum_scatter(
        ladder_sum.astype(jnp.bfloat16), "row", scatter_dimension=1, tiled=True
    ).astype(jnp.float32)
    ladder = lax.all_to_all(
        reduced.astype(jnp.bfloat16), "col", split_axis=2, concat_axis=0, tiled=True
    ).astype(reduced.dtype)
    resid = source.reshape(pair_count, a_local, b_local).astype(jnp.float32) + ladder
    split_tile = resid.reshape(pair_count, col_count, group_size, row_count, group_size)
    received = lax.all_to_all(
        lax.all_to_all(
            split_tile.astype(jnp.bfloat16), "row", split_axis=3, concat_axis=3, tiled=True
        ),
        "col",
        split_axis=1,
        concat_axis=1,
        tiled=True,
    ).astype(split_tile.dtype)
    swapped = received.transpose(0, 1, 4, 3, 2).reshape(occ_count, occ_count, a_local, b_local)
    swapped = swapped.transpose(1, 0, 2, 3).reshape(pair_count, a_local, b_local)
    rsym = resid + swapped
    occ_pair = (occ_energy[:, None] + occ_energy[None, :]).reshape(pair_count)
    vir_rows = lax.dynamic_slice_in_dim(vir_energy, row_id * a_local, a_local)
    vir_cols = lax.dynamic_slice_in_dim(
        vir_energy.reshape(row_count, col_count, group_size), col_id, 1, 1
    ).reshape(b_local)
    denominator = occ_pair[:, None, None] - vir_rows[None, :, None] - vir_cols[None, None, :]
    updated = mask_tile * (amp_tile.astype(jnp.float32) + rsym / denominator)
    return updated.astype(jnp.bfloat16).reshape(1, 1, pair_count, a_local * b_local)


def solution(mesh):
    in_specs = (
        P("row", "col", None, None),
        P("row", "col", None, None),
        P(None, ("row", "col"), None),
        P(),
        P(),
        P(),
    )
    out_specs = P("row", "col", None, None)
    return jax.shard_map(shards, mesh=mesh, in_specs=in_specs, out_specs=out_specs, check_vma=False)
```

profile of v0, /device:TPU:1, one launch (start us, length us, event | category | flops | bytes accessed | tf_op | source)
XLA Modules:
  0.0 289.3 jit_solution(16413758966883116259)
XLA Ops:
  6.5 13.3 %all_to_all.49 = bf16[16,4,1024]{2,1,0:T(4,128)(2,1)S(1)} all-to-all(bf16[16,4,1024]{2,1,0:T(4,128)(2,1)} %param.8), channel_id=1, replica_groups=mesh['row'=16,'col'=16] {'row'}, dimensions={0} | all-to-all | bytes 262144 | tf_op jit(solution)/shard_map/all_to_all | solution.py:54
  19.8 0.7 all_to_all.40
  20.5 0.0 all-gather.5.cloned.1.call-update
  20.6 0.0 all-gather.3.cloned.1.call-start
  20.6 1.1 reshape.206
  21.7 0.8 convert_element_type.70
  22.5 0.1 copy.58
  22.6 1.2 multiply_convert_fusion
  23.9 0.2 reshape.233
  24.1 20.5 %all_to_all.50 = bf16[16,2,2048]{2,1,0:T(2,128)(2,1)S(1)} all-to-all(bf16[16,2,2048]{2,1,0:T(2,128)(2,1)S(1)} %reshape.233), channel_id=1, replica_groups=mesh['row'=16,'col'=16] {'col'}, dimensions={0} | all-to-all | bytes 262144 | tf_op jit(solution)/shard_map/all_to_all | solution.py:58
  44.6 0.2 reshape.234
  44.8 0.2 copy.59
  45.0 0.9 all_to_all.38
  45.9 0.0 all-gather.3.cloned.1.call-update
  45.9 0.0 reduce-scatter.4.cloned.1.call-start
  46.0 35.0 %all-gather.5.cloned.1.call-done = bf16[1,1024,1024]{2,1,0:T(8,128)(2,1)} async-done(((bf16[1,64,1024]{2,1,0:T(8,128)(2,1)}), bf16[1,1024,1024]{2,1,0:T(8,128)(2,1)}) %all-gather.5.cloned.1.call-update) | async-done | bytes 2097168 | tf_op jit(solution)/shard_map/all_gather | solution.py:55
  81.0 2.7 reshape.200
  83.7 2.3 copy.62
  86.1 4.1 %squeeze.10 = bf16[1024,1024]{1,0:T(8,128)(2,1)} reshape(bf16[1,16,16,4,1024]{4,3,2,1,0:T(4,128)(2,1)} %copy.62) | data formatting | bytes 4194304 | tf_op jit(solution)/shard_map/while/body/jit(dynamic_index_in_dim)/squeeze | solution.py:29
  90.2 2.6 copy.60
  92.8 2.7 reshape.199
  95.5 2.3 copy.61
  97.9 4.0 %squeeze.9 = bf16[1024,1024]{0,1:T(8,128)(2,1)} reshape(bf16[1,1024,16,16,4]{1,4,3,2,0:T(4,128)(2,1)} %copy.61) | data formatting | bytes 4194304 | tf_op jit(solution)/shard_map/while/body/jit(dynamic_index_in_dim)/squeeze | solution.py:29
  101.8 16.3 %all-gather.3.cloned.1.call-done = bf16[1,1024,1024]{2,1,0:T(8,128)(2,1)} async-done(((bf16[1,64,1024]{2,1,0:T(8,128)(2,1)}), bf16[1,1024,1024]{2,1,0:T(8,128)(2,1)}) %all-gather.3.cloned.1.call-update) | async-done | bytes 2097168 | tf_op jit(solution)/shard_map/all_gather | solution.py:61
  118.1 7.3 %convert_bitcast_fusion.1 = bf16[1,1024,1024]{1,2,0:T(8,128)(2,1)S(1)} fusion(bf16[1024,1024]{1,0:T(8,128)(2,1)} %squeeze.10, bf16[1024,1024]{0,1:T(8,128)(2,1)} %squeeze.9, bf16[1,1024,1024]{2,1,0:T(8,128)(2,1)} %all-gather.3.cloned.1.call-done), kind=kOutput, calls=%fused_computation.5 | convolution fusion | flops 4297064448 | bytes 8388608 | tf_op jit(solution)/shard_map/while/body/eval_jaxpr/ac,pcb->pab/dot_general | solution.py:25
  125.5 7.8 %copy.72 = bf16[1,1024,1024]{2,0,1:T(2,128)(2,1)} copy(bf16[1,1024,1024]{1,2,0:T(8,128)(2,1)S(1)} %convert_bitcast_fusion.1) | data formatting | bytes 4194304
  133.3 4.3 %copy.81 = bf16[1024,1,1024]{2,0,1:T(8,128)(2,1)} copy(bf16[1024,1,1024]{2,1,0:T(2,128)(2,1)} %bitcast.94) | data formatting | bytes 4194304
  137.6 0.0 reduce-scatter.4.cloned.1.call-update
  137.6 63.6 %reduce-scatter.4.cloned.1.call-done = bf16[64,1024]{1,0:T(8,128)(2,1)} async-done(((bf16[1024,1024]{1,0:T(8,128)(2,1)}), bf16[64,1024]{1,0:T(8,128)(2,1)}) %reduce-scatter.4.cloned.1.call-update) | async-done | bytes 131088
  201.2 1.0 reshape_bitcast_fusion
  202.3 0.5 copy.63
  202.7 0.5 broadcast.172
  203.3 2.3 reduce.4
  205.5 0.9 reshape.235
  206.4 8.9 %all-to-all-start.2 = ((bf16[16,2,2048]{2,1,0:T(2,128)(2,1)}), bf16[16,2,2048]{2,1,0:T(2,128)(2,1)S(1)}, u32[]{:S(2)}, u32[]{:S(2)}) async-start(bf16[16,2,2048]{2,1,0:T(2,128)(2,1)} %reshape.235), calls=%async_computation.2 | async-start | bytes 262144 | tf_op jit(solution)/shard_map/all_to_all | solution.py:66
  215.4 1.7 copy.66
  217.0 7.7 %all-to-all-done.2 = bf16[16,2,2048]{2,1,0:T(2,128)(2,1)S(1)} async-done(((bf16[16,2,2048]{2,1,0:T(2,128)(2,1)}), bf16[16,2,2048]{2,1,0:T(2,128)(2,1)S(1)}, u32[]{:S(2)}, u32[]{:S(2)}) %all-to-all-start.2) | async-done | bytes 131104 | tf_op jit(solution)/shard_map/all_to_all | solution.py:66
  224.7 0.3 reshape.236
  225.0 0.3 copy.64
  225.3 0.1 reshape.214
  225.5 1.0 copy.82
  226.5 1.7 copy.67
  228.1 3.1 %copy_bitcast_fusion.3 = bf16[16,16,4,4,16]{4,3,2,1,0:T(4,128)(2,1)} fusion(f32[16,16,4,16,4]{0,4,3,2,1:T(4,128)} %bitcast.97, f32[16,16,4,16,4]{0,4,3,2,1:T(4,128)S(1)} %bitcast.96), kind=kLoop, calls=%fused_computation.45 | loop fusion | flops 131072 | bytes 655360
  231.2 2.5 reshape.237
  233.8 13.1 %all_to_all.51 = bf16[16,2,2048]{2,1,0:T(2,128)(2,1)S(1)} all-to-all(bf16[16,2,2048]{2,1,0:T(2,128)(2,1)S(1)} %reshape.237), channel_id=1, replica_groups=mesh['row'=16,'col'=16] {'row'}, dimensions={0} | all-to-all | bytes 262144 | tf_op jit(solution)/shard_map/all_to_all | solution.py:72
  246.9 0.7 reshape.238
  247.6 0.0 copy-start.4
  247.6 0.5 copy_bitcast_fusion.2
  248.1 1.8 reshape.239
  249.9 3.5 %all-to-all-start.4 = ((bf16[16,2,2048]{2,1,0:T(2,128)(2,1)}), bf16[16,2,2048]{2,1,0:T(2,128)(2,1)S(1)}, u32[]{:S(2)}, u32[]{:S(2)}) async-start(bf16[16,2,2048]{2,1,0:T(2,128)(2,1)} %reshape.239), calls=%async_computation.4 | async-start | bytes 262144 | tf_op jit(solution)/shard_map/all_to_all | solution.py:71
  253.4 0.1 broadcast_add_fusion
  253.5 1.0 reshape.207
  254.5 0.1 reshape.204
  254.7 0.1 sub.56
  254.8 0.1 dynamic_slice.11
  254.9 0.1 add.110
  255.0 0.1 broadcast_subtract_fusion
  255.0 7.9 %all-to-all-done.4 = bf16[16,2,2048]{2,1,0:T(2,128)(2,1)S(1)} async-done(((bf16[16,2,2048]{2,1,0:T(2,128)(2,1)}), bf16[16,2,2048]{2,1,0:T(2,128)(2,1)S(1)}, u32[]{:S(2)}, u32[]{:S(2)}) %all-to-all-start.4) | async-done | bytes 131104 | tf_op jit(solution)/shard_map/all_to_all | solution.py:71
  262.9 1.7 reshape.240
  264.6 1.5 convert_bitcast_fusion
  266.1 8.9 %copy.70 = f32[16,16,4,16,4]{4,3,2,1,0:T(8,128)} copy(f32[16,16,4,16,4]{0,2,4,3,1:T(4,128)S(1)} %convert_bitcast_fusion) | data formatting | bytes 524288 | tf_op jit(solution)/shard_map/reshape | solution.py:81
  275.0 6.5 %reshape.217 = f32[4,4,64,64]{3,2,1,0:T(8,128)S(1)} reshape(f32[16,16,4,16,4]{4,3,2,1,0:T(8,128)} %copy.70) | data formatting | bytes 524288 | tf_op jit(solution)/shard_map/reshape | solution.py:81
  281.6 0.3 fusion.14
  281.9 0.9 reshape.205
  (15 shorter events, 0.1 us)
Async XLA Ops:
  6.5 74.5 %all-gather.5.cloned.1.call-start = ((), (), s32[]{:S(2)}) async-start(), calls=%async_computation.7 | async-start | bytes 2228224 | tf_op jit(solution)/shard_map/all_gather | solution.py:55
  20.6 97.6 %all-gather.3.cloned.1.call-start = ((), (), s32[]{:S(2)}) async-start(), calls=%async_computation.6 | async-start | bytes 2228224 | tf_op jit(solution)/shard_map/all_gather | solution.py:61
  45.9 155.3 %reduce-scatter.4.cloned.1.call-start = ((), (), s32[]{:S(2)}) async-start(), calls=%async_computation.8 | async-start | bytes 2228224
  86.1 4.1 %copy-start = (bf16[1,1024,1024]{2,1,0:T(8,128)(2,1)S(1)}, bf16[1,1024,1024]{2,1,0:T(8,128)(2,1)}, u32[]{:S(2)}) copy-start(bf16[1,1024,1024]{2,1,0:T(8,128)(2,1)} %all-gather.5.cloned.1.call-done) | copy-start | bytes 6291460
  137.6 77.8 %copy-start.3 = (bf16[1,1,16,4096]{3,2,1,0:T(8,128)(2,1)S(1)}, bf16[1,1,16,4096]{3,2,1,0:T(8,128)(2,1)}, u32[]{:S(2)}) copy-start(bf16[1,1,16,4096]{3,2,1,0:T(8,128)(2,1)} %param.7) | copy-start | bytes 393220
  206.4 18.2 %all-to-all-start.2 = ((bf16[16,2,2048]{2,1,0:T(2,128)(2,1)}), bf16[16,2,2048]{2,1,0:T(2,128)(2,1)S(1)}, u32[]{:S(2)}, u32[]{:S(2)}) async-start(bf16[16,2,2048]{2,1,0:T(2,128)(2,1)} %reshape.235), calls=%async_computation.2 | async-start | bytes 262144 | tf_op jit(solution)/shard_map/all_to_all | solution.py:66
  246.9 6.5 %copy-start.5 = (f32[4]{0:T(128)S(1)}, f32[4]{0:T(128)}, u32[]{:S(2)}) copy-start(f32[4]{0:T(128)} %param.10) | copy-start | bytes 52
  247.6 6.9 %copy-start.4 = (f32[1024]{0:T(1024)S(1)}, f32[1024]{0:T(1024)}, u32[]{:S(2)}) copy-start(f32[1024]{0:T(1024)} %param.11) | copy-start | bytes 12292
  249.9 13.1 %all-to-all-start.4 = ((bf16[16,2,2048]{2,1,0:T(2,128)(2,1)}), bf16[16,2,2048]{2,1,0:T(2,128)(2,1)S(1)}, u32[]{:S(2)}, u32[]{:S(2)}) async-start(bf16[16,2,2048]{2,1,0:T(2,128)(2,1)} %reshape.239), calls=%async_computation.4 | async-start | bytes 262144 | tf_op jit(solution)/shard_map/all_to_all | solution.py:71
  275.0 6.5 %copy-start.1 = (f32[16,64,64]{2,1,0:T(8,128)S(1)}, f32[16,64,64]{2,1,0:T(8,128)}, u32[]{:S(2)}) copy-start(f32[16,64,64]{2,1,0:T(8,128)} %reshape.207) | copy-start | bytes 786436
  275.0 6.5 %copy-start.2 = (f32[16,64,64]{2,1,0:T(8,128)S(1)}, f32[16,64,64]{2,1,0:T(8,128)}, u32[]{:S(2)}) copy-start(f32[16,64,64]{2,1,0:T(8,128)} %get-tuple-element.14) | copy-start | bytes 786436
Sparse Core Ops, SparseCore 0:
  20.7 60.2 all-gather.4
  82.8 35.2 all-gather.2
  137.7 63.4 reduce-scatter.3
where the time goes:
time: 290 us; the launch traced here: 289 us
  waiting for transfers between devices  131 us (45%)
  local copies, waits for them, and re-layouts  69.2 us (24%)
  blocking collectives  47 us (16%)
  between operations  13.4 us (5%)
  starting transfers between devices  12.5 us (4%)
  matrix products  8.57 us (3%)
  other arithmetic  8.16 us (3%)
    unnamed x4, waiting for transfers between devices  63.7 us
    all_gather x1, waiting for transfers between devices, shards(): col_ordered = lax.all_gather(share_rows, 'col', axis=1, tiled=True)  35 us
    unnamed x25, local copies, waits for them, and re-layouts  22.5 us
    all_to_all x1, blocking collectives, shards(): lax.all_to_all(masked, 'col', split_axis=0, concat_axis=2, tiled=True)  20.5 us
    all_gather x1, waiting for transfers between devices, shards(): lax.all_gather(mine, 'row', axis=1, tiled=True)  16.3 us
    reshape x3, local copies, waits for them, and re-layouts, shards(): swapped.transpose(1, 0, 2, 3).reshape(pair_count, a_local, b_local)  15.4 us
    all_to_all x1, blocking collectives, shards(): lax.all_to_all(factors, 'row', split_axis=0, concat_axis=1, tiled=True)  13.3 us
    all_to_all x1, blocking collectives, shards(): lax.all_to_all(split_tile.astype(jnp.bfloat16), 'row', split_axis=3, conc...  13.1 us
  transfers between devices with their start and end apart: 5, of which 5 were waited for; matrix products, arithmetic and copies ran while one was open for 10% of the time, Pallas kernels for 0%

commit v1 on v0

v1 whole, which is shorter than its diff:
```python
import functools

import jax
import jax.numpy as jnp
import numpy as np
from jax import lax
from jax.experimental import pallas as pl
from jax.experimental.pallas import tpu as pltpu
from jax.sharding import Mesh
from jax.sharding import PartitionSpec as P

AXES = ("x", "zl", "core", "zh", "y")
PLANE = ("x", "y")
SLOTS = ("zh", "zl", "core")
PAIR_OF_SLOT = (1, 4, 2, 8, 3, 12, 6, 9, 7, 13, 11, 14, 0, 5, 10, 15)
N_OFF = 12
VMEM = pltpu.CompilerParams(vmem_limit_bytes=40 * 1024 * 1024)
F32 = jnp.float32
BF16 = jnp.bfloat16
NT = (((1,), (1,)), ((), ()))


def _one_hot(source_of):
    source_of = np.asarray(source_of).reshape(-1)
    size = source_of.size
    out = np.zeros((size, size), np.float32)
    out[np.arange(size), source_of] = 1
    return out


def _grid(*sizes):
    return np.meshgrid(*[np.arange(s) for s in sizes], indexing="ij")


def _tables():
    zc, j, h = _grid(4, 32, 2)
    rows_nat = _one_hot(zc * 64 + h * 32 + j)
    rb, zh, k = _grid(16, 4, 4)
    cols_rb = _one_hot(zh * 64 + rb * 4 + k).T
    ya, zc, zh, k = _grid(4, 4, 4, 4)
    a_loc = zh * 16 + ya * 4 + k
    rows_src = _one_hot(zc * 64 + (a_loc % 2) * 32 + a_loc // 2)
    x, zh, zc, k = _grid(4, 4, 4, 4)
    cols_src = _one_hot(zh * 64 + (x * 4 + zc) * 4 + k).T
    first = np.stack([rows_nat, cols_rb, rows_src, cols_src])
    zc, zh, y, k = _grid(4, 4, 4, 4)
    swap_a = _one_hot(((y * 4 + zh) * 4 + zc) * 4 + k)
    zh, x, zc, k = _grid(4, 4, 4, 4)
    swap_b = _one_hot(((x * 4 + zc) * 4 + zh) * 4 + k).T
    last = np.stack([swap_a, swap_b, rows_nat.T])
    y, x, zc, k = _grid(4, 4, 4, 4)
    rows_b = _one_hot(((zc * 4 + x) * 4 + y) * 4 + k)
    nat = np.zeros((2, 256, 512), np.float32)
    for parity in range(2):
        y, rl, zh, k = _grid(4, 4, 4, 4)
        nat[parity, rl * 64 + zh * 16 + y * 4 + k, y * 128 + (parity * 4 + rl) * 16 + zh * 4 + k] = 1
    return [np.asarray(t, jnp.bfloat16) for t in (first, last, rows_b, nat)]


def _perm(left, right):
    return jnp.dot(left, right, preferred_element_type=F32).astype(BF16)


def _mask_kernel(place_ref, amps_ref, source_ref, screen_ref, sent_ref, mask_ref, flat_ref):
    block = screen_ref[place_ref[0]].astype(F32)
    lane_block = (lax.broadcasted_iota(jnp.int32, (8, 128), 1) % 64) // 8
    spread = (lax.broadcasted_iota(jnp.int32, (8, 128), 0) == lane_block).astype(F32)
    mask = jnp.dot(block, spread, preferred_element_type=F32)
    mask_ref[...] = mask
    for first, ref in ((0, amps_ref), (32, source_ref)):
        for j in range(32):
            tile = ref[:, j * 128 : (j + 1) * 128].astype(F32)
            if first == 0:
                tile = tile * mask
            flat_ref[pl.ds(j, 16, stride=32), :] = tile
        for slot, pair in enumerate(PAIR_OF_SLOT):
            sent_ref[slot, first : first + 32, :] = flat_ref[pair * 32 : pair * 32 + 32, :].astype(BF16)


def _block_kernel(got_ref, first_ref, sent_ref, kept_ref):

    def block(offset):
        tall = []
        for zc in range(4):
            wide = []
            for zh in range(4):
                part = got_ref[zh * 4 + zc, offset : offset + 32, :]
                wide.append(jnp.concatenate([part[:, :64], part[:, 64:]], axis=0))
            tall.append(jnp.concatenate(wide, axis=1))
        return jnp.concatenate(tall, axis=0)

    amp = _perm(_perm(first_ref[0], block(0)), first_ref[1])
    src = block(32)
    kept_ref[...] = _perm(first_ref[0], src)
    swap = _perm(_perm(first_ref[2], src), first_ref[3])
    for x in range(4):
        for y in range(4):
            to = x * 4 + y
            sent_ref[to, :256, :] = amp[:, :128]
            sent_ref[to, 256:512, :] = amp[:, 128:]
            piece = swap[y * 64 : y * 64 + 64, x * 64 : x * 64 + 64]
            sent_ref[to, 512:, :] = jnp.concatenate([piece[:32], piece[32:]], axis=1)


def _ladder_kernel(
    place_ref, fac_ref, own_ref, other_ref, rows_ref, nat_ref, out_ref, sym_ref, inner_ref, left_ref, right_ref
):
    diagonal = place_ref[1] >= N_OFF
    for zh in range(4):
        part = _perm(rows_ref[...], fac_ref[zh * 256 : zh * 256 + 256, :])
        for y in range(4):
            right_ref[y * 256 + zh * 64 : y * 256 + zh * 64 + 64, :] = part[y * 64 : y * 64 + 64]
        for zc in range(4):
            for x in range(4):
                to = x * 256 + zc * 64 + zh * 16
                at = (zh * 4 + zc) * 64 + x * 16
                left_ref[to : to + 16, :] = fac_ref[at : at + 16, :]

    def gathered(ref, x, half):
        return [ref[x * 4 + y, half * 256 : half * 256 + 256, :] for y in range(4)]

    for i in range(4):
        for j in range(4):
            own = jnp.concatenate(gathered(own_ref, i, j // 2), axis=1)
            other = jnp.concatenate(gathered(other_ref, j, i // 2), axis=1)
            mine = jnp.concatenate(gathered(own_ref, j, i // 2), axis=1)
            other = jnp.where(diagonal, mine, other)
            total = lax.dot_general(own, nat_ref[j % 2], NT, preferred_element_type=F32)
            total += lax.dot_general(nat_ref[i % 2], other, NT, preferred_element_type=F32)
            sym_ref[i * 256 : i * 256 + 256, j * 256 : j * 256 + 256] = total.astype(BF16)
    for i in range(4):
        for j in range(4):
            inner_ref[i * 256 : i * 256 + 256, j * 256 : j * 256 + 256] = lax.dot_general(
                sym_ref[i * 256 : i * 256 + 256, :],
                right_ref[j * 256 : j * 256 + 256, :],
                NT,
                preferred_element_type=F32,
            ).astype(BF16)
    for x in range(4):
        for y in range(4):
            out_ref[x * 4 + y] = _perm(
                left_ref[x * 256 : x * 256 + 256, :], inner_ref[:, y * 256 : y * 256 + 256]
            )


def _sum_kernel(place_ref, part_ref, kept_ref, own_ref, other_ref, last_ref, sent_ref):
    diagonal = place_ref[1] >= N_OFF
    total = part_ref[0].astype(F32)
    for q in range(1, 16):
        total += part_ref[q].astype(F32)
    total += kept_ref[...].astype(F32)
    tall = []
    for x in range(4):
        wide = []
        for y in range(4):
            part = jnp.where(diagonal, own_ref[x * 4 + y], other_ref[x * 4 + y])
            wide.append(jnp.concatenate([part[:, :64], part[:, 64:]], axis=0))
        tall.append(jnp.concatenate(wide, axis=1))
    swap = jnp.concatenate(tall, axis=0)
    turned = lax.dot_general(last_ref[0], swap, NT, preferred_element_type=F32).astype(BF16)
    total += jnp.dot(turned, last_ref[1], preferred_element_type=F32)
    packed = _perm(last_ref[2], total.astype(BF16))
    for zh in range(4):
        for zc in range(4):
            piece = packed[zc * 64 : zc * 64 + 64, zh * 64 : zh * 64 + 64]
            sent_ref[zh * 4 + zc] = jnp.concatenate([piece[:32], piece[32:]], axis=1)


def _update_kernel(place_ref, occ_ref, rsym_ref, amps_ref, mask_ref, vir_ref, out_ref, flat_ref):
    row = place_ref[2]
    col = place_ref[3]
    exact = lax.Precision.HIGHEST

    def iota(shape, dim):
        return lax.broadcasted_iota(jnp.int32, shape, dim)

    mine = vir_ref[pl.ds(row // 2, 1), :]
    l_row = iota((32, 128), 1) - (row % 2) * 64
    in_row = (l_row // 2 == iota((32, 128), 0)) & (l_row >= 0)
    picked = jnp.where(in_row, jnp.broadcast_to(mine, (32, 128)), 0.0)
    same_half = (iota((128, 128), 0) % 2 == iota((128, 128), 1) // 64).astype(F32)
    vir_a = jnp.dot(picked, same_half, precision=exact, preferred_element_type=F32)
    lane = iota((128, 128), 1)
    want = ((lane // 4) % 2) * 64 + col * 4 + lane % 4
    choose = (iota((128, 128), 0) == want).astype(F32)
    by_block = jnp.dot(vir_ref[...], choose, precision=exact, preferred_element_type=F32)
    own_block = iota((8, 128), 0) == (iota((8, 128), 1) % 64) // 8
    vir_b = jnp.sum(jnp.where(own_block, by_block, 0.0), axis=0, keepdims=True)
    vir = vir_a + vir_b
    for slot, pair in enumerate(PAIR_OF_SLOT):
        denom = (occ_ref[pair // 4] + occ_ref[pair % 4]) - vir
        change = rsym_ref[slot].astype(F32) / denom
        old = amps_ref[slot].astype(F32)
        flat_ref[pair * 32 : pair * 32 + 32, :] = old + mask_ref[pair : pair + 1, :] * change
    for j in range(32):
        out_ref[:, j * 128 : (j + 1) * 128] = flat_ref[pl.ds(j, 16, stride=32), :].astype(BF16)


def _vmem(shape=None, index=None):
    if shape is None:
        return pl.BlockSpec(memory_space=pltpu.VMEM)
    return pl.BlockSpec(shape, index, memory_space=pltpu.VMEM)


SMEM = pl.BlockSpec(memory_space=pltpu.SMEM)


def _shards(tables, amps, source, factors, screen, occ_energy, vir_energy):
    first, last, rows_b, nat = tables
    x, zl, core = lax.axis_index("x"), lax.axis_index("zl"), lax.axis_index("core")
    zh, y = lax.axis_index("zh"), lax.axis_index("y")
    place = jnp.stack([x * 2 + zl, zh * 4 + zl * 2 + core, x * 4 + zl * 2 + core, zh * 4 + y])
    place = place.astype(jnp.int32)

    share = lax.all_to_all(factors, PLANE, 0, 0, tiled=True).reshape(64, 1024)
    fac = lax.all_gather(share, SLOTS, axis=0, tiled=True)

    sent, mask = pl.pallas_call(
        _mask_kernel,
        out_shape=(jax.ShapeDtypeStruct((16, 64, 128), BF16), jax.ShapeDtypeStruct((16, 128), F32)),
        in_specs=[SMEM, _vmem(), _vmem(), _vmem()],
        out_specs=(_vmem(), _vmem()),
        scratch_shapes=[pltpu.VMEM((512, 128), F32)],
        name="mask_amps",
    )(place, amps.reshape(16, 4096), source.reshape(16, 4096), screen.transpose(1, 0, 2))
    got = lax.all_to_all(sent, SLOTS, 0, 0, tiled=True)
    block, kept = pl.pallas_call(
        _block_kernel,
        out_shape=(jax.ShapeDtypeStruct((16, 544, 128), BF16), jax.ShapeDtypeStruct((256, 256), BF16)),
        in_specs=[_vmem(), _vmem()],
        out_specs=(_vmem(), _vmem()),
        compiler_params=VMEM,
        name="make_block",
    )(got, first)
    own = lax.all_to_all(block, PLANE, 0, 0, tiled=True)
    other = lax.ppermute(own, "core", [(0, 1), (1, 0)])
    square = pltpu.VMEM((1024, 1024), BF16)
    partial = pl.pallas_call(
        _ladder_kernel,
        out_shape=jax.ShapeDtypeStruct((16, 256, 256), BF16),
        in_specs=[SMEM] + [_vmem()] * 5,
        out_specs=_vmem(),
        scratch_shapes=[square] * 4,
        compiler_params=VMEM,
        name="ladder",
    )(place, fac, own, other, rows_b, nat)
    parts = lax.all_to_all(partial, PLANE, 0, 0, tiled=True)
    tail = _vmem((16, 32, 128), lambda i: (0, 16, 0))
    summed = pl.pallas_call(
        _sum_kernel,
        out_shape=jax.ShapeDtypeStruct((16, 32, 128), BF16),
        grid=(1,),
        in_specs=[SMEM, _vmem(), _vmem(), tail, tail, _vmem()],
        out_specs=_vmem(),
        compiler_params=VMEM,
        name="sum_parts",
    )(place, parts, kept, own, other, last)
    rsym = lax.all_to_all(summed, SLOTS, 0, 0, tiled=True)
    head = _vmem((16, 32, 128), lambda i: (0, 0, 0))
    out = pl.pallas_call(
        _update_kernel,
        out_shape=jax.ShapeDtypeStruct((16, 4096), BF16),
        grid=(1,),
        in_specs=[SMEM, SMEM, _vmem(), head, _vmem(), _vmem()],
        out_specs=_vmem(),
        scratch_shapes=[pltpu.VMEM((512, 128), F32)],
        name="update",
    )(place, occ_energy, rsym, sent, mask, vir_energy.reshape(8, 128))
    return out.reshape(1, 1, 16, 4096)


def solution(mesh):
    fine = Mesh(mesh.devices.reshape(4, 2, 2, 4, 4), AXES)
    row, col = ("x", "zl", "core"), ("zh", "y")
    in_specs = (
        P(row, col, None, None),
        P(row, col, None, None),
        P(None, row + col, None),
        P(),
        P(),
        P(),
    )
    shards = functools.partial(_shards, _tables())
    return jax.shard_map(shards, mesh=fine, in_specs=in_specs, out_specs=P(row, col, None, None), check_vma=False)
```

time: 290 us -> 162 us (0.56)
  waiting for transfers between devices: 131 us -> 40.6 us
  local copies, waits for them, and re-layouts: 69.2 us -> 6.17 us
  blocking collectives: 47 us -> 70.9 us
  Pallas kernels: 0 us -> 15.8 us
  matrix products: 8.57 us -> 0 us
  other arithmetic: 8.16 us -> 0.56 us
    unnamed x4 -> x1, waiting for transfers between devices: 63.7 us -> 0.02 us
    all_gather x2 -> x1, waiting for transfers between devices: 51.4 us -> 7.54 us  [_shards(): fac = lax.all_gather(share, SLOTS, axis=0, tiled=True)]
    all_to_all x3, blocking collectives: 47 us -> 70.9 us  [the longest x1 33.6 us: _shards(): parts = lax.all_to_all(partial, PLANE, 0, 0, tiled=True)]
    reshape x7 -> x1, local copies, waits for them, and re-layouts: 21.9 us -> 0.69 us  [_shards(): share = lax.all_to_all(factors, PLANE, 0, 0, tiled=True).reshape(64, 1024)]
    all_to_all x2, waiting for transfers between devices: 15.5 us -> 33 us  [the longest x1 29.1 us: _shards(): own = lax.all_to_all(block, PLANE, 0, 0, tiled=True)]
    unnamed x25 -> x15, local copies, waits for them, and re-layouts: 22.5 us -> 5.48 us
    pallas_call x0 -> x5, Pallas kernels: none -> 15.8 us  [the longest x1 8.9 us: _shards(): pl.pallas_call(_ladder_kernel, out_shape=jax.ShapeDtypeStruct((16, 256, 2...]
    dot_general x2 -> x0, matrix products: 8.57 us -> none  [the longest x1 7.35 us: step(): jnp.einsum('ac,pcb->pab', left_one, inner_part, preferred_element_type=jn...]
  transfers between devices with their start and end apart: 5 -> 4, of which waited for: 5 -> 3; matrix products, arithmetic and copies ran while one was open for 10% -> 0% of each run, Pallas kernels for 0% -> 0%
where the time goes in v1:
time: 162 us; the launch traced here: 161 us
  blocking collectives  70.9 us (44%)
  waiting for transfers between devices  40.6 us (25%)
  Pallas kernels  15.8 us (10%)
  starting transfers between devices  13.7 us (8%)
  between operations  13.5 us (8%)
  local copies, waits for them, and re-layouts  6.17 us (4%)
    all_to_all x1, blocking collectives, _shards(): parts = lax.all_to_all(partial, PLANE, 0, 0, tiled=True)  33.6 us
    all_to_all x1, waiting for transfers between devices, _shards(): own = lax.all_to_all(block, PLANE, 0, 0, tiled=True)  29.1 us
    all_to_all x1, blocking collectives, _shards(): got = lax.all_to_all(sent, SLOTS, 0, 0, tiled=True)  21.7 us
    all_to_all x1, blocking collectives, _shards(): rsym = lax.all_to_all(summed, SLOTS, 0, 0, tiled=True)  15.6 us
    pallas_call x1, Pallas kernels, _shards(): pl.pallas_call(_ladder_kernel, out_shape=jax.ShapeDtypeStruct((16, 256, 2...  8.9 us
    all_gather x1, waiting for transfers between devices, _shards(): fac = lax.all_gather(share, SLOTS, axis=0, tiled=True)  7.54 us
    all_to_all x1, starting transfers between devices, _shards(): share = lax.all_to_all(factors, PLANE, 0, 0, tiled=True).reshape(64, 1024)  6.76 us
    unnamed x15, local copies, waits for them, and re-layouts  5.48 us
  transfers between devices with their start and end apart: 4, of which 3 were waited for; matrix products, arithmetic and copies ran while one was open for 0% of the time, Pallas kernels for 0%

profile of v1, /device:TPU:1, one launch (start us, length us, event | category | flops | bytes accessed | tf_op | source)
XLA Modules:
  0.0 161.2 jit_solution(1657224876282993886)
XLA Ops:
  6.5 1.5 copy.11
  8.0 0.6 pad_add_fusion.place_ref
  8.6 2.2 %mask_amps.1 = (bf16[16,64,128]{2,1,0:T(8,128)(2,1)}, f32[16,128]{1,0:T(8,128)}) custom-call(s32[4]{0:T(128)} %pad_add_fusion.place_ref, bf16[16,4096]{1,0:T(8,128)(2,1)} %bitcast.10, bf16[16,4096]{1,0:T(8,128)(2,1)} %bitcast.11, s32[8,16,8]{2,1,0:T(8,128)} %bitcast.9), custom_call_target="tpu_custom_call" | custom-call | tf_op jit(solution)/shard_map/mask_amps/pallas_call | solution.py:218
  10.8 21.7 %all_to_all.25.got_ref = bf16[16,64,128]{2,1,0:T(8,128)(2,1)S(1)} all-to-all(bf16[16,64,128]{2,1,0:T(8,128)(2,1)} %get-tuple-element.9.amps_ref), channel_id=1, replica_groups=mesh['x'=4,'zl'=2,'core'=2,'zh'=4,'y'=4] {'zh','zl','core'}, dimensions={0} | all-to-all | bytes 524288 | tf_op jit(solution)/shard_map/all_to_all | solution.py:226
  32.4 6.8 %all-to-all-start = ((bf16[16,4,1024]{2,1,0:T(4,128)(2,1)}), bf16[16,4,1024]{2,1,0:T(4,128)(2,1)S(1)}, u32[]{:S(2)}, u32[]{:S(2)}) async-start(bf16[16,4,1024]{2,1,0:T(4,128)(2,1)} %param.12), calls=%async_computation | async-start | bytes 262144 | tf_op jit(solution)/shard_map/all_to_all | solution.py:215
  39.2 0.0 copy-start.3
  39.2 1.0 copy-done.3
  40.3 0.8 make_block.1
  41.1 0.0 copy-start
  41.1 1.4 copy-done
  42.4 3.9 %all-to-all-done = bf16[16,4,1024]{2,1,0:T(4,128)(2,1)S(1)} async-done(((bf16[16,4,1024]{2,1,0:T(4,128)(2,1)}), bf16[16,4,1024]{2,1,0:T(4,128)(2,1)S(1)}, u32[]{:S(2)}, u32[]{:S(2)}) %all-to-all-start) | async-done | bytes 131104 | tf_op jit(solution)/shard_map/all_to_all | solution.py:215
  46.4 0.0 copy-start.2
  46.4 0.0 copy-start.5
  46.4 0.0 copy-start.6
  46.4 3.9 %all-to-all-start.2 = ((bf16[16,544,128]{2,1,0:T(8,128)(2,1)}), bf16[16,544,128]{2,1,0:T(8,128)(2,1)S(1)}, u32[]{:S(2)}, u32[]{:S(2)}) async-start(bf16[16,544,128]{2,1,0:T(8,128)(2,1)} %copy-done), calls=%async_computation.2 | async-start | bytes 4456448 | tf_op jit(solution)/shard_map/all_to_all | solution.py:235
  50.2 0.0 all-gather.2.cloned.1.call-start
  50.3 0.7 reshape.15
  51.0 0.0 all-gather.2.cloned.1.call-update
  51.0 29.1 %all-to-all-done.2.own_ref = bf16[16,544,128]{2,1,0:T(8,128)(2,1)S(1)} async-done(((bf16[16,544,128]{2,1,0:T(8,128)(2,1)}), bf16[16,544,128]{2,1,0:T(8,128)(2,1)S(1)}, u32[]{:S(2)}, u32[]{:S(2)}) %all-to-all-start.2) | async-done | bytes 2228256 | tf_op jit(solution)/shard_map/all_to_all | solution.py:235
  80.1 3.1 %collective-permute-start = (bf16[16,544,128]{2,1,0:T(8,128)(2,1)S(1)}, bf16[16,544,128]{2,1,0:T(8,128)(2,1)}, u32[]{:S(2)}, u32[]{:S(2)}) collective-permute-start(bf16[16,544,128]{2,1,0:T(8,128)(2,1)S(1)} %all-to-all-done.2.own_ref), channel_id=1, source_target_pairs={{0,16},{16,0},{1,17},{17,1},{2,18},{18,2},{3,19},{19,3},{4,20},{20... | collective-permute-start | bytes 6684680 | tf_op jit(solution)/shard_map/ppermute | solution.py:236
  83.2 7.5 %all-gather.2.cloned.1.call-done.fac_ref = bf16[1024,1024]{1,0:T(8,128)(2,1)} async-done(((bf16[64,1024]{1,0:T(8,128)(2,1)}), bf16[1024,1024]{1,0:T(8,128)(2,1)}) %all-gather.2.cloned.1.call-update) | async-done | bytes 2097168 | tf_op jit(solution)/shard_map/all_gather | solution.py:216
  90.7 0.0 collective-permute-done.other_ref
  90.7 0.0 copy-done.2
  90.7 0.0 copy-done.5
  90.7 0.0 copy-done.6
  90.7 0.0 copy-start.1
  90.7 1.6 copy-done.1
  92.3 8.9 %ladder.1 = bf16[16,256,256]{2,1,0:T(8,128)(2,1)S(1)} custom-call(s32[4]{0:T(128)S(1)} %copy-done.6, bf16[1024,1024]{1,0:T(8,128)(2,1)S(1)} %copy-done.1, bf16[16,544,128]{2,1,0:T(8,128)(2,1)S(1)} %all-to-all-done.2.own_ref, bf16[16,544,128]{2,1,0:T(8,128)(2,1)} %collective-permute-done.other_ref, bf16[256,256]{1,0:T(8,128)(2,1)S(1)} %copy-done.5, ...), custom_call_target="tpu_custom_call" | custom-call | tf_op jit(solution)/shard_map/ladder/pallas_call | solution.py:238
  101.2 0.0 copy-start.4
  101.2 33.6 %all_to_all.26.part_ref = bf16[16,256,256]{2,1,0:T(8,128)(2,1)S(1)} all-to-all(bf16[16,256,256]{2,1,0:T(8,128)(2,1)S(1)} %ladder.1), channel_id=1, replica_groups=mesh['x'=4,'zl'=2,'core'=2,'zh'=4,'y'=4] {'x','y'}, dimensions={0} | all-to-all | bytes 4194304 | tf_op jit(solution)/shard_map/all_to_all | solution.py:247
  134.9 0.0 copy-done.4
  134.9 1.9 %sum_parts.1 = bf16[16,32,128]{2,1,0:T(8,128)(2,1)S(1)} custom-call(s32[4]{0:T(128)S(1)} %copy-done.6, bf16[16,256,256]{2,1,0:T(8,128)(2,1)S(1)} %all_to_all.26.part_ref, bf16[256,256]{1,0:T(8,128)(2,1)S(1)} %get-tuple-element.11.kept_ref, bf16[16,544,128]{2,1,0:T(8,128)(2,1)S(1)} %all-to-all-done.2.own_ref, ...), custom_call_target="tpu_custom_call" | custom-call | tf_op jit(solution)/shard_map/sum_parts/pallas_call | solution.py:249
  136.7 15.6 %all_to_all.27.rsym_ref = bf16[16,32,128]{2,1,0:T(8,128)(2,1)} all-to-all(bf16[16,32,128]{2,1,0:T(8,128)(2,1)S(1)} %sum_parts.1), channel_id=1, replica_groups=mesh['x'=4,'zl'=2,'core'=2,'zh'=4,'y'=4] {'zh','zl','core'}, dimensions={0} | all-to-all | bytes 262144 | tf_op jit(solution)/shard_map/all_to_all | solution.py:258
  152.3 2.1 %update.1 = bf16[16,4096]{1,0:T(8,128)(2,1)} custom-call(s32[4]{0:T(128)} %pad_add_fusion.place_ref, f32[4]{0:T(128)} %occ_ref.1, bf16[16,32,128]{2,1,0:T(8,128)(2,1)} %all_to_all.27.rsym_ref, bf16[16,64,128]{2,1,0:T(8,128)(2,1)} %get-tuple-element.9.amps_ref, f32[16,128]{1,0:T(8,128)} %get-tuple-element.12.mask_ref, f32[8,128]{1,0:T(8,128)} %bitcast.12), custom_call_target="tpu_custom_call" | custom-call | tf_op jit(solution)/shard_map/update/pallas_call | solution.py:260
Async XLA Ops:
  32.4 13.9 %all-to-all-start = ((bf16[16,4,1024]{2,1,0:T(4,128)(2,1)}), bf16[16,4,1024]{2,1,0:T(4,128)(2,1)S(1)}, u32[]{:S(2)}, u32[]{:S(2)}) async-start(bf16[16,4,1024]{2,1,0:T(4,128)(2,1)} %param.12), calls=%async_computation | async-start | bytes 262144 | tf_op jit(solution)/shard_map/all_to_all | solution.py:215
  39.2 1.0 copy-start.3
  41.1 1.4 copy-start
  46.4 44.3 %copy-start.2 = (bf16[2,256,512]{2,1,0:T(8,128)(2,1)S(1)}, bf16[2,256,512]{2,1,0:T(8,128)(2,1)}, u32[]{:S(2)}) copy-start(bf16[2,256,512]{2,1,0:T(8,128)(2,1)} %constant.35.clone.nat_ref) | copy-start | bytes 1572868
  46.4 44.3 %copy-start.5 = (bf16[256,256]{1,0:T(8,128)(2,1)S(1)}, bf16[256,256]{1,0:T(8,128)(2,1)}, u32[]{:S(2)}) copy-start(bf16[256,256]{1,0:T(8,128)(2,1)} %constant.34.clone.rows_ref) | copy-start | bytes 393220
  46.4 44.3 %copy-start.6 = (s32[4]{0:T(128)S(1)}, s32[4]{0:T(128)}, u32[]{:S(2)}) copy-start(s32[4]{0:T(128)} %pad_add_fusion.place_ref) | copy-start | bytes 52
  46.4 33.7 %all-to-all-start.2 = ((bf16[16,544,128]{2,1,0:T(8,128)(2,1)}), bf16[16,544,128]{2,1,0:T(8,128)(2,1)S(1)}, u32[]{:S(2)}, u32[]{:S(2)}) async-start(bf16[16,544,128]{2,1,0:T(8,128)(2,1)} %copy-done), calls=%async_computation.2 | async-start | bytes 4456448 | tf_op jit(solution)/shard_map/all_to_all | solution.py:235
  50.2 40.5 %all-gather.2.cloned.1.call-start = ((), (), s32[]{:S(2)}) async-start(), calls=%async_computation.5 | async-start | bytes 2228224 | tf_op jit(solution)/shard_map/all_gather | solution.py:216
  80.1 10.6 %collective-permute-start = (bf16[16,544,128]{2,1,0:T(8,128)(2,1)S(1)}, bf16[16,544,128]{2,1,0:T(8,128)(2,1)}, u32[]{:S(2)}, u32[]{:S(2)}) collective-permute-start(bf16[16,544,128]{2,1,0:T(8,128)(2,1)S(1)} %all-to-all-done.2.own_ref), channel_id=1, source_target_pairs={{0,16},{16,0},{1,17},{17,1},{2,18},{18,2},{3,19},{19,3},{4,20},{20... | collective-permute-start | bytes 6684680 | tf_op jit(solution)/shard_map/ppermute | solution.py:236
  90.7 1.6 copy-start.1
  101.2 33.6 %copy-start.4 = (bf16[3,256,256]{2,1,0:T(8,128)(2,1)S(1)}, bf16[3,256,256]{2,1,0:T(8,128)(2,1)}, u32[]{:S(2)}) copy-start(bf16[3,256,256]{2,1,0:T(8,128)(2,1)} %constant.36.clone.last_ref) | copy-start | bytes 1179652
Sparse Core Ops, SparseCore 0:
  52.9 37.7 all-gather.1

commit v2 on v1

--- a/solution.py
+++ b/solution.py
@@ -12,12 +12,14 @@
 AXES = ("x", "zl", "core", "zh", "y")
 PLANE = ("x", "y")
 SLOTS = ("zh", "zl", "core")
+DEEP = ("zl", "zh")
 PAIR_OF_SLOT = (1, 4, 2, 8, 3, 12, 6, 9, 7, 13, 11, 14, 0, 5, 10, 15)
 N_OFF = 12
 VMEM = pltpu.CompilerParams(vmem_limit_bytes=40 * 1024 * 1024)
 F32 = jnp.float32
 BF16 = jnp.bfloat16
 NT = (((1,), (1,)), ((), ()))
+TN = (((0,), (0,)), ((), ()))
 
 
 def _one_hot(source_of):
@@ -65,7 +67,7 @@
     block = screen_ref[place_ref[0]].astype(F32)
     lane_block = (lax.broadcasted_iota(jnp.int32, (8, 128), 1) % 64) // 8
     spread = (lax.broadcasted_iota(jnp.int32, (8, 128), 0) == lane_block).astype(F32)
-    mask = jnp.dot(block, spread, preferred_element_type=F32)
+    mask = lax.dot_general(block, spread, TN, preferred_element_type=F32)
     mask_ref[...] = mask
     for first, ref in ((0, amps_ref), (32, source_ref)):
         for j in range(32):
@@ -102,10 +104,33 @@
             sent_ref[to, 512:, :] = jnp.concatenate([piece[:32], piece[32:]], axis=1)
 
 
+def _order_kernel(place_ref, *refs):
+    deep = place_ref[1] // 2
+    for k in range(8):
+        refs[9][pl.ds(pl.multiple_of((deep + 8 - k) % 8 * 64, 64), 64), :] = refs[k][...]
+
+
 def _ladder_kernel(
-    place_ref, fac_ref, own_ref, other_ref, rows_ref, nat_ref, out_ref, sym_ref, inner_ref, left_ref, right_ref
+    place_ref,
+    mine_ref,
+    next_ref,
+    own_ref,
+    other_ref,
+    rows_ref,
+    nat_ref,
+    out_ref,
+    fac_ref,
+    sym_ref,
+    inner_ref,
+    left_ref,
+    right_ref,
 ):
     diagonal = place_ref[1] >= N_OFF
+    core = place_ref[1] % 2
+    for z in range(8):
+        rows = slice(z * 64, z * 64 + 64)
+        fac_ref[pl.ds(pl.multiple_of(z * 128 + core * 64, 64), 64), :] = mine_ref[rows, :]
+        fac_ref[pl.ds(pl.multiple_of(z * 128 + 64 - core * 64, 64), 64), :] = next_ref[rows, :]
     for zh in range(4):
         part = _perm(rows_ref[...], fac_ref[zh * 256 : zh * 256 + 256, :])
         for y in range(4):
@@ -196,6 +221,11 @@
         out_ref[:, j * 128 : (j + 1) * 128] = flat_ref[pl.ds(j, 16, stride=32), :].astype(BF16)
 
 
+def _along_z(step):
+    place = [(z % 2) * 4 + z // 2 for z in range(8)]
+    return [(place[z], place[(z + step) % 8]) for z in range(8)]
+
+
 def _vmem(shape=None, index=None):
     if shape is None:
         return pl.BlockSpec(memory_space=pltpu.VMEM)
@@ -213,8 +243,6 @@
     place = place.astype(jnp.int32)
 
     share = lax.all_to_all(factors, PLANE, 0, 0, tiled=True).reshape(64, 1024)
-    fac = lax.all_gather(share, SLOTS, axis=0, tiled=True)
-
     sent, mask = pl.pallas_call(
         _mask_kernel,
         out_shape=(jax.ShapeDtypeStruct((16, 64, 128), BF16), jax.ShapeDtypeStruct((16, 128), F32)),
@@ -222,7 +250,8 @@
         out_specs=(_vmem(), _vmem()),
         scratch_shapes=[pltpu.VMEM((512, 128), F32)],
         name="mask_amps",
-    )(place, amps.reshape(16, 4096), source.reshape(16, 4096), screen.transpose(1, 0, 2))
+    )(place, amps.reshape(16, 4096), source.reshape(16, 4096), screen.transpose(1, 2, 0))
+    share, sent = lax.optimization_barrier((share, sent))
     got = lax.all_to_all(sent, SLOTS, 0, 0, tiled=True)
     block, kept = pl.pallas_call(
         _block_kernel,
@@ -232,18 +261,30 @@
         compiler_params=VMEM,
         name="make_block",
     )(got, first)
+    share, block = lax.optimization_barrier((share, block))
+    pieces = [share] + [lax.ppermute(share, DEEP, _along_z(k)) for k in range(1, 8)]
     own = lax.all_to_all(block, PLANE, 0, 0, tiled=True)
+    fac, own = pl.pallas_call(
+        _order_kernel,
+        out_shape=(jax.ShapeDtypeStruct((512, 1024), BF16), jax.ShapeDtypeStruct((16, 544, 128), BF16)),
+        in_specs=[SMEM] + [_vmem()] * 8 + [pl.BlockSpec(memory_space=pl.ANY)],
+        out_specs=(_vmem(), pl.BlockSpec(memory_space=pl.ANY)),
+        input_output_aliases={9: 1},
+        compiler_params=VMEM,
+        name="order_factors",
+    )(place, *pieces, own)
     other = lax.ppermute(own, "core", [(0, 1), (1, 0)])
+    fac_other = lax.ppermute(fac, "core", [(0, 1), (1, 0)])
     square = pltpu.VMEM((1024, 1024), BF16)
     partial = pl.pallas_call(
         _ladder_kernel,
         out_shape=jax.ShapeDtypeStruct((16, 256, 256), BF16),
-        in_specs=[SMEM] + [_vmem()] * 5,
+        in_specs=[SMEM] + [_vmem()] * 6,
         out_specs=_vmem(),
-        scratch_shapes=[square] * 4,
+        scratch_shapes=[square] * 5,
         compiler_params=VMEM,
         name="ladder",
-    )(place, fac, own, other, rows_b, nat)
+    )(place, fac, fac_other, own, other, rows_b, nat)
     parts = lax.all_to_all(partial, PLANE, 0, 0, tiled=True)
     tail = _vmem((16, 32, 128), lambda i: (0, 16, 0))
     summed = pl.pallas_call(

time: 162 us -> 148 us (0.914)
  waiting for transfers between devices: 40.6 us -> 23.8 us
  starting transfers between devices: 13.7 us -> 27.2 us
  between operations: 13.5 us -> 0.13 us
  local copies, waits for them, and re-layouts: 6.17 us -> 8.71 us
    all_to_all x1, waiting for transfers between devices: 29.1 us -> 0.74 us  [_shards(): own = lax.all_to_all(block, PLANE, 0, 0, tiled=True)]
    ppermute x0 -> x8, waiting for transfers between devices: none -> 19.1 us  [the longest x7 13.9 us: _shards(): lax.ppermute(share, DEEP, _along_z(k))]
    ppermute x0 -> x8, starting transfers between devices: none -> 15 us  [the longest x7 14.7 us: _shards(): lax.ppermute(share, DEEP, _along_z(k))]
    all_gather x1 -> x0, waiting for transfers between devices: 7.54 us -> none  [_shards(): fac = lax.all_gather(share, SLOTS, axis=0, tiled=True)]
    unnamed x15 -> x28, local copies, waits for them, and re-layouts: 5.48 us -> 8.67 us
    ppermute x1, starting transfers between devices: 3.09 us -> 0.83 us  [_shards(): other = lax.ppermute(own, 'core', [(0, 1), (1, 0)])]
  transfers between devices with their start and end apart: 4 -> 11, of which waited for: 3 -> 6; matrix products, arithmetic and copies ran while one was open for 0% -> 0% of each run, Pallas kernels for 0% -> 2%
where the time goes in v2:
time: 148 us
  blocking collectives  72 us (49%)
  starting transfers between devices  27.2 us (18%)
  waiting for transfers between devices  23.8 us (16%)
  Pallas kernels  15.3 us (10%)
  local copies, waits for them, and re-layouts  8.71 us (6%)
    all_to_all x1, blocking collectives, _shards(): parts = lax.all_to_all(partial, PLANE, 0, 0, tiled=True)  33.9 us
    all_to_all x1, blocking collectives, _shards(): got = lax.all_to_all(sent, SLOTS, 0, 0, tiled=True)  22.1 us
    all_to_all x1, blocking collectives, _shards(): rsym = lax.all_to_all(summed, SLOTS, 0, 0, tiled=True)  16 us
    ppermute x7, starting transfers between devices, _shards(): lax.ppermute(share, DEEP, _along_z(k))  14.7 us
    ppermute x7, waiting for transfers between devices, _shards(): lax.ppermute(share, DEEP, _along_z(k))  13.9 us
    unnamed x28, local copies, waits for them, and re-layouts  8.67 us
    pallas_call x1, Pallas kernels, _shards(): pl.pallas_call(_ladder_kernel, out_shape=jax.ShapeDtypeStruct((16, 256, 2...  8.09 us
    all_to_all x1, starting transfers between devices, _shards(): share = lax.all_to_all(factors, PLANE, 0, 0, tiled=True).reshape(64, 1024)  7.58 us
  transfers between devices with their start and end apart: 11, of which 6 were waited for; matrix products, arithmetic and copies ran while one was open for 0% of the time, Pallas kernels for 2%

profile of v2, /device:TPU:1, one launch (start us, length us, event | category | flops | bytes accessed | tf_op | source)
XLA Modules:
  0.0 147.9 jit_solution(15818422425863625889)
XLA Ops:
  0.0 7.6 %all-to-all-start = ((bf16[16,4,1024]{2,1,0:T(4,128)(2,1)}), bf16[16,4,1024]{2,1,0:T(4,128)(2,1)S(1)}, u32[]{:S(2)}, u32[]{:S(2)}) async-start(bf16[16,4,1024]{2,1,0:T(4,128)(2,1)} %param.12), calls=%async_computation | async-start | bytes 262144 | tf_op jit(solution)/shard_map/all_to_all | solution.py:245
  7.6 0.6 pad_add_fusion.place_ref
  8.2 2.2 %mask_amps.1 = (bf16[16,64,128]{2,1,0:T(8,128)(2,1)}, f32[16,128]{1,0:T(8,128)}) custom-call(s32[4]{0:T(128)} %pad_add_fusion.place_ref, bf16[16,4096]{1,0:T(8,128)(2,1)} %bitcast.9, bf16[16,4096]{1,0:T(8,128)(2,1)} %bitcast.10, s32[8,8,16]{2,1,0:T(8,128)} %bitcast.11), custom_call_target="tpu_custom_call" | custom-call | tf_op jit(solution)/shard_map/mask_amps/pallas_call | solution.py:246
  10.5 4.0 %all-to-all-done = bf16[16,4,1024]{2,1,0:T(4,128)(2,1)S(1)} async-done(((bf16[16,4,1024]{2,1,0:T(4,128)(2,1)}), bf16[16,4,1024]{2,1,0:T(4,128)(2,1)S(1)}, u32[]{:S(2)}, u32[]{:S(2)}) %all-to-all-start) | async-done | bytes 131104 | tf_op jit(solution)/shard_map/all_to_all | solution.py:245
  14.5 22.1 %all_to_all.25.got_ref = bf16[16,64,128]{2,1,0:T(8,128)(2,1)S(1)} all-to-all(bf16[16,64,128]{2,1,0:T(8,128)(2,1)} %get-tuple-element.17.amps_ref), channel_id=1, replica_groups=mesh['x'=4,'zl'=2,'core'=2,'zh'=4,'y'=4] {'zh','zl','core'}, dimensions={0} | all-to-all | bytes 524288 | tf_op jit(solution)/shard_map/all_to_all | solution.py:255
  36.6 0.0 copy-start.2
  36.6 1.0 copy-done.2
  37.7 0.8 make_block.1
  38.5 0.0 copy-start
  38.5 1.4 copy-done
  39.9 0.0 copy-start.13
  39.9 3.9 %all-to-all-start.2 = ((bf16[16,544,128]{2,1,0:T(8,128)(2,1)}), bf16[16,544,128]{2,1,0:T(8,128)(2,1)S(1)}, u32[]{:S(2)}, u32[]{:S(2)}) async-start(bf16[16,544,128]{2,1,0:T(8,128)(2,1)} %copy-done), calls=%async_computation.2 | async-start | bytes 4456448 | tf_op jit(solution)/shard_map/all_to_all | solution.py:266
  43.7 0.0 copy-start.1
  43.7 0.0 copy-start.4
  43.7 0.1 collective-permute-start.6
  43.8 0.6 collective-permute-start.5
  44.4 3.3 %collective-permute-start.4 = (bf16[64,1024]{1,0:T(8,128)(2,1)S(1)}, bf16[64,1024]{1,0:T(8,128)(2,1)S(1)}, u32[]{:S(2)}, u32[]{:S(2)}) collective-permute-start(bf16[64,1024]{1,0:T(8,128)(2,1)S(1)} %reshape.15.refs_0_), channel_id=1, source_target_pairs={{0,40},{32,12},{4,44},{36,0},{8,32},{40,4},{12,36},{44,8},{1,41},{... | collective-permute-start | bytes 393224 | tf_op jit(solution)/shard_map/ppermute | solution.py:265
  47.7 2.2 %collective-permute-start.3 = (bf16[64,1024]{1,0:T(8,128)(2,1)S(1)}, bf16[64,1024]{1,0:T(8,128)(2,1)S(1)}, u32[]{:S(2)}, u32[]{:S(2)}) collective-permute-start(bf16[64,1024]{1,0:T(8,128)(2,1)S(1)} %reshape.15.refs_0_), channel_id=1, source_target_pairs={{0,8},{32,40},{4,12},{36,44},{8,0},{40,32},{12,4},{44,36},{1,9},{3... | collective-permute-start | bytes 393224 | tf_op jit(solution)/shard_map/ppermute | solution.py:265
  50.0 1.1 collective-permute-start.2
  51.1 0.0 collective-permute-done.6.refs_7_
  51.1 2.8 %collective-permute-start.1 = (bf16[64,1024]{1,0:T(8,128)(2,1)S(1)}, bf16[64,1024]{1,0:T(8,128)(2,1)S(1)}, u32[]{:S(2)}, u32[]{:S(2)}) collective-permute-start(bf16[64,1024]{1,0:T(8,128)(2,1)S(1)} %reshape.15.refs_0_), channel_id=1, source_target_pairs={{0,4},{32,36},{4,8},{36,40},{8,12},{40,44},{12,0},{44,32},{1,5},{3... | collective-permute-start | bytes 393224 | tf_op jit(solution)/shard_map/ppermute | solution.py:265
  53.9 1.0 collective-permute-done.5.refs_6_
  54.9 4.5 %collective-permute-start = (bf16[64,1024]{1,0:T(8,128)(2,1)S(1)}, bf16[64,1024]{1,0:T(8,128)(2,1)S(1)}, u32[]{:S(2)}, u32[]{:S(2)}) collective-permute-start(bf16[64,1024]{1,0:T(8,128)(2,1)S(1)} %reshape.15.refs_0_), channel_id=1, source_target_pairs={{0,32},{32,4},{4,36},{36,8},{8,40},{40,12},{12,44},{44,0},{1,33},{... | collective-permute-start | bytes 393224 | tf_op jit(solution)/shard_map/ppermute | solution.py:265
  59.4 0.0 collective-permute-done.4.refs_5_
  59.4 0.0 collective-permute-done.3.refs_4_
  59.4 0.0 copy-start.5
  59.4 0.6 copy-done.5
  60.1 9.2 %collective-permute-done.2.refs_3_ = bf16[64,1024]{1,0:T(8,128)(2,1)S(1)} collective-permute-done((bf16[64,1024]{1,0:T(8,128)(2,1)S(1)}, bf16[64,1024]{1,0:T(8,128)(2,1)S(1)}, u32[]{:S(2)}, u32[]{:S(2)}) %collective-permute-start.2) | collective-permute-done | bytes 131104 | tf_op jit(solution)/shard_map/ppermute | solution.py:265
  69.3 0.0 copy-start.7
  69.3 0.6 copy-done.7
  69.9 0.0 collective-permute-done.1.refs_2_
  69.9 0.0 copy-start.9
  69.9 0.7 copy-done.9
  70.6 3.7 %collective-permute-done.refs_1_ = bf16[64,1024]{1,0:T(8,128)(2,1)S(1)} collective-permute-done((bf16[64,1024]{1,0:T(8,128)(2,1)S(1)}, bf16[64,1024]{1,0:T(8,128)(2,1)S(1)}, u32[]{:S(2)}, u32[]{:S(2)}) %collective-permute-start) | collective-permute-done | bytes 131104 | tf_op jit(solution)/shard_map/ppermute | solution.py:265
  74.3 0.0 copy-start.11
  74.3 0.7 copy-done.11
  74.9 0.7 all-to-all-done.2.refs_8_
  75.7 0.0 copy-done.13
  75.7 0.0 copy-start.6
  75.7 0.9 copy-done.6
  76.6 0.0 copy-start.8
  76.6 0.9 copy-done.8
  77.5 0.0 copy-start.10
  77.5 0.9 copy-done.10
  78.4 0.0 copy-start.12
  78.4 0.9 copy-done.12
  79.3 0.7 order_factors.1
  80.0 0.8 collective-permute-start.8
  80.8 0.3 collective-permute-start.7
  81.1 5.2 %collective-permute-done.7.next_ref = bf16[512,1024]{1,0:T(8,128)(2,1)S(1)} collective-permute-done((bf16[512,1024]{1,0:T(8,128)(2,1)S(1)}, bf16[512,1024]{1,0:T(8,128)(2,1)S(1)}, u32[]{:S(2)}, u32[]{:S(2)}) %collective-permute-start.7) | collective-permute-done | bytes 1048608 | tf_op jit(solution)/shard_map/ppermute | solution.py:277
  86.3 0.0 collective-permute-done.8.other_ref
  86.3 0.0 copy-done.1
  86.3 0.0 copy-done.4
  86.3 8.1 %ladder.1 = bf16[16,256,256]{2,1,0:T(8,128)(2,1)S(1)} custom-call(s32[4]{0:T(128)S(1)} %copy-done.13, bf16[512,1024]{1,0:T(8,128)(2,1)S(1)} %get-tuple-element.21.mine_ref, bf16[512,1024]{1,0:T(8,128)(2,1)S(1)} %collective-permute-done.7.next_ref, bf16[16,544,128]{2,1,0:T(8,128)(2,1)S(1)} %get-tuple-element.22.own_ref, ...), custom_call_target="tpu_custom_call" | custom-call | tf_op jit(solution)/shard_map/ladder/pallas_call | solution.py:279
  94.4 0.0 copy-start.3
  94.4 33.9 %all_to_all.26.part_ref = bf16[16,256,256]{2,1,0:T(8,128)(2,1)S(1)} all-to-all(bf16[16,256,256]{2,1,0:T(8,128)(2,1)S(1)} %ladder.1), channel_id=1, replica_groups=mesh['x'=4,'zl'=2,'core'=2,'zh'=4,'y'=4] {'x','y'}, dimensions={0} | all-to-all | bytes 4194304 | tf_op jit(solution)/shard_map/all_to_all | solution.py:288
  128.3 0.0 copy-done.3
  128.3 1.5 sum_parts.1
  129.7 16.0 %all_to_all.27.rsym_ref = bf16[16,32,128]{2,1,0:T(8,128)(2,1)} all-to-all(bf16[16,32,128]{2,1,0:T(8,128)(2,1)S(1)} %sum_parts.1), channel_id=1, replica_groups=mesh['x'=4,'zl'=2,'core'=2,'zh'=4,'y'=4] {'zh','zl','core'}, dimensions={0} | all-to-all | bytes 262144 | tf_op jit(solution)/shard_map/all_to_all | solution.py:299
  145.8 2.1 %update.1 = bf16[16,4096]{1,0:T(8,128)(2,1)} custom-call(s32[4]{0:T(128)} %pad_add_fusion.place_ref, f32[4]{0:T(128)} %occ_ref.1, bf16[16,32,128]{2,1,0:T(8,128)(2,1)} %all_to_all.27.rsym_ref, bf16[16,64,128]{2,1,0:T(8,128)(2,1)} %get-tuple-element.17.amps_ref, f32[16,128]{1,0:T(8,128)} %get-tuple-element.24.mask_ref, f32[8,128]{1,0:T(8,128)} %bitcast.12), custom_call_target="tpu_custom_call" | custom-call | tf_op jit(solution)/shard_map/update/pallas_call | solution.py:301
  (1 shorter events, 0.0 us)
Async XLA Ops:
  0.0 14.5 %all-to-all-start = ((bf16[16,4,1024]{2,1,0:T(4,128)(2,1)}), bf16[16,4,1024]{2,1,0:T(4,128)(2,1)S(1)}, u32[]{:S(2)}, u32[]{:S(2)}) async-start(bf16[16,4,1024]{2,1,0:T(4,128)(2,1)} %param.12), calls=%async_computation | async-start | bytes 262144 | tf_op jit(solution)/shard_map/all_to_all | solution.py:245
  36.6 1.0 copy-start.2
  38.5 1.4 copy-start
  39.9 35.8 %copy-start.13 = (s32[4]{0:T(128)S(1)}, s32[4]{0:T(128)}, u32[]{:S(2)}) copy-start(s32[4]{0:T(128)} %pad_add_fusion.place_ref) | copy-start | bytes 52
  39.9 35.8 %all-to-all-start.2 = ((bf16[16,544,128]{2,1,0:T(8,128)(2,1)}), bf16[16,544,128]{2,1,0:T(8,128)(2,1)S(1)}, u32[]{:S(2)}, u32[]{:S(2)}) async-start(bf16[16,544,128]{2,1,0:T(8,128)(2,1)} %copy-done), calls=%async_computation.2 | async-start | bytes 4456448 | tf_op jit(solution)/shard_map/all_to_all | solution.py:266
  43.7 42.6 %copy-start.1 = (bf16[2,256,512]{2,1,0:T(8,128)(2,1)S(1)}, bf16[2,256,512]{2,1,0:T(8,128)(2,1)}, u32[]{:S(2)}) copy-start(bf16[2,256,512]{2,1,0:T(8,128)(2,1)} %constant.35.clone.nat_ref) | copy-start | bytes 1572868
  43.7 42.5 %copy-start.4 = (bf16[256,256]{1,0:T(8,128)(2,1)S(1)}, bf16[256,256]{1,0:T(8,128)(2,1)}, u32[]{:S(2)}) copy-start(bf16[256,256]{1,0:T(8,128)(2,1)} %constant.34.clone.rows_ref) | copy-start | bytes 393220
  43.7 7.3 %collective-permute-start.6 = (bf16[64,1024]{1,0:T(8,128)(2,1)S(1)}, bf16[64,1024]{1,0:T(8,128)(2,1)S(1)}, u32[]{:S(2)}, u32[]{:S(2)}) collective-permute-start(bf16[64,1024]{1,0:T(8,128)(2,1)S(1)} %reshape.15.refs_0_), channel_id=1, source_target_pairs={{0,44},{32,0},{4,32},{36,4},{8,36},{40,8},{12,40},{44,12},{1,45},{... | collective-permute-start | bytes 393224 | tf_op jit(solution)/shard_map/ppermute | solution.py:265
  43.8 11.0 %collective-permute-start.5 = (bf16[64,1024]{1,0:T(8,128)(2,1)S(1)}, bf16[64,1024]{1,0:T(8,128)(2,1)S(1)}, u32[]{:S(2)}, u32[]{:S(2)}) collective-permute-start(bf16[64,1024]{1,0:T(8,128)(2,1)S(1)} %reshape.15.refs_0_), channel_id=1, source_target_pairs={{0,12},{32,44},{4,0},{36,32},{8,4},{40,36},{12,8},{44,40},{1,13},{... | collective-permute-start | bytes 393224 | tf_op jit(solution)/shard_map/ppermute | solution.py:265
  44.4 15.0 %collective-permute-start.4 = (bf16[64,1024]{1,0:T(8,128)(2,1)S(1)}, bf16[64,1024]{1,0:T(8,128)(2,1)S(1)}, u32[]{:S(2)}, u32[]{:S(2)}) collective-permute-start(bf16[64,1024]{1,0:T(8,128)(2,1)S(1)} %reshape.15.refs_0_), channel_id=1, source_target_pairs={{0,40},{32,12},{4,44},{36,0},{8,32},{40,4},{12,36},{44,8},{1,41},{... | collective-permute-start | bytes 393224 | tf_op jit(solution)/shard_map/ppermute | solution.py:265
  47.7 11.7 %collective-permute-start.3 = (bf16[64,1024]{1,0:T(8,128)(2,1)S(1)}, bf16[64,1024]{1,0:T(8,128)(2,1)S(1)}, u32[]{:S(2)}, u32[]{:S(2)}) collective-permute-start(bf16[64,1024]{1,0:T(8,128)(2,1)S(1)} %reshape.15.refs_0_), channel_id=1, source_target_pairs={{0,8},{32,40},{4,12},{36,44},{8,0},{40,32},{12,4},{44,36},{1,9},{3... | collective-permute-start | bytes 393224 | tf_op jit(solution)/shard_map/ppermute | solution.py:265
  50.0 19.3 %collective-permute-start.2 = (bf16[64,1024]{1,0:T(8,128)(2,1)S(1)}, bf16[64,1024]{1,0:T(8,128)(2,1)S(1)}, u32[]{:S(2)}, u32[]{:S(2)}) collective-permute-start(bf16[64,1024]{1,0:T(8,128)(2,1)S(1)} %reshape.15.refs_0_), channel_id=1, source_target_pairs={{0,36},{32,8},{4,40},{36,12},{8,44},{40,0},{12,32},{44,4},{1,37},{... | collective-permute-start | bytes 393224 | tf_op jit(solution)/shard_map/ppermute | solution.py:265
  51.1 18.9 %collective-permute-start.1 = (bf16[64,1024]{1,0:T(8,128)(2,1)S(1)}, bf16[64,1024]{1,0:T(8,128)(2,1)S(1)}, u32[]{:S(2)}, u32[]{:S(2)}) collective-permute-start(bf16[64,1024]{1,0:T(8,128)(2,1)S(1)} %reshape.15.refs_0_), channel_id=1, source_target_pairs={{0,4},{32,36},{4,8},{36,40},{8,12},{40,44},{12,0},{44,32},{1,5},{3... | collective-permute-start | bytes 393224 | tf_op jit(solution)/shard_map/ppermute | solution.py:265
  54.9 19.4 %collective-permute-start = (bf16[64,1024]{1,0:T(8,128)(2,1)S(1)}, bf16[64,1024]{1,0:T(8,128)(2,1)S(1)}, u32[]{:S(2)}, u32[]{:S(2)}) collective-permute-start(bf16[64,1024]{1,0:T(8,128)(2,1)S(1)} %reshape.15.refs_0_), channel_id=1, source_target_pairs={{0,32},{32,4},{4,36},{36,8},{8,40},{40,12},{12,44},{44,0},{1,33},{... | collective-permute-start | bytes 393224 | tf_op jit(solution)/shard_map/ppermute | solution.py:265
  59.4 0.7 copy-start.5
  69.3 0.6 copy-start.7
  69.9 0.7 copy-start.9
  74.3 0.7 copy-start.11
  75.7 0.9 copy-start.6
  76.6 0.9 copy-start.8
  77.5 0.9 copy-start.10
  78.4 0.9 copy-start.12
  80.0 6.3 %collective-permute-start.8 = (bf16[16,544,128]{2,1,0:T(8,128)(2,1)S(1)}, bf16[16,544,128]{2,1,0:T(8,128)(2,1)S(1)}, u32[]{:S(2)}, u32[]{:S(2)}) collective-permute-start(bf16[16,544,128]{2,1,0:T(8,128)(2,1)S(1)} %get-tuple-element.22.own_ref), channel_id=1, source_target_pairs={{0,16},{16,0},{1,17},{17,1},{2,18},{18,2},{3,19},{19,3},{4,20},{20... | collective-permute-start | bytes 6684680 | tf_op jit(solution)/shard_map/ppermute | solution.py:276
  80.8 5.5 %collective-permute-start.7 = (bf16[512,1024]{1,0:T(8,128)(2,1)S(1)}, bf16[512,1024]{1,0:T(8,128)(2,1)S(1)}, u32[]{:S(2)}, u32[]{:S(2)}) collective-permute-start(bf16[512,1024]{1,0:T(8,128)(2,1)S(1)} %get-tuple-element.21.mine_ref), channel_id=1, source_target_pairs={{0,16},{16,0},{1,17},{17,1},{2,18},{18,2},{3,19},{19,3},{4,20},{20... | collective-permute-start | bytes 3145736 | tf_op jit(solution)/shard_map/ppermute | solution.py:277
  94.4 33.9 %copy-start.3 = (bf16[3,256,256]{2,1,0:T(8,128)(2,1)S(1)}, bf16[3,256,256]{2,1,0:T(8,128)(2,1)}, u32[]{:S(2)}) copy-start(bf16[3,256,256]{2,1,0:T(8,128)(2,1)} %constant.36.clone.last_ref) | copy-start | bytes 1179652

commit v3 on v1

v3 whole, which is shorter than its diff:
```python
import functools

import jax
import jax.numpy as jnp
import numpy as np
from jax import lax
from jax.experimental import pallas as pl
from jax.experimental.pallas import tpu as pltpu
from jax.sharding import Mesh
from jax.sharding import PartitionSpec as P

AXES = ("x", "zl", "core", "zh", "y")
ROWS = ("x", "zl", "core")
COLS = ("zh", "y")
CHIPS = ("x", "zl")
VMEM = pltpu.CompilerParams(vmem_limit_bytes=40 * 1024 * 1024)
F32 = jnp.float32
BF16 = jnp.bfloat16
NT = (((1,), (1,)), ((), ()))
TN = (((0,), (0,)), ((), ()))


def _one_hot(source_of):
    source_of = np.asarray(source_of).reshape(-1)
    size = source_of.size
    out = np.zeros((size, size), np.float32)
    out[np.arange(size), source_of] = 1
    return out


def _grid(*sizes):
    return np.meshgrid(*[np.arange(s) for s in sizes], indexing="ij")


def _tables():
    j, h = _grid(32, 2)
    rows = _one_hot(h * 32 + j)
    small = np.stack([rows, rows.T, np.eye(64, dtype=np.float32)])
    row, col, k = _grid(16, 16, 4)
    wide = _one_hot(col * 64 + row * 4 + k).T
    row, col, k = _grid(4, 16, 4)
    rows_b = _one_hot(col * 16 + row * 4 + k)
    return [np.asarray(t, jnp.bfloat16) for t in (small, wide, rows_b)]


def _perm(left, right):
    return jnp.dot(left, right, preferred_element_type=F32).astype(BF16)


def _unpack(part):
    return jnp.concatenate([part[:, :64], part[:, 64:]], axis=0)


def _pack(piece):
    return jnp.concatenate([piece[:32], piece[32:]], axis=1)


def _spread_kernel(fac_ref, out_ref, sems):
    copies = [pltpu.make_async_copy(fac_ref, out_ref.at[k * 16 : k * 16 + 16], sems.at[k]) for k in range(4)]
    for copy in copies:
        copy.start()
    for copy in copies:
        copy.wait()


def _mask_kernel(place_ref, amps_ref, source_ref, screen_ref, sent_ref, mask_ref, flat_ref):
    block = screen_ref[place_ref[0]].astype(F32)
    lane_block = (lax.broadcasted_iota(jnp.int32, (8, 128), 1) % 64) // 8
    spread = (lax.broadcasted_iota(jnp.int32, (8, 128), 0) == lane_block).astype(F32)
    mask = lax.dot_general(block, spread, TN, preferred_element_type=F32)
    mask_ref[...] = mask
    for first, ref in ((0, amps_ref), (32, source_ref)):
        for j in range(32):
            tile = ref[:, j * 128 : (j + 1) * 128].astype(F32)
            if first == 0:
                tile = tile * mask
            flat_ref[pl.ds(j, 16, stride=32), :] = tile
        for pair in range(16):
            sent_ref[pair, first : first + 32, :] = flat_ref[pair * 32 : pair * 32 + 32, :].astype(BF16)


def _block_kernel(got_ref, small_ref, wide_ref, near_ref, far_ref, sent_ref, kept_ref, amp_ref, src_ref, sems):
    del near_ref, far_ref

    def block(offset):
        wide = jnp.concatenate([_unpack(got_ref[c, offset : offset + 32, :]) for c in range(16)], axis=1)
        return _perm(small_ref[0], wide)

    amp_ref[...] = _perm(block(0), wide_ref[...])
    copies = [pltpu.make_async_copy(amp_ref, sent_ref.at[to], sems.at[to]) for to in range(8)]
    for copy in copies:
        copy.start()
    src_ref[...] = block(32)
    copies.append(pltpu.make_async_copy(src_ref, kept_ref, sems.at[8]))
    copies[8].start()
    for copy in copies:
        copy.wait()


def _gate_kernel(own_ref, last_ref, out_ref):
    del own_ref, last_ref, out_ref


def _ladder_kernel(
    place_ref,
    mine_ref,
    near_ref,
    far_ref,
    last_ref,
    own_ref,
    other_ref,
    rows_ref,
    keep_ref,
    give_ref,
    amp_ref,
    inner_ref,
    left_ref,
    right_ref,
    sems,
):
    core, y = place_ref[1], place_ref[3]
    behind, ahead, across = (y + 3) % 4, (y + 1) % 4, (y + 2) % 4
    copies = (
        pltpu.make_async_copy(mine_ref, right_ref.at[:, y], sems.at[0]),
        pltpu.make_async_copy(near_ref, right_ref.at[:, behind], sems.at[1]),
        pltpu.make_async_copy(far_ref, right_ref.at[:, ahead], sems.at[2]),
        pltpu.make_async_copy(last_ref, right_ref.at[:, across], sems.at[3]),
        pltpu.make_async_copy(own_ref, amp_ref.at[:, core], sems.at[4]),
        pltpu.make_async_copy(other_ref, amp_ref.at[:, 1 - core], sems.at[5]),
    )
    for copy in copies:
        copy.start()
    for copy in copies[:4]:
        copy.wait()
    for x in range(4):
        rows = [right_ref[col // 4, col % 4, x * 16 : x * 16 + 16, :] for col in range(16)]
        left_ref[x * 256 : x * 256 + 256, :] = _perm(rows_ref[...], jnp.concatenate(rows, axis=0))
    for copy in copies[4:]:
        copy.wait()
    for i in range(4):
        for j in range(4):
            inner_ref[i * 256 : i * 256 + 256, j * 256 : j * 256 + 256] = lax.dot_general(
                amp_ref[i * 2 : i * 2 + 2].reshape(256, 1024),
                right_ref[j].reshape(256, 1024),
                NT,
                preferred_element_type=F32,
            ).astype(BF16)
    first = core == 0
    for x in range(4):
        for j in range(4):
            cols = slice(j * 256, j * 256 + 256)
            part = _perm(left_ref[x * 256 : x * 256 + 256, :], inner_ref[:, cols])
            for zl in range(2):
                zero = part[zl * 128 : zl * 128 + 64]
                one = part[zl * 128 + 64 : zl * 128 + 128]
                keep_ref[x * 2 + zl, :, cols] = jnp.where(first, zero, one)
                give_ref[x * 2 + zl, :, cols] = jnp.where(first, one, zero)


def _sum_kernel(part_ref, kept_ref, wide_ref, resid_ref, sent_ref):
    total = kept_ref[...].astype(F32)
    for chip in range(8):
        total += part_ref[chip].astype(F32)
    resid = total.astype(BF16)
    resid_ref[...] = resid
    natural = _perm(resid, wide_ref[...])
    for row in range(16):
        sent_ref[row] = _pack(natural[:, row * 64 : row * 64 + 64])


def _swap_kernel(got_ref, resid_ref, small_ref, wide_ref, sent_ref):
    tall = jnp.concatenate([_unpack(got_ref[row]) for row in range(16)], axis=0)
    turned = lax.dot_general(small_ref[2], tall, NT, preferred_element_type=F32).astype(BF16)
    turned = lax.dot_general(turned, wide_ref[...], NT, preferred_element_type=F32).astype(BF16)
    straight = _perm(small_ref[1], resid_ref[...])
    turned = _perm(small_ref[1], turned)
    for col in range(16):
        sent_ref[col, :32, :] = _pack(straight[:, col * 64 : col * 64 + 64])
        sent_ref[col, 32:, :] = _pack(turned[:, col * 64 : col * 64 + 64])


def _update_kernel(place_ref, occ_ref, resid_ref, amps_ref, mask_ref, vir_ref, out_ref, flat_ref):
    row = place_ref[5]
    col = place_ref[4]
    exact = lax.Precision.HIGHEST

    def iota(shape, dim):
        return lax.broadcasted_iota(jnp.int32, shape, dim)

    mine = vir_ref[pl.ds(row // 2, 1), :]
    l_row = iota((32, 128), 1) - (row % 2) * 64
    in_row = (l_row // 2 == iota((32, 128), 0)) & (l_row >= 0)
    picked = jnp.where(in_row, jnp.broadcast_to(mine, (32, 128)), 0.0)
    same_half = (iota((128, 128), 0) % 2 == iota((128, 128), 1) // 64).astype(F32)
    vir_a = jnp.dot(picked, same_half, precision=exact, preferred_element_type=F32)
    lane = iota((128, 128), 1)
    want = ((lane // 4) % 2) * 64 + col * 4 + lane % 4
    choose = (iota((128, 128), 0) == want).astype(F32)
    by_block = jnp.dot(vir_ref[...], choose, precision=exact, preferred_element_type=F32)
    own_block = iota((8, 128), 0) == (iota((8, 128), 1) % 64) // 8
    vir_b = jnp.sum(jnp.where(own_block, by_block, 0.0), axis=0, keepdims=True)
    vir = vir_a + vir_b
    for pair in range(16):
        i, j = pair // 4, pair % 4
        denom = (occ_ref[i] + occ_ref[j]) - vir
        rsym = resid_ref[pair, :32].astype(F32) + resid_ref[j * 4 + i, 32:].astype(F32)
        old = amps_ref[pair].astype(F32)
        flat_ref[pair * 32 : pair * 32 + 32, :] = old + mask_ref[pair : pair + 1, :] * (rsym / denom)
    for j in range(32):
        out_ref[:, j * 128 : (j + 1) * 128] = flat_ref[pl.ds(j, 16, stride=32), :].astype(BF16)


def _vmem(shape=None, index=None):
    if shape is None:
        return pl.BlockSpec(memory_space=pltpu.VMEM)
    return pl.BlockSpec(shape, index, memory_space=pltpu.VMEM)


SMEM = pl.BlockSpec(memory_space=pltpu.SMEM)
HBM = pl.BlockSpec(memory_space=pltpu.HBM)


def _sds(*shape, dtype=BF16):
    return jax.ShapeDtypeStruct(shape, dtype)


def _turn(value, step):
    return lax.ppermute(value, "y", [(i, (i + step) % 4) for i in range(4)])


def _shards(tables, amps, source, factors, screen, occ_energy, vir_energy):
    small, wide, rows_b = tables
    x, zl, core = lax.axis_index("x"), lax.axis_index("zl"), lax.axis_index("core")
    zh, y = lax.axis_index("zh"), lax.axis_index("y")
    place = jnp.stack([x * 2 + zl, core, zh, y, zh * 4 + y, x * 4 + zl * 2 + core]).astype(jnp.int32)

    spread = pl.pallas_call(
        _spread_kernel,
        out_shape=_sds(64, 4, 1024),
        in_specs=[_vmem()],
        out_specs=HBM,
        scratch_shapes=[pltpu.SemaphoreType.DMA((4,))],
        name="spread_factors",
    )(factors)
    fac = lax.all_to_all(spread, ("zh",) + ROWS, 0, 0, tiled=True).reshape(4, 64, 1024)
    sent, mask = pl.pallas_call(
        _mask_kernel,
        out_shape=(_sds(16, 64, 128), _sds(16, 128, dtype=F32)),
        in_specs=[SMEM, _vmem(), _vmem(), _vmem()],
        out_specs=(_vmem(), _vmem()),
        scratch_shapes=[pltpu.VMEM((512, 128), F32)],
        name="mask_amps",
    )(place, amps.reshape(16, 4096), source.reshape(16, 4096), screen.transpose(1, 2, 0))
    fac, sent = lax.optimization_barrier((fac, sent))
    near, far = _turn(fac, 1), _turn(fac, 3)
    opposite = _turn(near, 1)
    got = lax.all_to_all(sent, COLS, 0, 0, tiled=True)
    block, kept = pl.pallas_call(
        _block_kernel,
        out_shape=(_sds(8, 64, 1024), _sds(64, 1024)),
        in_specs=[_vmem(), _vmem(), _vmem(), HBM, HBM],
        out_specs=(HBM, HBM),
        scratch_shapes=[
            pltpu.VMEM((64, 1024), BF16),
            pltpu.VMEM((64, 1024), BF16),
            pltpu.SemaphoreType.DMA((9,)),
        ],
        compiler_params=VMEM,
        name="make_block",
    )(got, small, wide, near, far)
    own = lax.all_to_all(block, CHIPS, 0, 0, tiled=True)
    own = pl.pallas_call(
        _gate_kernel,
        out_shape=_sds(8, 64, 1024),
        in_specs=[HBM] * 2,
        out_specs=HBM,
        input_output_aliases={0: 0},
        compiler_params=VMEM,
        name="gate",
    )(own, opposite)
    other = lax.ppermute(own, "core", [(0, 1), (1, 0)])
    square = pltpu.VMEM((1024, 1024), BF16)
    keep, give = pl.pallas_call(
        _ladder_kernel,
        out_shape=(_sds(8, 64, 1024), _sds(8, 64, 1024)),
        in_specs=[SMEM] + [HBM] * 6 + [_vmem()],
        out_specs=(_vmem(), _vmem()),
        scratch_shapes=[
            pltpu.VMEM((8, 2, 64, 1024), BF16),
            square,
            square,
            pltpu.VMEM((4, 4, 64, 1024), BF16),
            pltpu.SemaphoreType.DMA((6,)),
        ],
        compiler_params=VMEM,
        name="ladder",
    )(place, fac, near, far, opposite, own, other, rows_b)
    taken = lax.ppermute(give, "core", [(0, 1), (1, 0)])
    partial = (keep.astype(F32) + taken.astype(F32)).astype(BF16)
    parts = lax.all_to_all(partial, CHIPS, 0, 0, tiled=True)
    resid, turn = pl.pallas_call(
        _sum_kernel,
        out_shape=(_sds(64, 1024), _sds(16, 32, 128)),
        in_specs=[_vmem()] * 3,
        out_specs=(_vmem(), _vmem()),
        compiler_params=VMEM,
        name="sum_parts",
    )(parts, kept, wide)
    turned = lax.all_to_all(turn, ROWS, 0, 0, tiled=True)
    last = pl.pallas_call(
        _swap_kernel,
        out_shape=_sds(16, 64, 128),
        in_specs=[_vmem()] * 4,
        out_specs=_vmem(),
        compiler_params=VMEM,
        name="swap_virtuals",
    )(turned, resid, small, wide)
    back = lax.all_to_all(last, COLS, 0, 0, tiled=True)
    head = _vmem((16, 32, 128), lambda i: (0, 0, 0))
    out = pl.pallas_call(
        _update_kernel,
        out_shape=_sds(16, 4096),
        grid=(1,),
        in_specs=[SMEM, SMEM, _vmem(), head, _vmem(), _vmem()],
        out_specs=_vmem(),
        scratch_shapes=[pltpu.VMEM((512, 128), F32)],
        name="update",
    )(place, occ_energy, back, sent, mask, vir_energy.reshape(8, 128))
    return out.reshape(1, 1, 16, 4096)


def solution(mesh):
    fine = Mesh(mesh.devices.reshape(4, 2, 2, 4, 4), AXES)
    in_specs = (
        P(ROWS, COLS, None, None),
        P(ROWS, COLS, None, None),
        P(None, ROWS + COLS, None),
        P(),
        P(),
        P(),
    )
    shards = functools.partial(_shards, _tables())
    return jax.shard_map(shards, mesh=fine, in_specs=in_specs, out_specs=P(ROWS, COLS, None, None), check_vma=False)
```

time: 162 us -> 139 us (0.86)
  between operations: 13.5 us -> 0.17 us
  starting transfers between devices: 13.7 us -> 24.2 us
  blocking collectives: 70.9 us -> 60.6 us
  waiting for transfers between devices: 40.6 us -> 31.1 us
  local copies, waits for them, and re-layouts: 6.17 us -> 4.43 us
    all_to_all x2, waiting for transfers between devices: 33 us -> 14.4 us  [the longest x1 14.1 us: _shards(): lax.all_to_all(spread, ('zh',) + ROWS, 0, 0, tiled=True)]
    ppermute x0 -> x4, waiting for transfers between devices: none -> 14.4 us  [the longest x3 12.1 us: _turn(): return lax.ppermute(value, 'y', [(i, (i + step) % 4) for i in range(4)])]
    all_to_all x3 -> x4, blocking collectives: 70.9 us -> 60.6 us  [the longest x1 19.6 us: _shards(): parts = lax.all_to_all(partial, CHIPS, 0, 0, tiled=True)]
    all_gather x1 -> x0, waiting for transfers between devices: 7.54 us -> none  [_shards(): fac = lax.all_gather(share, SLOTS, axis=0, tiled=True)]
    all_to_all x2, starting transfers between devices: 10.6 us -> 17.3 us  [the longest x1 13 us: _shards(): lax.all_to_all(spread, ('zh',) + ROWS, 0, 0, tiled=True)]
    ppermute x0 -> x4, starting transfers between devices: none -> 3.28 us  [the longest x3 2.82 us: _turn(): return lax.ppermute(value, 'y', [(i, (i + step) % 4) for i in range(4)])]
    ppermute x1, waiting for transfers between devices: 0.01 us -> 2.29 us  [_shards(): other = lax.ppermute(own, 'core', [(0, 1), (1, 0)])]
    unnamed x15 -> x28, local copies, waits for them, and re-layouts: 5.48 us -> 3.69 us
  transfers between devices with their start and end apart: 4 -> 7, of which waited for: 3 -> 5; matrix products, arithmetic and copies ran while one was open for 0% -> 0% of each run, Pallas kernels for 0% -> 2%
where the time goes in v3:
time: 139 us; the launch traced here: 138 us
  blocking collectives  60.6 us (44%)
  waiting for transfers between devices  31.1 us (22%)
  starting transfers between devices  24.2 us (17%)
  Pallas kernels  16.8 us (12%)
  local copies, waits for them, and re-layouts  4.43 us (3%)
    all_to_all x1, blocking collectives, _shards(): parts = lax.all_to_all(partial, CHIPS, 0, 0, tiled=True)  19.6 us
    all_to_all x1, blocking collectives, _shards(): got = lax.all_to_all(sent, COLS, 0, 0, tiled=True)  16.9 us
    all_to_all x1, waiting for transfers between devices, _shards(): lax.all_to_all(spread, ('zh',) + ROWS, 0, 0, tiled=True)  14.1 us
    all_to_all x1, blocking collectives, _shards(): back = lax.all_to_all(last, COLS, 0, 0, tiled=True)  13.6 us
    all_to_all x1, starting transfers between devices, _shards(): lax.all_to_all(spread, ('zh',) + ROWS, 0, 0, tiled=True)  13 us
    ppermute x3, waiting for transfers between devices, _turn(): return lax.ppermute(value, 'y', [(i, (i + step) % 4) for i in range(4)])  12.1 us
    all_to_all x1, blocking collectives, _shards(): turned = lax.all_to_all(turn, ROWS, 0, 0, tiled=True)  10.5 us
    pallas_call x1, Pallas kernels, _shards(): pl.pallas_call(_ladder_kernel, out_shape=(_sds(8, 64, 1024), _sds(8, 64,...  6.16 us
  transfers between devices with their start and end apart: 7, of which 5 were waited for; matrix products, arithmetic and copies ran while one was open for 0% of the time, Pallas kernels for 2%

profile of v3, /device:TPU:1, one launch (start us, length us, event | category | flops | bytes accessed | tf_op | source)
XLA Modules:
  0.0 137.7 jit_solution(12599754137105809297)
XLA Ops:
  0.0 0.0 copy-start
  0.0 0.0 copy-start.11
  0.0 1.9 %spread_factors.1 = bf16[64,4,1024]{2,1,0:T(4,128)(2,1)} custom-call(bf16[16,4,1024]{2,1,0:T(4,128)(2,1)} %fac_ref.1), custom_call_target="tpu_custom_call" | custom-call | tf_op jit(solution)/shard_map/spread_factors/pallas_call | solution.py:237
  1.9 13.0 %all-to-all-start = ((bf16[64,4,1024]{2,1,0:T(4,128)(2,1)}), bf16[64,4,1024]{2,1,0:T(4,128)(2,1)S(1)}, u32[]{:S(2)}, u32[]{:S(2)}) async-start(bf16[64,4,1024]{2,1,0:T(4,128)(2,1)} %spread_factors.1), calls=%async_computation | async-start | bytes 1048576 | tf_op jit(solution)/shard_map/all_to_all | solution.py:245
  14.9 0.6 stack.27.place_ref
  15.5 2.2 %mask_amps.1 = (bf16[16,64,128]{2,1,0:T(8,128)(2,1)}, f32[16,128]{1,0:T(8,128)}) custom-call(s32[6]{0:T(128)} %stack.27.place_ref, bf16[16,4096]{1,0:T(8,128)(2,1)} %bitcast.11, bf16[16,4096]{1,0:T(8,128)(2,1)} %bitcast.12, s32[8,8,16]{2,1,0:T(8,128)} %bitcast.13), custom_call_target="tpu_custom_call" | custom-call | tf_op jit(solution)/shard_map/mask_amps/pallas_call | solution.py:246
  17.8 14.1 %all-to-all-done = bf16[64,4,1024]{2,1,0:T(4,128)(2,1)S(1)} async-done(((bf16[64,4,1024]{2,1,0:T(4,128)(2,1)}), bf16[64,4,1024]{2,1,0:T(4,128)(2,1)S(1)}, u32[]{:S(2)}, u32[]{:S(2)}) %all-to-all-start) | async-done | bytes 524320 | tf_op jit(solution)/shard_map/all_to_all | solution.py:245
  31.9 0.1 reshape.15.mine_ref
  32.0 0.0 copy-start.4
  32.0 2.8 %collective-permute-start.1 = (bf16[4,64,1024]{2,1,0:T(8,128)(2,1)S(1)}, bf16[4,64,1024]{2,1,0:T(8,128)(2,1)S(1)}, u32[]{:S(2)}, u32[]{:S(2)}) collective-permute-start(bf16[4,64,1024]{2,1,0:T(8,128)(2,1)S(1)} %reshape.15.mine_ref), channel_id=1, source_target_pairs={{0,3},{1,0},{2,1},{3,2},{4,7},{5,4},{6,5},{7,6},{8,11},{9,8},{10,9... | collective-permute-start | bytes 1572872 | tf_op jit(solution)/shard_map/ppermute | solution.py:228
  34.8 0.0 collective-permute-start
  34.8 16.9 %all_to_all.30.got_ref = bf16[16,64,128]{2,1,0:T(8,128)(2,1)S(1)} all-to-all(bf16[16,64,128]{2,1,0:T(8,128)(2,1)} %get-tuple-element.17.amps_ref), channel_id=1, replica_groups=mesh['x'=4,'zl'=2,'core'=2,'zh'=4,'y'=4] {'zh','y'}, dimensions={0} | all-to-all | bytes 524288 | tf_op jit(solution)/shard_map/all_to_all | solution.py:257
  51.7 0.0 collective-permute-done.1.far_ref
  51.7 0.0 collective-permute-done.near_ref
  51.7 0.0 copy-done
  51.7 0.0 copy-done.11
  51.7 0.0 copy-start.8
  51.7 2.6 %make_block.1 = (bf16[8,64,1024]{2,1,0:T(8,128)(2,1)S(1)}, bf16[64,1024]{1,0:T(8,128)(2,1)S(1)}) custom-call(bf16[16,64,128]{2,1,0:T(8,128)(2,1)S(1)} %all_to_all.30.got_ref, bf16[3,64,64]{2,1,0:T(8,128)(2,1)S(1)} %copy-done.11, bf16[1024,1024]{1,0:T(8,128)(2,1)S(1)} %copy-done, bf16[4,64,1024]{2,1,0:T(8,128)(2,1)S(1)} %collective-permute-done.near_ref, ...), custom_call_target="tpu_custom_call" | custom-call | tf_op jit(solution)/shard_map/make_block/pallas_call | solution.py:258
  54.4 0.0 copy-done.8
  54.4 0.0 copy-start.6
  54.4 0.8 copy-done.6
  55.2 0.0 copy-start.10
  55.2 1.0 copy-done.10
  56.2 0.0 copy-start.12
  56.2 0.0 copy-start.13
  56.2 0.0 copy-done.4
  56.2 4.3 %all-to-all-start.2 = ((bf16[8,64,1024]{2,1,0:T(8,128)(2,1)}), bf16[8,64,1024]{2,1,0:T(8,128)(2,1)S(1)}, u32[]{:S(2)}, u32[]{:S(2)}) async-start(bf16[8,64,1024]{2,1,0:T(8,128)(2,1)} %copy-done.10), calls=%async_computation.2 | async-start | bytes 2097152 | tf_op jit(solution)/shard_map/all_to_all | solution.py:271
  60.5 0.0 collective-permute-start.2
  60.5 12.1 %collective-permute-done.2.last_ref = bf16[4,64,1024]{2,1,0:T(8,128)(2,1)S(1)} collective-permute-done((bf16[4,64,1024]{2,1,0:T(8,128)(2,1)}, bf16[4,64,1024]{2,1,0:T(8,128)(2,1)S(1)}, u32[]{:S(2)}, u32[]{:S(2)}) %collective-permute-start.2) | collective-permute-done | bytes 524320 | tf_op jit(solution)/shard_map/ppermute | solution.py:228
  72.6 0.0 copy-start.1
  72.6 0.8 copy-done.1
  73.4 0.3 all-to-all-done.2.own_ref
  73.7 0.0 copy-start.2
  73.7 1.0 copy-done.2
  74.8 0.0 copy-start.3
  74.8 0.0 copy-start.5
  74.8 0.0 copy-start.7
  74.8 0.0 copy-start.9
  74.8 3.6 %collective-permute-start.3 = (bf16[8,64,1024]{2,1,0:T(8,128)(2,1)S(1)}, bf16[8,64,1024]{2,1,0:T(8,128)(2,1)S(1)}, u32[]{:S(2)}, u32[]{:S(2)}) collective-permute-start(bf16[8,64,1024]{2,1,0:T(8,128)(2,1)S(1)} %gate.1.own_ref), channel_id=1, source_target_pairs={{0,16},{16,0},{1,17},{17,1},{2,18},{18,2},{3,19},{19,3},{4,20},{20... | collective-permute-start | bytes 3145736 | tf_op jit(solution)/shard_map/ppermute | solution.py:281
  78.4 2.3 %collective-permute-done.3.other_ref = bf16[8,64,1024]{2,1,0:T(8,128)(2,1)S(1)} collective-permute-done((bf16[8,64,1024]{2,1,0:T(8,128)(2,1)S(1)}, bf16[8,64,1024]{2,1,0:T(8,128)(2,1)S(1)}, u32[]{:S(2)}, u32[]{:S(2)}) %collective-permute-start.3) | collective-permute-done | bytes 1048608 | tf_op jit(solution)/shard_map/ppermute | solution.py:281
  80.7 0.0 copy-done.12
  80.7 0.0 copy-done.13
  80.7 0.0 copy-done.3
  80.7 0.0 copy-done.5
  80.7 0.0 copy-done.7
  80.7 0.0 copy-done.9
  80.7 6.2 %ladder.1 = (bf16[8,64,1024]{2,1,0:T(8,128)(2,1)S(1)}, bf16[8,64,1024]{2,1,0:T(8,128)(2,1)S(1)}) custom-call(s32[6]{0:T(128)S(1)} %copy-done.13, bf16[4,64,1024]{2,1,0:T(8,128)(2,1)S(1)} %copy-done.5, bf16[4,64,1024]{2,1,0:T(8,128)(2,1)S(1)} %copy-done.9, bf16[4,64,1024]{2,1,0:T(8,128)(2,1)S(1)} %copy-done.7, bf16[4,64,1024]{2,1,0:T(8,128)(2,1)S(1)} %copy-done.3, ...), custom_call_target="tpu_custom_call" | custom-call | tf_op jit(solution)/shard_map/ladder/pallas_call | solution.py:283
  86.9 0.5 collective-permute-start.4
  87.4 2.3 %collective-permute-done.4 = bf16[8,64,1024]{2,1,0:T(8,128)(2,1)S(1)} collective-permute-done((bf16[8,64,1024]{2,1,0:T(8,128)(2,1)S(1)}, bf16[8,64,1024]{2,1,0:T(8,128)(2,1)S(1)}, u32[]{:S(2)}, u32[]{:S(2)}) %collective-permute-start.4) | collective-permute-done | bytes 1048608 | tf_op jit(solution)/shard_map/ppermute | solution.py:298
  89.7 0.4 add_convert_fusion
  90.1 19.6 %all_to_all.31.part_ref = bf16[8,64,1024]{2,1,0:T(8,128)(2,1)S(1)} all-to-all(bf16[8,64,1024]{2,1,0:T(8,128)(2,1)S(1)} %add_convert_fusion), channel_id=1, replica_groups=mesh['x'=4,'zl'=2,'core'=2,'zh'=4,'y'=4] {'x','zl'}, dimensions={0} | all-to-all | bytes 2097152 | tf_op jit(solution)/shard_map/all_to_all | solution.py:300
  109.7 0.6 sum_parts.1
  110.3 10.5 %all_to_all.32.got_ref = bf16[16,32,128]{2,1,0:T(8,128)(2,1)S(1)} all-to-all(bf16[16,32,128]{2,1,0:T(8,128)(2,1)S(1)} %get-tuple-element.22), channel_id=1, replica_groups=mesh['x'=4,'zl'=2,'core'=2,'zh'=4,'y'=4] {'x','zl','core'}, dimensions={0} | all-to-all | bytes 262144 | tf_op jit(solution)/shard_map/all_to_all | solution.py:309
  120.8 1.1 swap_virtuals.1
  121.9 13.6 %all_to_all.33.resid_ref = bf16[16,64,128]{2,1,0:T(8,128)(2,1)} all-to-all(bf16[16,64,128]{2,1,0:T(8,128)(2,1)S(1)} %swap_virtuals.1), channel_id=1, replica_groups=mesh['x'=4,'zl'=2,'core'=2,'zh'=4,'y'=4] {'zh','y'}, dimensions={0} | all-to-all | bytes 524288 | tf_op jit(solution)/shard_map/all_to_all | solution.py:318
  135.6 2.1 %update.1 = bf16[16,4096]{1,0:T(8,128)(2,1)} custom-call(s32[6]{0:T(128)} %stack.27.place_ref, f32[4]{0:T(128)} %occ_ref.1, bf16[16,64,128]{2,1,0:T(8,128)(2,1)} %all_to_all.33.resid_ref, bf16[16,64,128]{2,1,0:T(8,128)(2,1)} %get-tuple-element.17.amps_ref, f32[16,128]{1,0:T(8,128)} %get-tuple-element.24.mask_ref, f32[8,128]{1,0:T(8,128)} %bitcast.14), custom_call_target="tpu_custom_call" | custom-call | tf_op jit(solution)/shard_map/update/pallas_call | solution.py:320
  (1 shorter events, 0.0 us)
Async XLA Ops:
  0.0 51.7 %copy-start = (bf16[1024,1024]{1,0:T(8,128)(2,1)S(1)}, bf16[1024,1024]{1,0:T(8,128)(2,1)}, u32[]{:S(2)}) copy-start(bf16[1024,1024]{1,0:T(8,128)(2,1)} %constant.32.clone.wide_ref) | copy-start | bytes 6291460
  0.0 51.7 %copy-start.11 = (bf16[3,64,64]{2,1,0:T(8,128)(2,1)S(1)}, bf16[3,64,64]{2,1,0:T(8,128)(2,1)}, u32[]{:S(2)}) copy-start(bf16[3,64,64]{2,1,0:T(8,128)(2,1)} %constant.31.clone.small_ref) | copy-start | bytes 73732
  1.9 30.0 %all-to-all-start = ((bf16[64,4,1024]{2,1,0:T(4,128)(2,1)}), bf16[64,4,1024]{2,1,0:T(4,128)(2,1)S(1)}, u32[]{:S(2)}, u32[]{:S(2)}) async-start(bf16[64,4,1024]{2,1,0:T(4,128)(2,1)} %spread_factors.1), calls=%async_computation | async-start | bytes 1048576 | tf_op jit(solution)/shard_map/all_to_all | solution.py:245
  32.0 24.2 %copy-start.4 = (bf16[4,64,1024]{2,1,0:T(8,128)(2,1)}, bf16[4,64,1024]{2,1,0:T(8,128)(2,1)S(1)}, u32[]{:S(2)}) copy-start(bf16[4,64,1024]{2,1,0:T(8,128)(2,1)S(1)} %reshape.15.mine_ref) | copy-start | bytes 1572868
  32.0 19.7 %collective-permute-start.1 = (bf16[4,64,1024]{2,1,0:T(8,128)(2,1)S(1)}, bf16[4,64,1024]{2,1,0:T(8,128)(2,1)S(1)}, u32[]{:S(2)}, u32[]{:S(2)}) collective-permute-start(bf16[4,64,1024]{2,1,0:T(8,128)(2,1)S(1)} %reshape.15.mine_ref), channel_id=1, source_target_pairs={{0,3},{1,0},{2,1},{3,2},{4,7},{5,4},{6,5},{7,6},{8,11},{9,8},{10,9... | collective-permute-start | bytes 1572872 | tf_op jit(solution)/shard_map/ppermute | solution.py:228
  34.8 16.9 %collective-permute-start = (bf16[4,64,1024]{2,1,0:T(8,128)(2,1)S(1)}, bf16[4,64,1024]{2,1,0:T(8,128)(2,1)S(1)}, u32[]{:S(2)}, u32[]{:S(2)}) collective-permute-start(bf16[4,64,1024]{2,1,0:T(8,128)(2,1)S(1)} %reshape.15.mine_ref), channel_id=1, source_target_pairs={{0,1},{1,2},{2,3},{3,0},{4,5},{5,6},{6,7},{7,4},{8,9},{9,10},{10,1... | collective-permute-start | bytes 1572872 | tf_op jit(solution)/shard_map/ppermute | solution.py:228
  51.7 2.6 %copy-start.8 = (bf16[4,64,1024]{2,1,0:T(8,128)(2,1)}, bf16[4,64,1024]{2,1,0:T(8,128)(2,1)S(1)}, u32[]{:S(2)}) copy-start(bf16[4,64,1024]{2,1,0:T(8,128)(2,1)S(1)} %collective-permute-done.near_ref) | copy-start | bytes 1572868
  54.4 0.8 copy-start.6
  55.2 1.0 copy-start.10
  56.2 24.5 %copy-start.12 = (bf16[256,256]{1,0:T(8,128)(2,1)S(1)}, bf16[256,256]{1,0:T(8,128)(2,1)}, u32[]{:S(2)}) copy-start(bf16[256,256]{1,0:T(8,128)(2,1)} %constant.33.clone.rows_ref) | copy-start | bytes 393220
  56.2 24.5 %copy-start.13 = (s32[6]{0:T(128)S(1)}, s32[6]{0:T(128)}, u32[]{:S(2)}) copy-start(s32[6]{0:T(128)} %stack.27.place_ref) | copy-start | bytes 76
  56.2 17.5 %all-to-all-start.2 = ((bf16[8,64,1024]{2,1,0:T(8,128)(2,1)}), bf16[8,64,1024]{2,1,0:T(8,128)(2,1)S(1)}, u32[]{:S(2)}, u32[]{:S(2)}) async-start(bf16[8,64,1024]{2,1,0:T(8,128)(2,1)} %copy-done.10), calls=%async_computation.2 | async-start | bytes 2097152 | tf_op jit(solution)/shard_map/all_to_all | solution.py:271
  60.5 12.1 %collective-permute-start.2 = (bf16[4,64,1024]{2,1,0:T(8,128)(2,1)}, bf16[4,64,1024]{2,1,0:T(8,128)(2,1)S(1)}, u32[]{:S(2)}, u32[]{:S(2)}) collective-permute-start(bf16[4,64,1024]{2,1,0:T(8,128)(2,1)} %copy-done.8), channel_id=1, source_target_pairs={{0,1},{1,2},{2,3},{3,0},{4,5},{5,6},{6,7},{7,4},{8,9},{9,10},{10,1... | collective-permute-start | bytes 1572872 | tf_op jit(solution)/shard_map/ppermute | solution.py:228
  72.6 0.8 copy-start.1
  73.7 1.0 copy-start.2
  74.8 5.9 %copy-start.3 = (bf16[4,64,1024]{2,1,0:T(8,128)(2,1)S(1)}, bf16[4,64,1024]{2,1,0:T(8,128)(2,1)}, u32[]{:S(2)}) copy-start(bf16[4,64,1024]{2,1,0:T(8,128)(2,1)} %copy-done.1) | copy-start | bytes 1572868
  74.8 5.9 %copy-start.5 = (bf16[4,64,1024]{2,1,0:T(8,128)(2,1)S(1)}, bf16[4,64,1024]{2,1,0:T(8,128)(2,1)}, u32[]{:S(2)}) copy-start(bf16[4,64,1024]{2,1,0:T(8,128)(2,1)} %copy-done.4) | copy-start | bytes 1572868
  74.8 5.9 %copy-start.7 = (bf16[4,64,1024]{2,1,0:T(8,128)(2,1)S(1)}, bf16[4,64,1024]{2,1,0:T(8,128)(2,1)}, u32[]{:S(2)}) copy-start(bf16[4,64,1024]{2,1,0:T(8,128)(2,1)} %copy-done.6) | copy-start | bytes 1572868
  74.8 6.0 %copy-start.9 = (bf16[4,64,1024]{2,1,0:T(8,128)(2,1)S(1)}, bf16[4,64,1024]{2,1,0:T(8,128)(2,1)}, u32[]{:S(2)}) copy-start(bf16[4,64,1024]{2,1,0:T(8,128)(2,1)} %copy-done.8) | copy-start | bytes 1572868
  74.8 5.9 %collective-permute-start.3 = (bf16[8,64,1024]{2,1,0:T(8,128)(2,1)S(1)}, bf16[8,64,1024]{2,1,0:T(8,128)(2,1)S(1)}, u32[]{:S(2)}, u32[]{:S(2)}) collective-permute-start(bf16[8,64,1024]{2,1,0:T(8,128)(2,1)S(1)} %gate.1.own_ref), channel_id=1, source_target_pairs={{0,16},{16,0},{1,17},{17,1},{2,18},{18,2},{3,19},{19,3},{4,20},{20... | collective-permute-start | bytes 3145736 | tf_op jit(solution)/shard_map/ppermute | solution.py:281
  86.9 2.8 %collective-permute-start.4 = (bf16[8,64,1024]{2,1,0:T(8,128)(2,1)S(1)}, bf16[8,64,1024]{2,1,0:T(8,128)(2,1)S(1)}, u32[]{:S(2)}, u32[]{:S(2)}) collective-permute-start(bf16[8,64,1024]{2,1,0:T(8,128)(2,1)S(1)} %get-tuple-element.20), channel_id=1, source_target_pairs={{0,16},{16,0},{1,17},{17,1},{2,18},{18,2},{3,19},{19,3},{4,20},{20... | collective-permute-start | bytes 3145736 | tf_op jit(solution)/shard_map/ppermute | solution.py:298

commit v4 on v3

--- a/solution.py
+++ b/solution.py
@@ -63,42 +63,86 @@
         copy.wait()
 
 
-def _mask_kernel(place_ref, amps_ref, source_ref, screen_ref, sent_ref, mask_ref, flat_ref):
+def _mask_kernel(
+    place_ref,
+    amps_ref,
+    source_ref,
+    screen_ref,
+    held_ref,
+    mask_ref,
+    out0,
+    out1,
+    out2,
+    out3,
+    flat_ref,
+    flat2_ref,
+):
     block = screen_ref[place_ref[0]].astype(F32)
     lane_block = (lax.broadcasted_iota(jnp.int32, (8, 128), 1) % 64) // 8
     spread = (lax.broadcasted_iota(jnp.int32, (8, 128), 0) == lane_block).astype(F32)
     mask = lax.dot_general(block, spread, TN, preferred_element_type=F32)
     mask_ref[...] = mask
-    for first, ref in ((0, amps_ref), (32, source_ref)):
-        for j in range(32):
-            tile = ref[:, j * 128 : (j + 1) * 128].astype(F32)
-            if first == 0:
-                tile = tile * mask
-            flat_ref[pl.ds(j, 16, stride=32), :] = tile
-        for pair in range(16):
-            sent_ref[pair, first : first + 32, :] = flat_ref[pair * 32 : pair * 32 + 32, :].astype(BF16)
-
-
-def _block_kernel(got_ref, small_ref, wide_ref, near_ref, far_ref, sent_ref, kept_ref, amp_ref, src_ref, sems):
-    del near_ref, far_ref
+    y = place_ref[3]
+    for j in range(32):
+        tile = slice(j * 128, (j + 1) * 128)
+        flat_ref[pl.ds(j, 16, stride=32), :] = amps_ref[:, tile].astype(F32) * mask
+        flat2_ref[pl.ds(j, 16, stride=32), :] = source_ref[:, tile].astype(F32)
+    for pair in range(16):
+        held_ref[pair, :32] = flat_ref[pair * 32 : pair * 32 + 32, :].astype(BF16)
+        held_ref[pair, 32:] = flat2_ref[pair * 32 : pair * 32 + 32, :].astype(BF16)
+    for k, out in enumerate((out0, out1, out2, out3)):
+        to = (y + k) % 4
+        for zh in range(4):
+            rows = pl.ds(pl.multiple_of(zh * 128 + to * 32, 32), 32)
+            turned = pl.ds(pl.multiple_of(to * 128 + zh * 32, 32), 32)
+            out[zh, :32, :] = flat_ref[rows, :].astype(BF16)
+            out[zh, 32:64, :] = flat_ref[turned, :].astype(BF16)
+            out[zh, 64:, :] = flat2_ref[turned, :].astype(BF16)
+
+
+def _relay_kernel(place_ref, in0, in1, in2, in3, out0, out1, out2, out3):
+    zh, y = place_ref[2], place_ref[3]
+    for m, out in enumerate((out0, out1, out2, out3)):
+        for k, ref in enumerate((in0, in1, in2, in3)):
+            out[(y + 4 - k) % 4] = ref[(zh + m) % 4]
+
+
+def _block_kernel(place_ref, in0, in1, in2, in3, small_ref, wide_ref, amp_ref, sent_ref, got_ref):
+    zh = place_ref[2]
+    for m, ref in enumerate((in0, in1, in2, in3)):
+        got_ref[(zh + 4 - m) % 4] = ref[...]
 
     def block(offset):
-        wide = jnp.concatenate([_unpack(got_ref[c, offset : offset + 32, :]) for c in range(16)], axis=1)
-        return _perm(small_ref[0], wide)
-
-    amp_ref[...] = _perm(block(0), wide_ref[...])
-    copies = [pltpu.make_async_copy(amp_ref, sent_ref.at[to], sems.at[to]) for to in range(8)]
-    for copy in copies:
-        copy.start()
-    src_ref[...] = block(32)
-    copies.append(pltpu.make_async_copy(src_ref, kept_ref, sems.at[8]))
-    copies[8].start()
-    for copy in copies:
-        copy.wait()
-
-
-def _gate_kernel(own_ref, last_ref, out_ref):
-    del own_ref, last_ref, out_ref
+        parts = [_unpack(got_ref[c // 4, c % 4, offset : offset + 32, :]) for c in range(16)]
+        return _perm(small_ref[0], jnp.concatenate(parts, axis=1))
+
+    whole = jnp.concatenate([block(0), block(32), block(64)], axis=0)
+    whole = _perm(whole, wide_ref[...])
+    amp_ref[...] = whole[:64]
+    for row in range(16):
+        cols = slice(row * 64, row * 64 + 64)
+        sent_ref[row, :32, :] = _pack(whole[64:128, cols])
+        sent_ref[row, 32:, :] = _pack(whole[128:, cols])
+
+
+def _symmetric_kernel(
+    got_ref, amp_ref, small_ref, wide_ref, near_ref, far_ref, last_ref, sent_ref, kept_ref
+):
+    del near_ref, far_ref, last_ref
+
+    def turned(offset):
+        tall = jnp.concatenate([_unpack(got_ref[row, offset : offset + 32, :]) for row in range(16)], axis=0)
+        return lax.dot_general(small_ref[2], tall, NT, preferred_element_type=F32)
+
+    block = (amp_ref[...].astype(F32) + turned(0)).astype(BF16)
+    for to in range(8):
+        sent_ref[to] = block
+    source = turned(32).astype(BF16)
+    kept_ref[...] = lax.dot_general(source, wide_ref[...], NT, preferred_element_type=F32).astype(BF16)
+
+
+def _gate_kernel(value_ref, small_ref, out_ref):
+    del value_ref, small_ref, out_ref
 
 
 def _ladder_kernel(
@@ -157,29 +201,16 @@
                 give_ref[x * 2 + zl, :, cols] = jnp.where(first, one, zero)
 
 
-def _sum_kernel(part_ref, kept_ref, wide_ref, resid_ref, sent_ref):
+def _sum_kernel(part_ref, kept_ref, small_ref, sent_ref):
     total = kept_ref[...].astype(F32)
     for chip in range(8):
         total += part_ref[chip].astype(F32)
-    resid = total.astype(BF16)
-    resid_ref[...] = resid
-    natural = _perm(resid, wide_ref[...])
-    for row in range(16):
-        sent_ref[row] = _pack(natural[:, row * 64 : row * 64 + 64])
-
-
-def _swap_kernel(got_ref, resid_ref, small_ref, wide_ref, sent_ref):
-    tall = jnp.concatenate([_unpack(got_ref[row]) for row in range(16)], axis=0)
-    turned = lax.dot_general(small_ref[2], tall, NT, preferred_element_type=F32).astype(BF16)
-    turned = lax.dot_general(turned, wide_ref[...], NT, preferred_element_type=F32).astype(BF16)
-    straight = _perm(small_ref[1], resid_ref[...])
-    turned = _perm(small_ref[1], turned)
+    total = _perm(small_ref[1], total.astype(BF16))
     for col in range(16):
-        sent_ref[col, :32, :] = _pack(straight[:, col * 64 : col * 64 + 64])
-        sent_ref[col, 32:, :] = _pack(turned[:, col * 64 : col * 64 + 64])
-
-
-def _update_kernel(place_ref, occ_ref, resid_ref, amps_ref, mask_ref, vir_ref, out_ref, flat_ref):
+        sent_ref[col] = _pack(total[:, col * 64 : col * 64 + 64])
+
+
+def _update_kernel(place_ref, occ_ref, resid_ref, held_ref, mask_ref, vir_ref, out_ref, flat_ref):
     row = place_ref[5]
     col = place_ref[4]
     exact = lax.Precision.HIGHEST
@@ -203,29 +234,45 @@
     for pair in range(16):
         i, j = pair // 4, pair % 4
         denom = (occ_ref[i] + occ_ref[j]) - vir
-        rsym = resid_ref[pair, :32].astype(F32) + resid_ref[j * 4 + i, 32:].astype(F32)
-        old = amps_ref[pair].astype(F32)
+        rsym = resid_ref[pair].astype(F32) + held_ref[pair, 32:].astype(F32)
+        old = held_ref[pair, :32].astype(F32)
         flat_ref[pair * 32 : pair * 32 + 32, :] = old + mask_ref[pair : pair + 1, :] * (rsym / denom)
     for j in range(32):
         out_ref[:, j * 128 : (j + 1) * 128] = flat_ref[pl.ds(j, 16, stride=32), :].astype(BF16)
 
 
-def _vmem(shape=None, index=None):
-    if shape is None:
-        return pl.BlockSpec(memory_space=pltpu.VMEM)
-    return pl.BlockSpec(shape, index, memory_space=pltpu.VMEM)
+def _vmem():
+    return pl.BlockSpec(memory_space=pltpu.VMEM)
 
 
 SMEM = pl.BlockSpec(memory_space=pltpu.SMEM)
 HBM = pl.BlockSpec(memory_space=pltpu.HBM)
+ANY = pl.BlockSpec(memory_space=pl.ANY)
 
 
 def _sds(*shape, dtype=BF16):
     return jax.ShapeDtypeStruct(shape, dtype)
 
 
-def _turn(value, step):
-    return lax.ppermute(value, "y", [(i, (i + step) % 4) for i in range(4)])
+def _turn(value, axis, step):
+    if step == 0:
+        return value
+    return lax.ppermute(value, axis, [(i, (i + step) % 4) for i in range(4)])
+
+
+def _swap_cores(value):
+    return lax.ppermute(value, "core", [(0, 1), (1, 0)])
+
+
+def _after(value, small):
+    return pl.pallas_call(
+        _gate_kernel,
+        out_shape=jax.ShapeDtypeStruct(value.shape, value.dtype),
+        in_specs=[ANY, ANY],
+        out_specs=ANY,
+        input_output_aliases={0: 0},
+        name="gate",
+    )(value, small)
 
 
 def _shards(tables, amps, source, factors, screen, occ_energy, vir_energy):
@@ -243,42 +290,47 @@
         name="spread_factors",
     )(factors)
     fac = lax.all_to_all(spread, ("zh",) + ROWS, 0, 0, tiled=True).reshape(4, 64, 1024)
-    sent, mask = pl.pallas_call(
+    four = _sds(4, 96, 128)
+    held, mask, *outs = pl.pallas_call(
         _mask_kernel,
-        out_shape=(_sds(16, 64, 128), _sds(16, 128, dtype=F32)),
+        out_shape=(_sds(16, 64, 128), _sds(16, 128, dtype=F32)) + (four,) * 4,
         in_specs=[SMEM, _vmem(), _vmem(), _vmem()],
-        out_specs=(_vmem(), _vmem()),
-        scratch_shapes=[pltpu.VMEM((512, 128), F32)],
+        out_specs=(_vmem(),) * 6,
+        scratch_shapes=[pltpu.VMEM((512, 128), F32)] * 2,
         name="mask_amps",
     )(place, amps.reshape(16, 4096), source.reshape(16, 4096), screen.transpose(1, 2, 0))
-    fac, sent = lax.optimization_barrier((fac, sent))
-    near, far = _turn(fac, 1), _turn(fac, 3)
-    opposite = _turn(near, 1)
-    got = lax.all_to_all(sent, COLS, 0, 0, tiled=True)
-    block, kept = pl.pallas_call(
+    outs = [_turn(out, "y", k) for k, out in enumerate(outs)]
+    outs = pl.pallas_call(
+        _relay_kernel,
+        out_shape=(four,) * 4,
+        in_specs=[SMEM] + [_vmem()] * 4,
+        out_specs=(_vmem(),) * 4,
+        name="relay",
+    )(place, *outs)
+    fac = _after(fac, outs[1])
+    outs = [_turn(out, "zh", k) for k, out in enumerate(outs)]
+    near, far = _turn(fac, "y", 1), _turn(fac, "y", 3)
+    opposite = _turn(fac, "y", 2)
+    block, turn = pl.pallas_call(
         _block_kernel,
-        out_shape=(_sds(8, 64, 1024), _sds(64, 1024)),
-        in_specs=[_vmem(), _vmem(), _vmem(), HBM, HBM],
-        out_specs=(HBM, HBM),
-        scratch_shapes=[
-            pltpu.VMEM((64, 1024), BF16),
-            pltpu.VMEM((64, 1024), BF16),
-            pltpu.SemaphoreType.DMA((9,)),
-        ],
+        out_shape=(_sds(64, 1024), _sds(16, 64, 128)),
+        in_specs=[SMEM] + [_vmem()] * 6,
+        out_specs=(_vmem(), _vmem()),
+        scratch_shapes=[pltpu.VMEM((4, 4, 96, 128), BF16)],
         compiler_params=VMEM,
         name="make_block",
-    )(got, small, wide, near, far)
+    )(place, *outs, small, wide)
+    turn = lax.all_to_all(turn, ROWS, 0, 0, tiled=True)
+    block, kept = pl.pallas_call(
+        _symmetric_kernel,
+        out_shape=(_sds(8, 64, 1024), _sds(64, 1024)),
+        in_specs=[_vmem()] * 4 + [ANY] * 3,
+        out_specs=(_vmem(), _vmem()),
+        compiler_params=VMEM,
+        name="symmetrize",
+    )(turn, block, small, wide, near, far, opposite)
     own = lax.all_to_all(block, CHIPS, 0, 0, tiled=True)
-    own = pl.pallas_call(
-        _gate_kernel,
-        out_shape=_sds(8, 64, 1024),
-        in_specs=[HBM] * 2,
-        out_specs=HBM,
-        input_output_aliases={0: 0},
-        compiler_params=VMEM,
-        name="gate",
-    )(own, opposite)
-    other = lax.ppermute(own, "core", [(0, 1), (1, 0)])
+    other = _swap_cores(own)
     square = pltpu.VMEM((1024, 1024), BF16)
     keep, give = pl.pallas_call(
         _ladder_kernel,
@@ -295,37 +347,26 @@
         compiler_params=VMEM,
         name="ladder",
     )(place, fac, near, far, opposite, own, other, rows_b)
-    taken = lax.ppermute(give, "core", [(0, 1), (1, 0)])
+    taken = _swap_cores(give)
     partial = (keep.astype(F32) + taken.astype(F32)).astype(BF16)
     parts = lax.all_to_all(partial, CHIPS, 0, 0, tiled=True)
-    resid, turn = pl.pallas_call(
+    last = pl.pallas_call(
         _sum_kernel,
-        out_shape=(_sds(64, 1024), _sds(16, 32, 128)),
+        out_shape=_sds(16, 32, 128),
         in_specs=[_vmem()] * 3,
-        out_specs=(_vmem(), _vmem()),
+        out_specs=_vmem(),
         compiler_params=VMEM,
         name="sum_parts",
-    )(parts, kept, wide)
-    turned = lax.all_to_all(turn, ROWS, 0, 0, tiled=True)
-    last = pl.pallas_call(
-        _swap_kernel,
-        out_shape=_sds(16, 64, 128),
-        in_specs=[_vmem()] * 4,
-        out_specs=_vmem(),
-        compiler_params=VMEM,
-        name="swap_virtuals",
-    )(turned, resid, small, wide)
+    )(parts, kept, small)
     back = lax.all_to_all(last, COLS, 0, 0, tiled=True)
-    head = _vmem((16, 32, 128), lambda i: (0, 0, 0))
     out = pl.pallas_call(
         _update_kernel,
         out_shape=_sds(16, 4096),
-        grid=(1,),
-        in_specs=[SMEM, SMEM, _vmem(), head, _vmem(), _vmem()],
+        in_specs=[SMEM, SMEM, _vmem(), _vmem(), _vmem(), _vmem()],
         out_specs=_vmem(),
         scratch_shapes=[pltpu.VMEM((512, 128), F32)],
         name="update",
-    )(place, occ_energy, back, sent, mask, vir_energy.reshape(8, 128))
+    )(place, occ_energy, back, held, mask, vir_energy.reshape(8, 128))
     return out.reshape(1, 1, 16, 4096)
 
 

time: 139 us -> 133 us (0.957)
  waiting for transfers between devices: 31.1 us -> 17.1 us
  starting transfers between devices: 24.2 us -> 31.8 us
  blocking collectives: 60.6 us -> 64.1 us
  local copies, waits for them, and re-layouts: 4.43 us -> 2.24 us
    all_to_all x1, waiting for transfers between devices: 14.1 us -> 0.01 us  [_shards(): lax.all_to_all(spread, ('zh',) + ROWS, 0, 0, tiled=True)]
    ppermute x5 -> x11, starting transfers between devices: 6.91 us -> 18.7 us  [the longest x9 16.3 us: _turn(): return lax.ppermute(value, axis, [(i, (i + step) % 4) for i in range(4)])]
    all_to_all x2, blocking collectives: 27.4 us -> 31.7 us  [the longest x1 18.7 us: _shards(): own = lax.all_to_all(block, CHIPS, 0, 0, tiled=True)]
    all_to_all x1 -> x0, starting transfers between devices: 4.33 us -> none  [_shards(): own = lax.all_to_all(block, CHIPS, 0, 0, tiled=True)]
    unnamed x28 -> x18, local copies, waits for them, and re-layouts: 3.69 us -> 0.71 us
    all_to_all x1, blocking collectives: 19.6 us -> 17.9 us  [_shards(): parts = lax.all_to_all(partial, CHIPS, 0, 0, tiled=True)]
    pallas_call x5 -> x6, Pallas kernels: 6.46 us -> 6.87 us  [the longest x1 2.1 us: _shards(): pl.pallas_call(_update_kernel, out_shape=_sds(16, 4096), in_specs=[SMEM,...]
    ppermute x5 -> x11, waiting for transfers between devices: 16.7 us -> 17.1 us  [the longest x9 12.5 us: _turn(): return lax.ppermute(value, axis, [(i, (i + step) % 4) for i in range(4)])]
  transfers between devices with their start and end apart: 7 -> 12, of which waited for: 5 -> 7; matrix products, arithmetic and copies ran while one was open for 0% -> 1% of each run, Pallas kernels for 2% -> 4%
where the time goes in v4:
time: 133 us
  blocking collectives  64.1 us (48%)
  starting transfers between devices  31.8 us (24%)
  waiting for transfers between devices  17.1 us (13%)
  Pallas kernels  17 us (13%)
  local copies, waits for them, and re-layouts  2.24 us (2%)
    all_to_all x1, blocking collectives, _shards(): own = lax.all_to_all(block, CHIPS, 0, 0, tiled=True)  18.7 us
    all_to_all x1, blocking collectives, _shards(): parts = lax.all_to_all(partial, CHIPS, 0, 0, tiled=True)  17.9 us
    ppermute x9, starting transfers between devices, _turn(): return lax.ppermute(value, axis, [(i, (i + step) % 4) for i in range(4)])  16.3 us
    all_to_all x1, blocking collectives, _shards(): back = lax.all_to_all(last, COLS, 0, 0, tiled=True)  14.5 us
    all_to_all x1, starting transfers between devices, _shards(): lax.all_to_all(spread, ('zh',) + ROWS, 0, 0, tiled=True)  13.1 us
    all_to_all x1, blocking collectives, _shards(): turn = lax.all_to_all(turn, ROWS, 0, 0, tiled=True)  13 us
    ppermute x9, waiting for transfers between devices, _turn(): return lax.ppermute(value, axis, [(i, (i + step) % 4) for i in range(4)])  12.5 us
    pallas_call x1, Pallas kernels, _shards(): pl.pallas_call(_ladder_kernel, out_shape=(_sds(8, 64, 1024), _sds(8, 64,...  6.16 us
  transfers between devices with their start and end apart: 12, of which 7 were waited for; matrix products, arithmetic and copies ran while one was open for 1% of the time, Pallas kernels for 4%

profile of v4, /device:TPU:1, one launch (start us, length us, event | category | flops | bytes accessed | tf_op | source)
XLA Modules:
  0.0 132.8 jit_solution(7809468843507729736)
XLA Ops:
  0.0 1.7 %spread_factors.1 = bf16[64,4,1024]{2,1,0:T(4,128)(2,1)} custom-call(bf16[16,4,1024]{2,1,0:T(4,128)(2,1)} %fac_ref.1), custom_call_target="tpu_custom_call" | custom-call | tf_op jit(solution)/shard_map/spread_factors/pallas_call | solution.py:284
  1.7 0.0 copy-start
  1.8 0.0 copy-start.2
  1.8 13.1 %all-to-all-start = ((bf16[64,4,1024]{2,1,0:T(4,128)(2,1)}), bf16[64,4,1024]{2,1,0:T(4,128)(2,1)S(1)}, u32[]{:S(2)}, u32[]{:S(2)}) async-start(bf16[64,4,1024]{2,1,0:T(4,128)(2,1)} %spread_factors.1), calls=%async_computation | async-start | bytes 1048576 | tf_op jit(solution)/shard_map/all_to_all | solution.py:292
  14.9 0.6 stack.27.place_ref
  15.5 0.0 copy-start.5
  15.5 2.3 %mask_amps.1 = (bf16[16,64,128]{2,1,0:T(8,128)(2,1)}, f32[16,128]{1,0:T(8,128)}, bf16[4,96,128]{2,1,0:T(8,128)(2,1)}, bf16[4,96,128]{2,1,0:T(8,128)(2,1)}, bf16[...) custom-call(s32[6]{0:T(128)} %stack.27.place_ref, bf16[16,4096]{1,0:T(8,128)(2,1)} %bitcast.11, ...), custom_call_target="tpu_custom_call" | custom-call | tf_op jit(solution)/shard_map/mask_amps/pallas_call | solution.py:294
  17.8 1.3 collective-permute-start
  19.1 2.6 %collective-permute-start.1 = (bf16[4,96,128]{2,1,0:T(8,128)(2,1)}, bf16[4,96,128]{2,1,0:T(8,128)(2,1)S(1)}, u32[]{:S(2)}, u32[]{:S(2)}) collective-permute-start(bf16[4,96,128]{2,1,0:T(8,128)(2,1)} %get-tuple-element.23), channel_id=1, source_target_pairs={{0,2},{1,3},{2,0},{3,1},{4,6},{5,7},{6,4},{7,5},{8,10},{9,11},{10,... | collective-permute-start | bytes 294920 | tf_op jit(solution)/shard_map/ppermute | solution.py:260
  21.7 1.1 collective-permute-start.2
  22.8 0.5 collective-permute-done.in1
  23.3 0.0 copy-start.6
  23.3 3.2 %collective-permute-done.1.in2 = bf16[4,96,128]{2,1,0:T(8,128)(2,1)S(1)} collective-permute-done((bf16[4,96,128]{2,1,0:T(8,128)(2,1)}, bf16[4,96,128]{2,1,0:T(8,128)(2,1)S(1)}, u32[]{:S(2)}, u32[]{:S(2)}) %collective-permute-start.1) | collective-permute-done | bytes 98336 | tf_op jit(solution)/shard_map/ppermute | solution.py:260
  26.5 0.0 copy-start.7
  26.5 0.0 collective-permute-done.2.in3
  26.5 0.0 copy-start.8
  26.5 0.0 copy-done.6
  26.5 0.6 copy-done.7
  27.1 0.0 copy-done.8
  27.2 1.8 %relay.1 = (bf16[4,96,128]{2,1,0:T(8,128)(2,1)}, bf16[4,96,128]{2,1,0:T(8,128)(2,1)}, bf16[4,96,128]{2,1,0:T(8,128)(2,1)}, bf16[4,96,128]{2,1,0:T(8,128)(2,1)}) custom-call(s32[6]{0:T(128)} %stack.27.place_ref, bf16[4,96,128]{2,1,0:T(8,128)(2,1)} %get-tuple-element.21.in0, bf16[4,96,128]{2,1,0:T(8,128)(2,1)} %copy-done.6, bf16[4,96,128]{2,1,0:T(8,128)(2,1)} %copy-done.7, ...), custom_call_target="tpu_custom_call" | custom-call | tf_op jit(solution)/shard_map/relay/pallas_call | solution.py:303
  29.0 0.0 copy-start.4
  29.0 5.5 %collective-permute-start.7 = (bf16[4,96,128]{2,1,0:T(8,128)(2,1)}, bf16[4,96,128]{2,1,0:T(8,128)(2,1)S(1)}, u32[]{:S(2)}, u32[]{:S(2)}) collective-permute-start(bf16[4,96,128]{2,1,0:T(8,128)(2,1)} %get-tuple-element.27), channel_id=1, source_target_pairs={{0,8},{4,12},{8,0},{12,4},{1,9},{5,13},{9,1},{13,5},{2,10},{6,14},... | collective-permute-start | bytes 294920 | tf_op jit(solution)/shard_map/ppermute | solution.py:260
  34.5 0.2 collective-permute-start.8
  34.7 2.2 %collective-permute-start.6 = (bf16[4,96,128]{2,1,0:T(8,128)(2,1)}, bf16[4,96,128]{2,1,0:T(8,128)(2,1)S(1)}, u32[]{:S(2)}, u32[]{:S(2)}) collective-permute-start(bf16[4,96,128]{2,1,0:T(8,128)(2,1)} %get-tuple-element.25.small_ref), channel_id=1, source_target_pairs={{0,4},{4,8},{8,12},{12,0},{1,5},{5,9},{9,13},{13,1},{2,6},{6,10},{... | collective-permute-start | bytes 294920 | tf_op jit(solution)/shard_map/ppermute | solution.py:260
  36.9 0.0 all-to-all-done
  36.9 0.9 reshape.15.value_ref
  37.8 2.0 %collective-permute-start.5 = (bf16[4,64,1024]{2,1,0:T(8,128)(2,1)}, bf16[4,64,1024]{2,1,0:T(8,128)(2,1)S(1)}, u32[]{:S(2)}, u32[]{:S(2)}) collective-permute-start(bf16[4,64,1024]{2,1,0:T(8,128)(2,1)} %gate.1.mine_ref), channel_id=1, source_target_pairs={{0,2},{1,3},{2,0},{3,1},{4,6},{5,7},{6,4},{7,5},{8,10},{9,11},{10,... | collective-permute-start | bytes 1572872 | tf_op jit(solution)/shard_map/ppermute | solution.py:260
  39.8 0.6 collective-permute-start.4
  40.4 0.0 collective-permute-done.7.in2
  40.4 0.9 collective-permute-start.3
  41.3 3.5 %collective-permute-done.8.in3 = bf16[4,96,128]{2,1,0:T(8,128)(2,1)S(1)} collective-permute-done((bf16[4,96,128]{2,1,0:T(8,128)(2,1)}, bf16[4,96,128]{2,1,0:T(8,128)(2,1)S(1)}, u32[]{:S(2)}, u32[]{:S(2)}) %collective-permute-start.8) | collective-permute-done | bytes 98336 | tf_op jit(solution)/shard_map/ppermute | solution.py:260
  44.7 0.0 collective-permute-done.6.in1
  44.7 0.0 copy-done
  44.7 0.0 copy-done.2
  44.7 0.0 copy-done.5
  44.7 0.0 copy-done.4
  44.7 1.5 %make_block.1 = (bf16[64,1024]{1,0:T(8,128)(2,1)S(1)}, bf16[16,64,128]{2,1,0:T(8,128)(2,1)S(1)}) custom-call(s32[6]{0:T(128)S(1)} %copy-done.5, bf16[4,96,128]{2,1,0:T(8,128)(2,1)S(1)} %copy-done.4, bf16[4,96,128]{2,1,0:T(8,128)(2,1)S(1)} %collective-permute-done.6.in1, bf16[4,96,128]{2,1,0:T(8,128)(2,1)S(1)} %collective-permute-done.7.in2, ...), custom_call_target="tpu_custom_call" | custom-call | tf_op jit(solution)/shard_map/make_block/pallas_call | solution.py:314
  46.3 13.0 %all_to_all.25.got_ref = bf16[16,64,128]{2,1,0:T(8,128)(2,1)S(1)} all-to-all(bf16[16,64,128]{2,1,0:T(8,128)(2,1)S(1)} %get-tuple-element.29), channel_id=1, replica_groups=mesh['x'=4,'zl'=2,'core'=2,'zh'=4,'y'=4] {'x','zl','core'}, dimensions={0} | all-to-all | bytes 524288 | tf_op jit(solution)/shard_map/all_to_all | solution.py:323
  59.3 0.0 collective-permute-done.5.last_ref
  59.3 3.5 %collective-permute-done.4.far_ref = bf16[4,64,1024]{2,1,0:T(8,128)(2,1)S(1)} collective-permute-done((bf16[4,64,1024]{2,1,0:T(8,128)(2,1)}, bf16[4,64,1024]{2,1,0:T(8,128)(2,1)S(1)}, u32[]{:S(2)}, u32[]{:S(2)}) %collective-permute-start.4) | collective-permute-done | bytes 524320 | tf_op jit(solution)/shard_map/ppermute | solution.py:260
  62.8 1.8 %collective-permute-done.3.near_ref = bf16[4,64,1024]{2,1,0:T(8,128)(2,1)S(1)} collective-permute-done((bf16[4,64,1024]{2,1,0:T(8,128)(2,1)}, bf16[4,64,1024]{2,1,0:T(8,128)(2,1)S(1)}, u32[]{:S(2)}, u32[]{:S(2)}) %collective-permute-start.3) | collective-permute-done | bytes 524320 | tf_op jit(solution)/shard_map/ppermute | solution.py:260
  64.6 0.0 copy-start.1
  64.6 0.0 copy-start.3
  64.6 1.0 symmetrize.1
  65.7 18.7 %all_to_all.26.own_ref = bf16[8,64,1024]{2,1,0:T(8,128)(2,1)S(1)} all-to-all(bf16[8,64,1024]{2,1,0:T(8,128)(2,1)S(1)} %get-tuple-element.31), channel_id=1, replica_groups=mesh['x'=4,'zl'=2,'core'=2,'zh'=4,'y'=4] {'x','zl'}, dimensions={0} | all-to-all | bytes 2097152 | tf_op jit(solution)/shard_map/all_to_all | solution.py:332
  84.3 1.9 %collective-permute-start.9 = (bf16[8,64,1024]{2,1,0:T(8,128)(2,1)S(1)}, bf16[8,64,1024]{2,1,0:T(8,128)(2,1)S(1)}, u32[]{:S(2)}, u32[]{:S(2)}) collective-permute-start(bf16[8,64,1024]{2,1,0:T(8,128)(2,1)S(1)} %all_to_all.26.own_ref), channel_id=1, source_target_pairs={{0,16},{16,0},{1,17},{17,1},{2,18},{18,2},{3,19},{19,3},{4,20},{20... | collective-permute-start | bytes 3145736 | tf_op jit(solution)/shard_map/ppermute | solution.py:264
  86.3 2.3 %collective-permute-done.9.other_ref = bf16[8,64,1024]{2,1,0:T(8,128)(2,1)S(1)} collective-permute-done((bf16[8,64,1024]{2,1,0:T(8,128)(2,1)S(1)}, bf16[8,64,1024]{2,1,0:T(8,128)(2,1)S(1)}, u32[]{:S(2)}, u32[]{:S(2)}) %collective-permute-start.9) | collective-permute-done | bytes 1048608 | tf_op jit(solution)/shard_map/ppermute | solution.py:264
  88.6 0.0 copy-done.1
  88.6 0.0 copy-done.3
  88.6 6.2 %ladder.1 = (bf16[8,64,1024]{2,1,0:T(8,128)(2,1)S(1)}, bf16[8,64,1024]{2,1,0:T(8,128)(2,1)S(1)}) custom-call(s32[6]{0:T(128)S(1)} %copy-done.5, bf16[4,64,1024]{2,1,0:T(8,128)(2,1)S(1)} %copy-done.1, bf16[4,64,1024]{2,1,0:T(8,128)(2,1)S(1)} %collective-permute-done.3.near_ref, bf16[4,64,1024]{2,1,0:T(8,128)(2,1)S(1)} %collective-permute-done.4.far_ref, ...), custom_call_target="tpu_custom_call" | custom-call | tf_op jit(solution)/shard_map/ladder/pallas_call | solution.py:335
  94.7 0.5 collective-permute-start.10
  95.2 2.3 %collective-permute-done.10 = bf16[8,64,1024]{2,1,0:T(8,128)(2,1)S(1)} collective-permute-done((bf16[8,64,1024]{2,1,0:T(8,128)(2,1)S(1)}, bf16[8,64,1024]{2,1,0:T(8,128)(2,1)S(1)}, u32[]{:S(2)}, u32[]{:S(2)}) %collective-permute-start.10) | collective-permute-done | bytes 1048608 | tf_op jit(solution)/shard_map/ppermute | solution.py:264
  97.5 0.4 add_convert_fusion
  97.9 17.9 %all_to_all.27.part_ref = bf16[8,64,1024]{2,1,0:T(8,128)(2,1)S(1)} all-to-all(bf16[8,64,1024]{2,1,0:T(8,128)(2,1)S(1)} %add_convert_fusion), channel_id=1, replica_groups=mesh['x'=4,'zl'=2,'core'=2,'zh'=4,'y'=4] {'x','zl'}, dimensions={0} | all-to-all | bytes 2097152 | tf_op jit(solution)/shard_map/all_to_all | solution.py:352
  115.8 0.4 sum_parts.1
  116.2 14.5 %all_to_all.28.resid_ref = bf16[16,32,128]{2,1,0:T(8,128)(2,1)} all-to-all(bf16[16,32,128]{2,1,0:T(8,128)(2,1)S(1)} %sum_parts.1), channel_id=1, replica_groups=mesh['x'=4,'zl'=2,'core'=2,'zh'=4,'y'=4] {'zh','y'}, dimensions={0} | all-to-all | bytes 262144 | tf_op jit(solution)/shard_map/all_to_all | solution.py:361
  130.7 2.1 %update.1 = bf16[16,4096]{1,0:T(8,128)(2,1)} custom-call(s32[6]{0:T(128)} %stack.27.place_ref, f32[4]{0:T(128)} %occ_ref.1, bf16[16,32,128]{2,1,0:T(8,128)(2,1)} %all_to_all.28.resid_ref, bf16[16,64,128]{2,1,0:T(8,128)(2,1)} %get-tuple-element.35.held_ref, f32[16,128]{1,0:T(8,128)} %get-tuple-element.36.mask_ref, f32[8,128]{1,0:T(8,128)} %bitcast.14), custom_call_target="tpu_custom_call" | custom-call | tf_op jit(solution)/shard_map/update/pallas_call | solution.py:362
  (1 shorter events, 0.0 us)
Async XLA Ops:
  1.7 43.0 %copy-start = (bf16[1024,1024]{1,0:T(8,128)(2,1)S(1)}, bf16[1024,1024]{1,0:T(8,128)(2,1)}, u32[]{:S(2)}) copy-start(bf16[1024,1024]{1,0:T(8,128)(2,1)} %constant.32.clone.wide_ref) | copy-start | bytes 6291460
  1.8 43.0 %copy-start.2 = (bf16[3,64,64]{2,1,0:T(8,128)(2,1)S(1)}, bf16[3,64,64]{2,1,0:T(8,128)(2,1)}, u32[]{:S(2)}) copy-start(bf16[3,64,64]{2,1,0:T(8,128)(2,1)} %constant.31.clone.small_ref) | copy-start | bytes 73732
  1.8 35.1 %all-to-all-start = ((bf16[64,4,1024]{2,1,0:T(4,128)(2,1)}), bf16[64,4,1024]{2,1,0:T(4,128)(2,1)S(1)}, u32[]{:S(2)}, u32[]{:S(2)}) async-start(bf16[64,4,1024]{2,1,0:T(4,128)(2,1)} %spread_factors.1), calls=%async_computation | async-start | bytes 1048576 | tf_op jit(solution)/shard_map/all_to_all | solution.py:292
  15.5 29.2 %copy-start.5 = (s32[6]{0:T(128)S(1)}, s32[6]{0:T(128)}, u32[]{:S(2)}) copy-start(s32[6]{0:T(128)} %stack.27.place_ref) | copy-start | bytes 76
  17.8 5.5 %collective-permute-start = (bf16[4,96,128]{2,1,0:T(8,128)(2,1)}, bf16[4,96,128]{2,1,0:T(8,128)(2,1)S(1)}, u32[]{:S(2)}, u32[]{:S(2)}) collective-permute-start(bf16[4,96,128]{2,1,0:T(8,128)(2,1)} %get-tuple-element.22), channel_id=1, source_target_pairs={{0,1},{1,2},{2,3},{3,0},{4,5},{5,6},{6,7},{7,4},{8,9},{9,10},{10,1... | collective-permute-start | bytes 294920 | tf_op jit(solution)/shard_map/ppermute | solution.py:260
  19.1 7.4 %collective-permute-start.1 = (bf16[4,96,128]{2,1,0:T(8,128)(2,1)}, bf16[4,96,128]{2,1,0:T(8,128)(2,1)S(1)}, u32[]{:S(2)}, u32[]{:S(2)}) collective-permute-start(bf16[4,96,128]{2,1,0:T(8,128)(2,1)} %get-tuple-element.23), channel_id=1, source_target_pairs={{0,2},{1,3},{2,0},{3,1},{4,6},{5,7},{6,4},{7,5},{8,10},{9,11},{10,... | collective-permute-start | bytes 294920 | tf_op jit(solution)/shard_map/ppermute | solution.py:260
  21.7 4.8 %collective-permute-start.2 = (bf16[4,96,128]{2,1,0:T(8,128)(2,1)}, bf16[4,96,128]{2,1,0:T(8,128)(2,1)S(1)}, u32[]{:S(2)}, u32[]{:S(2)}) collective-permute-start(bf16[4,96,128]{2,1,0:T(8,128)(2,1)} %get-tuple-element.24), channel_id=1, source_target_pairs={{0,3},{1,0},{2,1},{3,2},{4,7},{5,4},{6,5},{7,6},{8,11},{9,8},{10,9... | collective-permute-start | bytes 294920 | tf_op jit(solution)/shard_map/ppermute | solution.py:260
  23.3 3.2 %copy-start.6 = (bf16[4,96,128]{2,1,0:T(8,128)(2,1)}, bf16[4,96,128]{2,1,0:T(8,128)(2,1)S(1)}, u32[]{:S(2)}) copy-start(bf16[4,96,128]{2,1,0:T(8,128)(2,1)S(1)} %collective-permute-done.in1) | copy-start | bytes 294916
  26.5 0.6 copy-start.7
  26.5 0.7 copy-start.8
  29.0 15.7 %copy-start.4 = (bf16[4,96,128]{2,1,0:T(8,128)(2,1)S(1)}, bf16[4,96,128]{2,1,0:T(8,128)(2,1)}, u32[]{:S(2)}) copy-start(bf16[4,96,128]{2,1,0:T(8,128)(2,1)} %get-tuple-element.26.in0) | copy-start | bytes 294916
  29.0 11.3 %collective-permute-start.7 = (bf16[4,96,128]{2,1,0:T(8,128)(2,1)}, bf16[4,96,128]{2,1,0:T(8,128)(2,1)S(1)}, u32[]{:S(2)}, u32[]{:S(2)}) collective-permute-start(bf16[4,96,128]{2,1,0:T(8,128)(2,1)} %get-tuple-element.27), channel_id=1, source_target_pairs={{0,8},{4,12},{8,0},{12,4},{1,9},{5,13},{9,1},{13,5},{2,10},{6,14},... | collective-permute-start | bytes 294920 | tf_op jit(solution)/shard_map/ppermute | solution.py:260
  34.5 10.2 %collective-permute-start.8 = (bf16[4,96,128]{2,1,0:T(8,128)(2,1)}, bf16[4,96,128]{2,1,0:T(8,128)(2,1)S(1)}, u32[]{:S(2)}, u32[]{:S(2)}) collective-permute-start(bf16[4,96,128]{2,1,0:T(8,128)(2,1)} %get-tuple-element.28), channel_id=1, source_target_pairs={{0,12},{4,0},{8,4},{12,8},{1,13},{5,1},{9,5},{13,9},{2,14},{6,2},{... | collective-permute-start | bytes 294920 | tf_op jit(solution)/shard_map/ppermute | solution.py:260
  34.7 10.0 %collective-permute-start.6 = (bf16[4,96,128]{2,1,0:T(8,128)(2,1)}, bf16[4,96,128]{2,1,0:T(8,128)(2,1)S(1)}, u32[]{:S(2)}, u32[]{:S(2)}) collective-permute-start(bf16[4,96,128]{2,1,0:T(8,128)(2,1)} %get-tuple-element.25.small_ref), channel_id=1, source_target_pairs={{0,4},{4,8},{8,12},{12,0},{1,5},{5,9},{9,13},{13,1},{2,6},{6,10},{... | collective-permute-start | bytes 294920 | tf_op jit(solution)/shard_map/ppermute | solution.py:260
  37.8 21.5 %collective-permute-start.5 = (bf16[4,64,1024]{2,1,0:T(8,128)(2,1)}, bf16[4,64,1024]{2,1,0:T(8,128)(2,1)S(1)}, u32[]{:S(2)}, u32[]{:S(2)}) collective-permute-start(bf16[4,64,1024]{2,1,0:T(8,128)(2,1)} %gate.1.mine_ref), channel_id=1, source_target_pairs={{0,2},{1,3},{2,0},{3,1},{4,6},{5,7},{6,4},{7,5},{8,10},{9,11},{10,... | collective-permute-start | bytes 1572872 | tf_op jit(solution)/shard_map/ppermute | solution.py:260
  39.8 23.0 %collective-permute-start.4 = (bf16[4,64,1024]{2,1,0:T(8,128)(2,1)}, bf16[4,64,1024]{2,1,0:T(8,128)(2,1)S(1)}, u32[]{:S(2)}, u32[]{:S(2)}) collective-permute-start(bf16[4,64,1024]{2,1,0:T(8,128)(2,1)} %gate.1.mine_ref), channel_id=1, source_target_pairs={{0,3},{1,0},{2,1},{3,2},{4,7},{5,4},{6,5},{7,6},{8,11},{9,8},{10,9... | collective-permute-start | bytes 1572872 | tf_op jit(solution)/shard_map/ppermute | solution.py:260
  40.4 24.3 %collective-permute-start.3 = (bf16[4,64,1024]{2,1,0:T(8,128)(2,1)}, bf16[4,64,1024]{2,1,0:T(8,128)(2,1)S(1)}, u32[]{:S(2)}, u32[]{:S(2)}) collective-permute-start(bf16[4,64,1024]{2,1,0:T(8,128)(2,1)} %gate.1.mine_ref), channel_id=1, source_target_pairs={{0,1},{1,2},{2,3},{3,0},{4,5},{5,6},{6,7},{7,4},{8,9},{9,10},{10,1... | collective-permute-start | bytes 1572872 | tf_op jit(solution)/shard_map/ppermute | solution.py:260
  64.6 23.9 %copy-start.1 = (bf16[4,64,1024]{2,1,0:T(8,128)(2,1)S(1)}, bf16[4,64,1024]{2,1,0:T(8,128)(2,1)}, u32[]{:S(2)}) copy-start(bf16[4,64,1024]{2,1,0:T(8,128)(2,1)} %gate.1.mine_ref) | copy-start | bytes 1572868
  64.6 23.9 %copy-start.3 = (bf16[256,256]{1,0:T(8,128)(2,1)S(1)}, bf16[256,256]{1,0:T(8,128)(2,1)}, u32[]{:S(2)}) copy-start(bf16[256,256]{1,0:T(8,128)(2,1)} %constant.33.clone.rows_ref) | copy-start | bytes 393220
  84.3 4.2 %collective-permute-start.9 = (bf16[8,64,1024]{2,1,0:T(8,128)(2,1)S(1)}, bf16[8,64,1024]{2,1,0:T(8,128)(2,1)S(1)}, u32[]{:S(2)}, u32[]{:S(2)}) collective-permute-start(bf16[8,64,1024]{2,1,0:T(8,128)(2,1)S(1)} %all_to_all.26.own_ref), channel_id=1, source_target_pairs={{0,16},{16,0},{1,17},{17,1},{2,18},{18,2},{3,19},{19,3},{4,20},{20... | collective-permute-start | bytes 3145736 | tf_op jit(solution)/shard_map/ppermute | solution.py:264
  94.7 2.8 %collective-permute-start.10 = (bf16[8,64,1024]{2,1,0:T(8,128)(2,1)S(1)}, bf16[8,64,1024]{2,1,0:T(8,128)(2,1)S(1)}, u32[]{:S(2)}, u32[]{:S(2)}) collective-permute-start(bf16[8,64,1024]{2,1,0:T(8,128)(2,1)S(1)} %get-tuple-element.33), channel_id=1, source_target_pairs={{0,16},{16,0},{1,17},{17,1},{2,18},{18,2},{3,19},{19,3},{4,20},{20... | collective-permute-start | bytes 3145736 | tf_op jit(solution)/shard_map/ppermute | solution.py:264

commit v5 on v4

--- a/solution.py
+++ b/solution.py
@@ -40,7 +40,13 @@
     wide = _one_hot(col * 64 + row * 4 + k).T
     row, col, k = _grid(4, 16, 4)
     rows_b = _one_hot(col * 16 + row * 4 + k)
-    return [np.asarray(t, jnp.bfloat16) for t in (small, wide, rows_b)]
+    h, row, k = _grid(2, 16, 4)
+    halves = _one_hot((row * 2 + h) * 4 + k)
+    return [np.asarray(t, jnp.bfloat16) for t in (small, wide, rows_b, halves)]
+
+
+def _chip():
+    return lax.axis_index("x") * 2 + lax.axis_index("zl")
 
 
 def _perm(left, right):
@@ -55,8 +61,11 @@
     return jnp.concatenate([piece[:32], piece[32:]], axis=1)
 
 
-def _spread_kernel(fac_ref, out_ref, sems):
-    copies = [pltpu.make_async_copy(fac_ref, out_ref.at[k * 16 : k * 16 + 16], sems.at[k]) for k in range(4)]
+def _spread_kernel(fac_ref, out_ref, wide_ref, send_ref, sems):
+    wide_ref[:, :4, :] = fac_ref[:, :, :512].astype(F32)
+    wide_ref[:, 4:, :] = fac_ref[:, :, 512:].astype(F32)
+    send_ref[...] = wide_ref[...].astype(BF16)
+    copies = [pltpu.make_async_copy(send_ref, out_ref.at[k * 16 : k * 16 + 16], sems.at[k]) for k in range(4)]
     for copy in copies:
         copy.start()
     for copy in copies:
@@ -64,7 +73,6 @@
 
 
 def _mask_kernel(
-    place_ref,
     amps_ref,
     source_ref,
     screen_ref,
@@ -77,12 +85,12 @@
     flat_ref,
     flat2_ref,
 ):
-    block = screen_ref[place_ref[0]].astype(F32)
+    block = screen_ref[_chip()].astype(F32)
     lane_block = (lax.broadcasted_iota(jnp.int32, (8, 128), 1) % 64) // 8
     spread = (lax.broadcasted_iota(jnp.int32, (8, 128), 0) == lane_block).astype(F32)
     mask = lax.dot_general(block, spread, TN, preferred_element_type=F32)
     mask_ref[...] = mask
-    y = place_ref[3]
+    y = lax.axis_index("y")
     for j in range(32):
         tile = slice(j * 128, (j + 1) * 128)
         flat_ref[pl.ds(j, 16, stride=32), :] = amps_ref[:, tile].astype(F32) * mask
@@ -100,15 +108,15 @@
             out[zh, 64:, :] = flat2_ref[turned, :].astype(BF16)
 
 
-def _relay_kernel(place_ref, in0, in1, in2, in3, out0, out1, out2, out3):
-    zh, y = place_ref[2], place_ref[3]
+def _relay_kernel(in0, in1, in2, in3, out0, out1, out2, out3):
+    zh, y = lax.axis_index("zh"), lax.axis_index("y")
     for m, out in enumerate((out0, out1, out2, out3)):
         for k, ref in enumerate((in0, in1, in2, in3)):
             out[(y + 4 - k) % 4] = ref[(zh + m) % 4]
 
 
-def _block_kernel(place_ref, in0, in1, in2, in3, small_ref, wide_ref, amp_ref, sent_ref, got_ref):
-    zh = place_ref[2]
+def _block_kernel(in0, in1, in2, in3, small_ref, wide_ref, amp_ref, sent_ref, got_ref):
+    zh = lax.axis_index("zh")
     for m, ref in enumerate((in0, in1, in2, in3)):
         got_ref[(zh + 4 - m) % 4] = ref[...]
 
@@ -145,60 +153,49 @@
     del value_ref, small_ref, out_ref
 
 
-def _ladder_kernel(
-    place_ref,
-    mine_ref,
-    near_ref,
-    far_ref,
-    last_ref,
-    own_ref,
-    other_ref,
-    rows_ref,
-    keep_ref,
-    give_ref,
-    amp_ref,
-    inner_ref,
-    left_ref,
-    right_ref,
-    sems,
-):
-    core, y = place_ref[1], place_ref[3]
-    behind, ahead, across = (y + 3) % 4, (y + 1) % 4, (y + 2) % 4
-    copies = (
-        pltpu.make_async_copy(mine_ref, right_ref.at[:, y], sems.at[0]),
-        pltpu.make_async_copy(near_ref, right_ref.at[:, behind], sems.at[1]),
-        pltpu.make_async_copy(far_ref, right_ref.at[:, ahead], sems.at[2]),
-        pltpu.make_async_copy(last_ref, right_ref.at[:, across], sems.at[3]),
-        pltpu.make_async_copy(own_ref, amp_ref.at[:, core], sems.at[4]),
-        pltpu.make_async_copy(other_ref, amp_ref.at[:, 1 - core], sems.at[5]),
-    )
-    for copy in copies:
-        copy.start()
-    for copy in copies[:4]:
-        copy.wait()
+def _factor_kernel(fac0, fac1, fac2, fac3, halves_ref, rows_ref, right_ref, left_ref):
+    y = lax.axis_index("y")
+    for k, ref in enumerate((fac0, fac1, fac2, fac3)):
+        for zh in range(4):
+            part = _perm(halves_ref[...], ref[zh])
+            right_ref[zh, (y + 4 - k) % 4] = jnp.concatenate([part[:64], part[64:]], axis=1)
     for x in range(4):
         rows = [right_ref[col // 4, col % 4, x * 16 : x * 16 + 16, :] for col in range(16)]
-        left_ref[x * 256 : x * 256 + 256, :] = _perm(rows_ref[...], jnp.concatenate(rows, axis=0))
-    for copy in copies[4:]:
-        copy.wait()
+        part = _perm(rows_ref[...], jnp.concatenate(rows, axis=0))
+        for zl in range(2):
+            for core in range(2):
+                at = zl * 128 + core * 64
+                left_ref[x * 2 + zl, core] = part[at : at + 64]
+
+
+def _second_step(left_ref, core, inner_ref, out_ref):
+    for x in range(2):
+        rows = jnp.concatenate([left_ref[x * 4 + chip, core] for chip in range(4)], axis=0)
+        for j in range(4):
+            cols = slice(j * 256, j * 256 + 256)
+            part = _perm(rows, inner_ref[:, cols])
+            for chip in range(4):
+                out_ref[x * 4 + chip, :, cols] = part[chip * 64 : chip * 64 + 64]
+
+
+def _ladder_kernel(own_ref, other_ref, right_ref, left_ref, inner_ref, give_ref):
+    core = lax.axis_index("core")
+    first = core == 0
     for i in range(4):
+        rows = []
+        for chip in (2 * i, 2 * i + 1):
+            own, other = own_ref[chip], other_ref[chip]
+            rows += [jnp.where(first, own, other), jnp.where(first, other, own)]
+        rows = jnp.concatenate(rows, axis=0)
         for j in range(4):
             inner_ref[i * 256 : i * 256 + 256, j * 256 : j * 256 + 256] = lax.dot_general(
-                amp_ref[i * 2 : i * 2 + 2].reshape(256, 1024),
-                right_ref[j].reshape(256, 1024),
-                NT,
-                preferred_element_type=F32,
+                rows, right_ref[j].reshape(256, 1024), NT, preferred_element_type=F32
             ).astype(BF16)
-    first = core == 0
-    for x in range(4):
-        for j in range(4):
-            cols = slice(j * 256, j * 256 + 256)
-            part = _perm(left_ref[x * 256 : x * 256 + 256, :], inner_ref[:, cols])
-            for zl in range(2):
-                zero = part[zl * 128 : zl * 128 + 64]
-                one = part[zl * 128 + 64 : zl * 128 + 128]
-                keep_ref[x * 2 + zl, :, cols] = jnp.where(first, zero, one)
-                give_ref[x * 2 + zl, :, cols] = jnp.where(first, one, zero)
+    _second_step(left_ref, 1 - core, inner_ref, give_ref)
+
+
+def _rest_kernel(left_ref, inner_ref, keep_ref):
+    _second_step(left_ref, lax.axis_index("core"), inner_ref, keep_ref)
 
 
 def _sum_kernel(part_ref, kept_ref, small_ref, sent_ref):
@@ -210,9 +207,9 @@
         sent_ref[col] = _pack(total[:, col * 64 : col * 64 + 64])
 
 
-def _update_kernel(place_ref, occ_ref, resid_ref, held_ref, mask_ref, vir_ref, out_ref, flat_ref):
-    row = place_ref[5]
-    col = place_ref[4]
+def _update_kernel(occ_ref, resid_ref, held_ref, mask_ref, vir_ref, out_ref, flat_ref):
+    row = _chip() * 2 + lax.axis_index("core")
+    col = lax.axis_index("zh") * 4 + lax.axis_index("y")
     exact = lax.Precision.HIGHEST
 
     def iota(shape, dim):
@@ -268,58 +265,54 @@
     return pl.pallas_call(
         _gate_kernel,
         out_shape=jax.ShapeDtypeStruct(value.shape, value.dtype),
-        in_specs=[ANY, ANY],
-        out_specs=ANY,
+        in_specs=[_vmem(), ANY],
+        out_specs=_vmem(),
         input_output_aliases={0: 0},
         name="gate",
     )(value, small)
 
 
 def _shards(tables, amps, source, factors, screen, occ_energy, vir_energy):
-    small, wide, rows_b = tables
-    x, zl, core = lax.axis_index("x"), lax.axis_index("zl"), lax.axis_index("core")
-    zh, y = lax.axis_index("zh"), lax.axis_index("y")
-    place = jnp.stack([x * 2 + zl, core, zh, y, zh * 4 + y, x * 4 + zl * 2 + core]).astype(jnp.int32)
-
+    small, wide, rows_b, halves = tables
     spread = pl.pallas_call(
         _spread_kernel,
-        out_shape=_sds(64, 4, 1024),
+        out_shape=_sds(64, 8, 512),
         in_specs=[_vmem()],
         out_specs=HBM,
-        scratch_shapes=[pltpu.SemaphoreType.DMA((4,))],
+        scratch_shapes=[pltpu.VMEM((16, 8, 512), F32), pltpu.VMEM((16, 8, 512), BF16)]
+        + [pltpu.SemaphoreType.DMA((4,))],
         name="spread_factors",
     )(factors)
-    fac = lax.all_to_all(spread, ("zh",) + ROWS, 0, 0, tiled=True).reshape(4, 64, 1024)
+    fac = lax.all_to_all(spread, ("zh",) + ROWS, 0, 0, tiled=True).reshape(4, 128, 512)
     four = _sds(4, 96, 128)
     held, mask, *outs = pl.pallas_call(
         _mask_kernel,
         out_shape=(_sds(16, 64, 128), _sds(16, 128, dtype=F32)) + (four,) * 4,
-        in_specs=[SMEM, _vmem(), _vmem(), _vmem()],
+        in_specs=[_vmem()] * 3,
         out_specs=(_vmem(),) * 6,
         scratch_shapes=[pltpu.VMEM((512, 128), F32)] * 2,
         name="mask_amps",
-    )(place, amps.reshape(16, 4096), source.reshape(16, 4096), screen.transpose(1, 2, 0))
+    )(amps.reshape(16, 4096), source.reshape(16, 4096), screen.transpose(1, 2, 0))
     outs = [_turn(out, "y", k) for k, out in enumerate(outs)]
     outs = pl.pallas_call(
         _relay_kernel,
         out_shape=(four,) * 4,
-        in_specs=[SMEM] + [_vmem()] * 4,
+        in_specs=[_vmem()] * 4,
         out_specs=(_vmem(),) * 4,
         name="relay",
-    )(place, *outs)
-    fac = _after(fac, outs[1])
+    )(*outs)
     outs = [_turn(out, "zh", k) for k, out in enumerate(outs)]
     near, far = _turn(fac, "y", 1), _turn(fac, "y", 3)
     opposite = _turn(fac, "y", 2)
     block, turn = pl.pallas_call(
         _block_kernel,
         out_shape=(_sds(64, 1024), _sds(16, 64, 128)),
-        in_specs=[SMEM] + [_vmem()] * 6,
+        in_specs=[_vmem()] * 6,
         out_specs=(_vmem(), _vmem()),
         scratch_shapes=[pltpu.VMEM((4, 4, 96, 128), BF16)],
         compiler_params=VMEM,
         name="make_block",
-    )(place, *outs, small, wide)
+    )(*outs, small, wide)
     turn = lax.all_to_all(turn, ROWS, 0, 0, tiled=True)
     block, kept = pl.pallas_call(
         _symmetric_kernel,
@@ -331,22 +324,30 @@
     )(turn, block, small, wide, near, far, opposite)
     own = lax.all_to_all(block, CHIPS, 0, 0, tiled=True)
     other = _swap_cores(own)
-    square = pltpu.VMEM((1024, 1024), BF16)
-    keep, give = pl.pallas_call(
+    right, left = pl.pallas_call(
+        _factor_kernel,
+        out_shape=(_sds(4, 4, 64, 1024), _sds(8, 2, 64, 1024)),
+        in_specs=[_vmem()] * 6,
+        out_specs=(_vmem(), _vmem()),
+        compiler_params=VMEM,
+        name="prepare_factors",
+    )(fac, near, opposite, far, halves, rows_b)
+    inner, give = pl.pallas_call(
         _ladder_kernel,
-        out_shape=(_sds(8, 64, 1024), _sds(8, 64, 1024)),
-        in_specs=[SMEM] + [HBM] * 6 + [_vmem()],
+        out_shape=(_sds(1024, 1024), _sds(8, 64, 1024)),
+        in_specs=[_vmem()] * 4,
         out_specs=(_vmem(), _vmem()),
-        scratch_shapes=[
-            pltpu.VMEM((8, 2, 64, 1024), BF16),
-            square,
-            square,
-            pltpu.VMEM((4, 4, 64, 1024), BF16),
-            pltpu.SemaphoreType.DMA((6,)),
-        ],
         compiler_params=VMEM,
         name="ladder",
-    )(place, fac, near, far, opposite, own, other, rows_b)
+    )(own, other, right, left)
+    keep = pl.pallas_call(
+        _rest_kernel,
+        out_shape=_sds(8, 64, 1024),
+        in_specs=[_vmem()] * 2,
+        out_specs=_vmem(),
+        compiler_params=VMEM,
+        name="ladder_rest",
+    )(left, inner)
     taken = _swap_cores(give)
     partial = (keep.astype(F32) + taken.astype(F32)).astype(BF16)
     parts = lax.all_to_all(partial, CHIPS, 0, 0, tiled=True)
@@ -362,11 +363,11 @@
     out = pl.pallas_call(
         _update_kernel,
         out_shape=_sds(16, 4096),
-        in_specs=[SMEM, SMEM, _vmem(), _vmem(), _vmem(), _vmem()],
+        in_specs=[SMEM, _vmem(), _vmem(), _vmem(), _vmem()],
         out_specs=_vmem(),
         scratch_shapes=[pltpu.VMEM((512, 128), F32)],
         name="update",
-    )(place, occ_energy, back, held, mask, vir_energy.reshape(8, 128))
+    )(occ_energy, back, held, mask, vir_energy.reshape(8, 128))
     return out.reshape(1, 1, 16, 4096)
 
 

time: 133 us -> 129 us (0.970)
  blocking collectives: 64.1 us -> 61.2 us
    ppermute x2, waiting for transfers between devices: 4.57 us -> 1.9 us  [_swap_cores(): return lax.ppermute(value, 'core', [(0, 1), (1, 0)])]
    ppermute x9, waiting for transfers between devices: 12.5 us -> 14.9 us  [_turn(): return lax.ppermute(value, axis, [(i, (i + step) % 4) for i in range(4)])]
    all_to_all x1, blocking collectives: 14.5 us -> 12.5 us  [_shards(): back = lax.all_to_all(last, COLS, 0, 0, tiled=True)]
    pallas_call x4 -> x5, Pallas kernels: 9.73 us -> 9.89 us  [the longest x1 3.46 us: _shards(): pl.pallas_call(_ladder_kernel, out_shape=(_sds(1024, 1024), _sds(8, 64, 1...]
  transfers between devices with their start and end apart: 12 -> 12, of which waited for: 7 -> 7; matrix products, arithmetic and copies ran while one was open for 1% -> 0% of each run, Pallas kernels for 4% -> 6%
where the time goes in v5:
time: 129 us
  blocking collectives  61.2 us (47%)
  starting transfers between devices  32.3 us (25%)
  waiting for transfers between devices  16.8 us (13%)
  Pallas kernels  16.7 us (13%)
  local copies, waits for them, and re-layouts  1.58 us (1%)
    all_to_all x1, blocking collectives, _shards(): own = lax.all_to_all(block, CHIPS, 0, 0, tiled=True)  18.7 us
    all_to_all x1, blocking collectives, _shards(): parts = lax.all_to_all(partial, CHIPS, 0, 0, tiled=True)  17.9 us
    ppermute x9, starting transfers between devices, _turn(): return lax.ppermute(value, axis, [(i, (i + step) % 4) for i in range(4)])  16.9 us
    ppermute x9, waiting for transfers between devices, _turn(): return lax.ppermute(value, axis, [(i, (i + step) % 4) for i in range(4)])  14.9 us
    all_to_all x1, starting transfers between devices, _shards(): lax.all_to_all(spread, ('zh',) + ROWS, 0, 0, tiled=True)  13 us
    all_to_all x1, blocking collectives, _shards(): back = lax.all_to_all(last, COLS, 0, 0, tiled=True)  12.5 us
    all_to_all x1, blocking collectives, _shards(): turn = lax.all_to_all(turn, ROWS, 0, 0, tiled=True)  12.2 us
    pallas_call x1, Pallas kernels, _shards(): pl.pallas_call(_ladder_kernel, out_shape=(_sds(1024, 1024), _sds(8, 64, 1...  3.46 us
  transfers between devices with their start and end apart: 12, of which 7 were waited for; matrix products, arithmetic and copies ran while one was open for 0% of the time, Pallas kernels for 6%

profile of v5, /device:TPU:1, one launch (start us, length us, event | category | flops | bytes accessed | tf_op | source)
XLA Modules:
  0.0 129.1 jit_solution(2217810927998298140)
XLA Ops:
  0.0 0.0 copy-start.1
  0.0 0.0 copy-start
  0.0 1.9 %spread_factors.1 = bf16[64,8,512]{2,1,0:T(8,128)(2,1)} custom-call(bf16[16,4,1024]{2,1,0:T(4,128)(2,1)} %fac_ref.1), custom_call_target="tpu_custom_call" | custom-call | tf_op jit(solution)/shard_map/spread_factors/pallas_call | solution.py:277
  1.9 13.0 %all-to-all-start = ((bf16[64,8,512]{2,1,0:T(8,128)(2,1)}), bf16[64,8,512]{2,1,0:T(8,128)(2,1)S(1)}, u32[]{:S(2)}, u32[]{:S(2)}) async-start(bf16[64,8,512]{2,1,0:T(8,128)(2,1)} %spread_factors.1), calls=%async_computation | async-start | bytes 1048576 | tf_op jit(solution)/shard_map/all_to_all | solution.py:286
  15.0 2.3 %mask_amps.1 = (bf16[16,64,128]{2,1,0:T(8,128)(2,1)}, f32[16,128]{1,0:T(8,128)}, bf16[4,96,128]{2,1,0:T(8,128)(2,1)}, bf16[4,96,128]{2,1,0:T(8,128)(2,1)}, bf16[...) custom-call(bf16[16,4096]{1,0:T(8,128)(2,1)} %bitcast.10, bf16[16,4096]{1,0:T(8,128)(2,1)} %bitcast.11, ...), custom_call_target="tpu_custom_call" | custom-call | tf_op jit(solution)/shard_map/mask_amps/pallas_call | solution.py:288
  17.2 1.3 %collective-permute-start.3 = (bf16[4,96,128]{2,1,0:T(8,128)(2,1)}, bf16[4,96,128]{2,1,0:T(8,128)(2,1)S(1)}, u32[]{:S(2)}, u32[]{:S(2)}) collective-permute-start(bf16[4,96,128]{2,1,0:T(8,128)(2,1)} %get-tuple-element.25), channel_id=1, source_target_pairs={{0,1},{1,2},{2,3},{3,0},{4,5},{5,6},{6,7},{7,4},{8,9},{9,10},{10,1... | collective-permute-start | bytes 294920 | tf_op jit(solution)/shard_map/ppermute | solution.py:257
  18.5 2.6 %collective-permute-start.4 = (bf16[4,96,128]{2,1,0:T(8,128)(2,1)}, bf16[4,96,128]{2,1,0:T(8,128)(2,1)S(1)}, u32[]{:S(2)}, u32[]{:S(2)}) collective-permute-start(bf16[4,96,128]{2,1,0:T(8,128)(2,1)} %get-tuple-element.26), channel_id=1, source_target_pairs={{0,2},{1,3},{2,0},{3,1},{4,6},{5,7},{6,4},{7,5},{8,10},{9,11},{10,... | collective-permute-start | bytes 294920 | tf_op jit(solution)/shard_map/ppermute | solution.py:257
  21.1 1.1 collective-permute-start.5
  22.2 0.5 collective-permute-done.3.in1
  22.7 0.0 copy-start.5
  22.7 3.2 %collective-permute-done.4.in2 = bf16[4,96,128]{2,1,0:T(8,128)(2,1)S(1)} collective-permute-done((bf16[4,96,128]{2,1,0:T(8,128)(2,1)}, bf16[4,96,128]{2,1,0:T(8,128)(2,1)S(1)}, u32[]{:S(2)}, u32[]{:S(2)}) %collective-permute-start.4) | collective-permute-done | bytes 98336 | tf_op jit(solution)/shard_map/ppermute | solution.py:257
  25.9 0.0 copy-start.6
  25.9 0.0 collective-permute-done.5.in3
  25.9 0.0 copy-start.7
  25.9 0.0 copy-done.5
  25.9 0.6 copy-done.6
  26.6 0.0 copy-done.7
  26.6 1.8 %relay.1 = (bf16[4,96,128]{2,1,0:T(8,128)(2,1)}, bf16[4,96,128]{2,1,0:T(8,128)(2,1)}, bf16[4,96,128]{2,1,0:T(8,128)(2,1)}, bf16[4,96,128]{2,1,0:T(8,128)(2,1)}) custom-call(bf16[4,96,128]{2,1,0:T(8,128)(2,1)} %get-tuple-element.24.in0, bf16[4,96,128]{2,1,0:T(8,128)(2,1)} %copy-done.5, bf16[4,96,128]{2,1,0:T(8,128)(2,1)} %copy-done.6, ...), custom_call_target="tpu_custom_call" | custom-call | tf_op jit(solution)/shard_map/relay/pallas_call | solution.py:297
  28.4 2.4 %collective-permute-start.6 = (bf16[4,96,128]{2,1,0:T(8,128)(2,1)}, bf16[4,96,128]{2,1,0:T(8,128)(2,1)S(1)}, u32[]{:S(2)}, u32[]{:S(2)}) collective-permute-start(bf16[4,96,128]{2,1,0:T(8,128)(2,1)} %get-tuple-element.29), channel_id=1, source_target_pairs={{0,4},{4,8},{8,12},{12,0},{1,5},{5,9},{9,13},{13,1},{2,6},{6,10},{... | collective-permute-start | bytes 294920 | tf_op jit(solution)/shard_map/ppermute | solution.py:257
  30.8 3.5 %collective-permute-start.7 = (bf16[4,96,128]{2,1,0:T(8,128)(2,1)}, bf16[4,96,128]{2,1,0:T(8,128)(2,1)S(1)}, u32[]{:S(2)}, u32[]{:S(2)}) collective-permute-start(bf16[4,96,128]{2,1,0:T(8,128)(2,1)} %get-tuple-element.30), channel_id=1, source_target_pairs={{0,8},{4,12},{8,0},{12,4},{1,9},{5,13},{9,1},{13,5},{2,10},{6,14},... | collective-permute-start | bytes 294920 | tf_op jit(solution)/shard_map/ppermute | solution.py:257
  34.3 3.2 %collective-permute-start.8 = (bf16[4,96,128]{2,1,0:T(8,128)(2,1)}, bf16[4,96,128]{2,1,0:T(8,128)(2,1)S(1)}, u32[]{:S(2)}, u32[]{:S(2)}) collective-permute-start(bf16[4,96,128]{2,1,0:T(8,128)(2,1)} %get-tuple-element.31), channel_id=1, source_target_pairs={{0,12},{4,0},{8,4},{12,8},{1,13},{5,1},{9,5},{13,9},{2,14},{6,2},{... | collective-permute-start | bytes 294920 | tf_op jit(solution)/shard_map/ppermute | solution.py:257
  37.5 0.0 all-to-all-done
  37.5 1.5 %collective-permute-start.2 = (bf16[4,128,512]{2,1,0:T(8,128)(2,1)S(1)}, bf16[4,128,512]{2,1,0:T(8,128)(2,1)S(1)}, u32[]{:S(2)}, u32[]{:S(2)}) collective-permute-start(bf16[4,128,512]{2,1,0:T(8,128)(2,1)S(1)} %bitcast.6), channel_id=1, source_target_pairs={{0,3},{1,0},{2,1},{3,2},{4,7},{5,4},{6,5},{7,6},{8,11},{9,8},{10,9... | collective-permute-start | bytes 1572872 | tf_op jit(solution)/shard_map/ppermute | solution.py:257
  39.0 0.5 collective-permute-start.1
  39.5 0.0 collective-permute-done.6.in1
  39.5 0.9 collective-permute-start
  40.3 1.5 %collective-permute-done.7.in2 = bf16[4,96,128]{2,1,0:T(8,128)(2,1)S(1)} collective-permute-done((bf16[4,96,128]{2,1,0:T(8,128)(2,1)}, bf16[4,96,128]{2,1,0:T(8,128)(2,1)S(1)}, u32[]{:S(2)}, u32[]{:S(2)}) %collective-permute-start.7) | collective-permute-done | bytes 98336 | tf_op jit(solution)/shard_map/ppermute | solution.py:257
  41.9 3.1 %collective-permute-done.8.in3 = bf16[4,96,128]{2,1,0:T(8,128)(2,1)S(1)} collective-permute-done((bf16[4,96,128]{2,1,0:T(8,128)(2,1)}, bf16[4,96,128]{2,1,0:T(8,128)(2,1)S(1)}, u32[]{:S(2)}, u32[]{:S(2)}) %collective-permute-start.8) | collective-permute-done | bytes 98336 | tf_op jit(solution)/shard_map/ppermute | solution.py:257
  45.0 0.0 copy-done.1
  45.0 0.0 copy-done
  45.0 0.0 copy-start.3
  45.0 0.9 copy-done.3
  45.9 1.0 make_block.1
  46.9 12.2 %all_to_all.25.got_ref = bf16[16,64,128]{2,1,0:T(8,128)(2,1)S(1)} all-to-all(bf16[16,64,128]{2,1,0:T(8,128)(2,1)S(1)} %get-tuple-element.32), channel_id=1, replica_groups=mesh['x'=4,'zl'=2,'core'=2,'zh'=4,'y'=4] {'x','zl','core'}, dimensions={0} | all-to-all | bytes 524288 | tf_op jit(solution)/shard_map/all_to_all | solution.py:316
  59.1 0.0 collective-permute-done.2.fac3.far_ref
  59.1 0.0 collective-permute-done.1.fac2.last_ref
  59.1 6.5 %collective-permute-done.fac1.near_ref = bf16[4,128,512]{2,1,0:T(8,128)(2,1)S(1)} collective-permute-done((bf16[4,128,512]{2,1,0:T(8,128)(2,1)S(1)}, bf16[4,128,512]{2,1,0:T(8,128)(2,1)S(1)}, u32[]{:S(2)}, u32[]{:S(2)}) %collective-permute-start) | collective-permute-done | bytes 524320 | tf_op jit(solution)/shard_map/ppermute | solution.py:257
  65.6 0.0 copy-start.2
  65.6 0.0 copy-start.4
  65.6 1.0 symmetrize.1
  66.7 18.7 %all_to_all.26.own_ref = bf16[8,64,1024]{2,1,0:T(8,128)(2,1)S(1)} all-to-all(bf16[8,64,1024]{2,1,0:T(8,128)(2,1)S(1)} %get-tuple-element.34), channel_id=1, replica_groups=mesh['x'=4,'zl'=2,'core'=2,'zh'=4,'y'=4] {'x','zl'}, dimensions={0} | all-to-all | bytes 2097152 | tf_op jit(solution)/shard_map/all_to_all | solution.py:325
  85.3 1.9 %collective-permute-start.9 = (bf16[8,64,1024]{2,1,0:T(8,128)(2,1)S(1)}, bf16[8,64,1024]{2,1,0:T(8,128)(2,1)S(1)}, u32[]{:S(2)}, u32[]{:S(2)}) collective-permute-start(bf16[8,64,1024]{2,1,0:T(8,128)(2,1)S(1)} %all_to_all.26.own_ref), channel_id=1, source_target_pairs={{0,16},{16,0},{1,17},{17,1},{2,18},{18,2},{3,19},{19,3},{4,20},{20... | collective-permute-start | bytes 3145736 | tf_op jit(solution)/shard_map/ppermute | solution.py:261
  87.3 0.0 copy-done.2
  87.3 0.0 copy-done.4
  87.3 1.4 %prepare_factors.1 = (bf16[4,4,64,1024]{3,2,1,0:T(8,128)(2,1)S(1)}, bf16[8,2,64,1024]{3,2,1,0:T(8,128)(2,1)S(1)}) custom-call(bf16[4,128,512]{2,1,0:T(8,128)(2,1)S(1)} %bitcast.9, bf16[4,128,512]{2,1,0:T(8,128)(2,1)S(1)} %collective-permute-done.fac1.near_ref, bf16[4,128,512]{2,1,0:T(8,128)(2,1)S(1)} %collective-permute-done.1.fac2.last_ref, ...), custom_call_target="tpu_custom_call" | custom-call | tf_op jit(solution)/shard_map/prepare_factors/pallas_call | solution.py:327
  88.7 0.9 collective-permute-done.9.other_ref
  89.6 3.5 %ladder.1 = (bf16[1024,1024]{1,0:T(8,128)(2,1)S(1)}, bf16[8,64,1024]{2,1,0:T(8,128)(2,1)S(1)}) custom-call(bf16[8,64,1024]{2,1,0:T(8,128)(2,1)S(1)} %all_to_all.26.own_ref, bf16[8,64,1024]{2,1,0:T(8,128)(2,1)S(1)} %collective-permute-done.9.other_ref, bf16[4,4,64,1024]{3,2,1,0:T(8,128)(2,1)S(1)} %get-tuple-element.35.right_ref, ...), custom_call_target="tpu_custom_call" | custom-call | tf_op jit(solution)/shard_map/ladder/pallas_call | solution.py:335
  93.0 0.5 collective-permute-start.10
  93.5 1.2 ladder_rest.1
  94.7 1.0 collective-permute-done.10
  95.8 0.4 add_convert_fusion
  96.2 17.9 %all_to_all.27.part_ref = bf16[8,64,1024]{2,1,0:T(8,128)(2,1)S(1)} all-to-all(bf16[8,64,1024]{2,1,0:T(8,128)(2,1)S(1)} %add_convert_fusion), channel_id=1, replica_groups=mesh['x'=4,'zl'=2,'core'=2,'zh'=4,'y'=4] {'x','zl'}, dimensions={0} | all-to-all | bytes 2097152 | tf_op jit(solution)/shard_map/all_to_all | solution.py:353
  114.1 0.4 sum_parts.1
  114.5 12.5 %all_to_all.28.resid_ref = bf16[16,32,128]{2,1,0:T(8,128)(2,1)} all-to-all(bf16[16,32,128]{2,1,0:T(8,128)(2,1)S(1)} %sum_parts.1), channel_id=1, replica_groups=mesh['x'=4,'zl'=2,'core'=2,'zh'=4,'y'=4] {'zh','y'}, dimensions={0} | all-to-all | bytes 262144 | tf_op jit(solution)/shard_map/all_to_all | solution.py:362
  127.0 2.1 %update.1 = bf16[16,4096]{1,0:T(8,128)(2,1)} custom-call(f32[4]{0:T(128)} %occ_ref.1, bf16[16,32,128]{2,1,0:T(8,128)(2,1)} %all_to_all.28.resid_ref, bf16[16,64,128]{2,1,0:T(8,128)(2,1)} %get-tuple-element.39.held_ref, f32[16,128]{1,0:T(8,128)} %get-tuple-element.40.mask_ref, f32[8,128]{1,0:T(8,128)} %bitcast.13), custom_call_target="tpu_custom_call" | custom-call | tf_op jit(solution)/shard_map/update/pallas_call | solution.py:363
Async XLA Ops:
  0.0 45.0 %copy-start.1 = (bf16[3,64,64]{2,1,0:T(8,128)(2,1)S(1)}, bf16[3,64,64]{2,1,0:T(8,128)(2,1)}, u32[]{:S(2)}) copy-start(bf16[3,64,64]{2,1,0:T(8,128)(2,1)} %constant.8.clone.small_ref) | copy-start | bytes 73732
  0.0 45.0 %copy-start = (bf16[1024,1024]{1,0:T(8,128)(2,1)S(1)}, bf16[1024,1024]{1,0:T(8,128)(2,1)}, u32[]{:S(2)}) copy-start(bf16[1024,1024]{1,0:T(8,128)(2,1)} %constant.9.clone.wide_ref) | copy-start | bytes 6291460
  1.9 35.5 %all-to-all-start = ((bf16[64,8,512]{2,1,0:T(8,128)(2,1)}), bf16[64,8,512]{2,1,0:T(8,128)(2,1)S(1)}, u32[]{:S(2)}, u32[]{:S(2)}) async-start(bf16[64,8,512]{2,1,0:T(8,128)(2,1)} %spread_factors.1), calls=%async_computation | async-start | bytes 1048576 | tf_op jit(solution)/shard_map/all_to_all | solution.py:286
  17.2 5.5 %collective-permute-start.3 = (bf16[4,96,128]{2,1,0:T(8,128)(2,1)}, bf16[4,96,128]{2,1,0:T(8,128)(2,1)S(1)}, u32[]{:S(2)}, u32[]{:S(2)}) collective-permute-start(bf16[4,96,128]{2,1,0:T(8,128)(2,1)} %get-tuple-element.25), channel_id=1, source_target_pairs={{0,1},{1,2},{2,3},{3,0},{4,5},{5,6},{6,7},{7,4},{8,9},{9,10},{10,1... | collective-permute-start | bytes 294920 | tf_op jit(solution)/shard_map/ppermute | solution.py:257
  18.5 7.4 %collective-permute-start.4 = (bf16[4,96,128]{2,1,0:T(8,128)(2,1)}, bf16[4,96,128]{2,1,0:T(8,128)(2,1)S(1)}, u32[]{:S(2)}, u32[]{:S(2)}) collective-permute-start(bf16[4,96,128]{2,1,0:T(8,128)(2,1)} %get-tuple-element.26), channel_id=1, source_target_pairs={{0,2},{1,3},{2,0},{3,1},{4,6},{5,7},{6,4},{7,5},{8,10},{9,11},{10,... | collective-permute-start | bytes 294920 | tf_op jit(solution)/shard_map/ppermute | solution.py:257
  21.1 4.8 %collective-permute-start.5 = (bf16[4,96,128]{2,1,0:T(8,128)(2,1)}, bf16[4,96,128]{2,1,0:T(8,128)(2,1)S(1)}, u32[]{:S(2)}, u32[]{:S(2)}) collective-permute-start(bf16[4,96,128]{2,1,0:T(8,128)(2,1)} %get-tuple-element.27), channel_id=1, source_target_pairs={{0,3},{1,0},{2,1},{3,2},{4,7},{5,4},{6,5},{7,6},{8,11},{9,8},{10,9... | collective-permute-start | bytes 294920 | tf_op jit(solution)/shard_map/ppermute | solution.py:257
  22.7 3.2 %copy-start.5 = (bf16[4,96,128]{2,1,0:T(8,128)(2,1)}, bf16[4,96,128]{2,1,0:T(8,128)(2,1)S(1)}, u32[]{:S(2)}) copy-start(bf16[4,96,128]{2,1,0:T(8,128)(2,1)S(1)} %collective-permute-done.3.in1) | copy-start | bytes 294916
  25.9 0.6 copy-start.6
  25.9 0.7 copy-start.7
  28.4 11.1 %collective-permute-start.6 = (bf16[4,96,128]{2,1,0:T(8,128)(2,1)}, bf16[4,96,128]{2,1,0:T(8,128)(2,1)S(1)}, u32[]{:S(2)}, u32[]{:S(2)}) collective-permute-start(bf16[4,96,128]{2,1,0:T(8,128)(2,1)} %get-tuple-element.29), channel_id=1, source_target_pairs={{0,4},{4,8},{8,12},{12,0},{1,5},{5,9},{9,13},{13,1},{2,6},{6,10},{... | collective-permute-start | bytes 294920 | tf_op jit(solution)/shard_map/ppermute | solution.py:257
  30.8 11.0 %collective-permute-start.7 = (bf16[4,96,128]{2,1,0:T(8,128)(2,1)}, bf16[4,96,128]{2,1,0:T(8,128)(2,1)S(1)}, u32[]{:S(2)}, u32[]{:S(2)}) collective-permute-start(bf16[4,96,128]{2,1,0:T(8,128)(2,1)} %get-tuple-element.30), channel_id=1, source_target_pairs={{0,8},{4,12},{8,0},{12,4},{1,9},{5,13},{9,1},{13,5},{2,10},{6,14},... | collective-permute-start | bytes 294920 | tf_op jit(solution)/shard_map/ppermute | solution.py:257
  34.3 10.7 %collective-permute-start.8 = (bf16[4,96,128]{2,1,0:T(8,128)(2,1)}, bf16[4,96,128]{2,1,0:T(8,128)(2,1)S(1)}, u32[]{:S(2)}, u32[]{:S(2)}) collective-permute-start(bf16[4,96,128]{2,1,0:T(8,128)(2,1)} %get-tuple-element.31), channel_id=1, source_target_pairs={{0,12},{4,0},{8,4},{12,8},{1,13},{5,1},{9,5},{13,9},{2,14},{6,2},{... | collective-permute-start | bytes 294920 | tf_op jit(solution)/shard_map/ppermute | solution.py:257
  37.5 21.6 %collective-permute-start.2 = (bf16[4,128,512]{2,1,0:T(8,128)(2,1)S(1)}, bf16[4,128,512]{2,1,0:T(8,128)(2,1)S(1)}, u32[]{:S(2)}, u32[]{:S(2)}) collective-permute-start(bf16[4,128,512]{2,1,0:T(8,128)(2,1)S(1)} %bitcast.6), channel_id=1, source_target_pairs={{0,3},{1,0},{2,1},{3,2},{4,7},{5,4},{6,5},{7,6},{8,11},{9,8},{10,9... | collective-permute-start | bytes 1572872 | tf_op jit(solution)/shard_map/ppermute | solution.py:257
  39.0 20.0 %collective-permute-start.1 = (bf16[4,128,512]{2,1,0:T(8,128)(2,1)S(1)}, bf16[4,128,512]{2,1,0:T(8,128)(2,1)S(1)}, u32[]{:S(2)}, u32[]{:S(2)}) collective-permute-start(bf16[4,128,512]{2,1,0:T(8,128)(2,1)S(1)} %bitcast.7), channel_id=1, source_target_pairs={{0,2},{1,3},{2,0},{3,1},{4,6},{5,7},{6,4},{7,5},{8,10},{9,11},{10,... | collective-permute-start | bytes 1572872 | tf_op jit(solution)/shard_map/ppermute | solution.py:257
  39.5 26.1 %collective-permute-start = (bf16[4,128,512]{2,1,0:T(8,128)(2,1)S(1)}, bf16[4,128,512]{2,1,0:T(8,128)(2,1)S(1)}, u32[]{:S(2)}, u32[]{:S(2)}) collective-permute-start(bf16[4,128,512]{2,1,0:T(8,128)(2,1)S(1)} %bitcast.8), channel_id=1, source_target_pairs={{0,1},{1,2},{2,3},{3,0},{4,5},{5,6},{6,7},{7,4},{8,9},{9,10},{10,1... | collective-permute-start | bytes 1572872 | tf_op jit(solution)/shard_map/ppermute | solution.py:257
  45.0 0.9 copy-start.3
  65.6 21.7 %copy-start.2 = (bf16[256,256]{1,0:T(8,128)(2,1)S(1)}, bf16[256,256]{1,0:T(8,128)(2,1)}, u32[]{:S(2)}) copy-start(bf16[256,256]{1,0:T(8,128)(2,1)} %constant.11.clone.rows_ref) | copy-start | bytes 393220
  65.6 21.7 %copy-start.4 = (bf16[128,128]{1,0:T(8,128)(2,1)S(1)}, bf16[128,128]{1,0:T(8,128)(2,1)}, u32[]{:S(2)}) copy-start(bf16[128,128]{1,0:T(8,128)(2,1)} %constant.10.clone.halves_ref) | copy-start | bytes 98308
  85.3 4.2 %collective-permute-start.9 = (bf16[8,64,1024]{2,1,0:T(8,128)(2,1)S(1)}, bf16[8,64,1024]{2,1,0:T(8,128)(2,1)S(1)}, u32[]{:S(2)}, u32[]{:S(2)}) collective-permute-start(bf16[8,64,1024]{2,1,0:T(8,128)(2,1)S(1)} %all_to_all.26.own_ref), channel_id=1, source_target_pairs={{0,16},{16,0},{1,17},{17,1},{2,18},{18,2},{3,19},{19,3},{4,20},{20... | collective-permute-start | bytes 3145736 | tf_op jit(solution)/shard_map/ppermute | solution.py:261
  93.0 2.7 %collective-permute-start.10 = (bf16[8,64,1024]{2,1,0:T(8,128)(2,1)S(1)}, bf16[8,64,1024]{2,1,0:T(8,128)(2,1)S(1)}, u32[]{:S(2)}, u32[]{:S(2)}) collective-permute-start(bf16[8,64,1024]{2,1,0:T(8,128)(2,1)S(1)} %get-tuple-element.37), channel_id=1, source_target_pairs={{0,16},{16,0},{1,17},{17,1},{2,18},{18,2},{3,19},{19,3},{4,20},{20... | collective-permute-start | bytes 3145736 | tf_op jit(solution)/shard_map/ppermute | solution.py:261

commit v6 on v5

--- a/solution.py
+++ b/solution.py
@@ -178,19 +178,33 @@
                 out_ref[x * 4 + chip, :, cols] = part[chip * 64 : chip * 64 + 64]
 
 
-def _ladder_kernel(own_ref, other_ref, right_ref, left_ref, inner_ref, give_ref):
+def _first_step(amp_ref, right_ref, put):
+    for i in range(2):
+        rows = amp_ref[i * 4 : i * 4 + 4].reshape(256, 1024)
+        for j in range(4):
+            part = lax.dot_general(rows, right_ref[j].reshape(256, 1024), NT, preferred_element_type=F32)
+            put(i, slice(j * 256, j * 256 + 256), part.astype(BF16))
+
+
+def _own_kernel(own_ref, right_ref, part_ref):
+    def put(i, cols, part):
+        part_ref[i * 4 : i * 4 + 4, :, cols] = part.reshape(4, 64, 256)
+
+    _first_step(own_ref, right_ref, put)
+
+
+def _ladder_kernel(other_ref, right_ref, left_ref, part_ref, inner_ref, give_ref):
     core = lax.axis_index("core")
     first = core == 0
-    for i in range(4):
-        rows = []
-        for chip in (2 * i, 2 * i + 1):
-            own, other = own_ref[chip], other_ref[chip]
-            rows += [jnp.where(first, own, other), jnp.where(first, other, own)]
-        rows = jnp.concatenate(rows, axis=0)
-        for j in range(4):
-            inner_ref[i * 256 : i * 256 + 256, j * 256 : j * 256 + 256] = lax.dot_general(
-                rows, right_ref[j].reshape(256, 1024), NT, preferred_element_type=F32
-            ).astype(BF16)
+
+    def put(i, cols, part):
+        for chip in range(4):
+            own, other = part_ref[i * 4 + chip, :, cols], part[chip * 64 : chip * 64 + 64]
+            at = (i * 4 + chip) * 128
+            inner_ref[at : at + 64, cols] = jnp.where(first, own, other)
+            inner_ref[at + 64 : at + 128, cols] = jnp.where(first, other, own)
+
+    _first_step(other_ref, right_ref, put)
     _second_step(left_ref, 1 - core, inner_ref, give_ref)
 
 
@@ -332,6 +346,14 @@
         compiler_params=VMEM,
         name="prepare_factors",
     )(fac, near, opposite, far, halves, rows_b)
+    part = pl.pallas_call(
+        _own_kernel,
+        out_shape=_sds(8, 64, 1024),
+        in_specs=[_vmem()] * 2,
+        out_specs=_vmem(),
+        compiler_params=VMEM,
+        name="ladder_own",
+    )(own, right)
     inner, give = pl.pallas_call(
         _ladder_kernel,
         out_shape=(_sds(1024, 1024), _sds(8, 64, 1024)),
@@ -339,7 +361,7 @@
         out_specs=(_vmem(), _vmem()),
         compiler_params=VMEM,
         name="ladder",
-    )(own, other, right, left)
+    )(other, right, left, part)
     keep = pl.pallas_call(
         _rest_kernel,
         out_shape=_sds(8, 64, 1024),

time: 129 us -> 129 us (level)
  transfers between devices with their start and end apart: 12 -> 12, of which waited for: 7 -> 6; matrix products, arithmetic and copies ran while one was open for 0% -> 0% of each run, Pallas kernels for 6% -> 7%
where the time goes in v6:
time: 129 us
  blocking collectives  61.5 us (48%)
  starting transfers between devices  31.9 us (25%)
  Pallas kernels  16.9 us (13%)
  waiting for transfers between devices  16.3 us (13%)
  local copies, waits for them, and re-layouts  1.58 us (1%)
    all_to_all x1, blocking collectives, _shards(): own = lax.all_to_all(block, CHIPS, 0, 0, tiled=True)  18.7 us
    all_to_all x1, blocking collectives, _shards(): parts = lax.all_to_all(partial, CHIPS, 0, 0, tiled=True)  18.1 us
    ppermute x9, starting transfers between devices, _turn(): return lax.ppermute(value, axis, [(i, (i + step) % 4) for i in range(4)])  16.9 us
    ppermute x9, waiting for transfers between devices, _turn(): return lax.ppermute(value, axis, [(i, (i + step) % 4) for i in range(4)])  14.9 us
    all_to_all x1, starting transfers between devices, _shards(): lax.all_to_all(spread, ('zh',) + ROWS, 0, 0, tiled=True)  13 us
    all_to_all x1, blocking collectives, _shards(): back = lax.all_to_all(last, COLS, 0, 0, tiled=True)  12.5 us
    all_to_all x1, blocking collectives, _shards(): turn = lax.all_to_all(turn, ROWS, 0, 0, tiled=True)  12.2 us
  transfers between devices with their start and end apart: 12, of which 6 were waited for; matrix products, arithmetic and copies ran while one was open for 0% of the time, Pallas kernels for 7%

profile of v6, /device:TPU:1, one launch (start us, length us, event | category | flops | bytes accessed | tf_op | source)
XLA Modules:
  0.0 128.7 jit_solution(17592301145553701124)
XLA Ops:
  0.0 0.0 copy-start.1
  0.0 0.0 copy-start
  0.0 1.9 %spread_factors.1 = bf16[64,8,512]{2,1,0:T(8,128)(2,1)} custom-call(bf16[16,4,1024]{2,1,0:T(4,128)(2,1)} %fac_ref.1), custom_call_target="tpu_custom_call" | custom-call | tf_op jit(solution)/shard_map/spread_factors/pallas_call | solution.py:291
  1.9 13.0 %all-to-all-start = ((bf16[64,8,512]{2,1,0:T(8,128)(2,1)}), bf16[64,8,512]{2,1,0:T(8,128)(2,1)S(1)}, u32[]{:S(2)}, u32[]{:S(2)}) async-start(bf16[64,8,512]{2,1,0:T(8,128)(2,1)} %spread_factors.1), calls=%async_computation | async-start | bytes 1048576 | tf_op jit(solution)/shard_map/all_to_all | solution.py:300
  15.0 2.3 %mask_amps.1 = (bf16[16,64,128]{2,1,0:T(8,128)(2,1)}, f32[16,128]{1,0:T(8,128)}, bf16[4,96,128]{2,1,0:T(8,128)(2,1)}, bf16[4,96,128]{2,1,0:T(8,128)(2,1)}, bf16[...) custom-call(bf16[16,4096]{1,0:T(8,128)(2,1)} %bitcast.10, bf16[16,4096]{1,0:T(8,128)(2,1)} %bitcast.11, ...), custom_call_target="tpu_custom_call" | custom-call | tf_op jit(solution)/shard_map/mask_amps/pallas_call | solution.py:302
  17.2 1.3 %collective-permute-start.3 = (bf16[4,96,128]{2,1,0:T(8,128)(2,1)}, bf16[4,96,128]{2,1,0:T(8,128)(2,1)S(1)}, u32[]{:S(2)}, u32[]{:S(2)}) collective-permute-start(bf16[4,96,128]{2,1,0:T(8,128)(2,1)} %get-tuple-element.25), channel_id=1, source_target_pairs={{0,1},{1,2},{2,3},{3,0},{4,5},{5,6},{6,7},{7,4},{8,9},{9,10},{10,1... | collective-permute-start | bytes 294920 | tf_op jit(solution)/shard_map/ppermute | solution.py:271
  18.5 2.6 %collective-permute-start.4 = (bf16[4,96,128]{2,1,0:T(8,128)(2,1)}, bf16[4,96,128]{2,1,0:T(8,128)(2,1)S(1)}, u32[]{:S(2)}, u32[]{:S(2)}) collective-permute-start(bf16[4,96,128]{2,1,0:T(8,128)(2,1)} %get-tuple-element.26), channel_id=1, source_target_pairs={{0,2},{1,3},{2,0},{3,1},{4,6},{5,7},{6,4},{7,5},{8,10},{9,11},{10,... | collective-permute-start | bytes 294920 | tf_op jit(solution)/shard_map/ppermute | solution.py:271
  21.1 1.1 collective-permute-start.5
  22.2 0.5 collective-permute-done.3.in1
  22.7 0.0 copy-start.5
  22.7 3.2 %collective-permute-done.4.in2 = bf16[4,96,128]{2,1,0:T(8,128)(2,1)S(1)} collective-permute-done((bf16[4,96,128]{2,1,0:T(8,128)(2,1)}, bf16[4,96,128]{2,1,0:T(8,128)(2,1)S(1)}, u32[]{:S(2)}, u32[]{:S(2)}) %collective-permute-start.4) | collective-permute-done | bytes 98336 | tf_op jit(solution)/shard_map/ppermute | solution.py:271
  25.9 0.0 copy-start.6
  25.9 0.0 collective-permute-done.5.in3
  25.9 0.0 copy-start.7
  25.9 0.0 copy-done.5
  25.9 0.6 copy-done.6
  26.6 0.0 copy-done.7
  26.6 1.8 %relay.1 = (bf16[4,96,128]{2,1,0:T(8,128)(2,1)}, bf16[4,96,128]{2,1,0:T(8,128)(2,1)}, bf16[4,96,128]{2,1,0:T(8,128)(2,1)}, bf16[4,96,128]{2,1,0:T(8,128)(2,1)}) custom-call(bf16[4,96,128]{2,1,0:T(8,128)(2,1)} %get-tuple-element.24.in0, bf16[4,96,128]{2,1,0:T(8,128)(2,1)} %copy-done.5, bf16[4,96,128]{2,1,0:T(8,128)(2,1)} %copy-done.6, ...), custom_call_target="tpu_custom_call" | custom-call | tf_op jit(solution)/shard_map/relay/pallas_call | solution.py:311
  28.4 2.4 %collective-permute-start.6 = (bf16[4,96,128]{2,1,0:T(8,128)(2,1)}, bf16[4,96,128]{2,1,0:T(8,128)(2,1)S(1)}, u32[]{:S(2)}, u32[]{:S(2)}) collective-permute-start(bf16[4,96,128]{2,1,0:T(8,128)(2,1)} %get-tuple-element.29), channel_id=1, source_target_pairs={{0,4},{4,8},{8,12},{12,0},{1,5},{5,9},{9,13},{13,1},{2,6},{6,10},{... | collective-permute-start | bytes 294920 | tf_op jit(solution)/shard_map/ppermute | solution.py:271
  30.8 3.5 %collective-permute-start.7 = (bf16[4,96,128]{2,1,0:T(8,128)(2,1)}, bf16[4,96,128]{2,1,0:T(8,128)(2,1)S(1)}, u32[]{:S(2)}, u32[]{:S(2)}) collective-permute-start(bf16[4,96,128]{2,1,0:T(8,128)(2,1)} %get-tuple-element.30), channel_id=1, source_target_pairs={{0,8},{4,12},{8,0},{12,4},{1,9},{5,13},{9,1},{13,5},{2,10},{6,14},... | collective-permute-start | bytes 294920 | tf_op jit(solution)/shard_map/ppermute | solution.py:271
  34.3 3.2 %collective-permute-start.8 = (bf16[4,96,128]{2,1,0:T(8,128)(2,1)}, bf16[4,96,128]{2,1,0:T(8,128)(2,1)S(1)}, u32[]{:S(2)}, u32[]{:S(2)}) collective-permute-start(bf16[4,96,128]{2,1,0:T(8,128)(2,1)} %get-tuple-element.31), channel_id=1, source_target_pairs={{0,12},{4,0},{8,4},{12,8},{1,13},{5,1},{9,5},{13,9},{2,14},{6,2},{... | collective-permute-start | bytes 294920 | tf_op jit(solution)/shard_map/ppermute | solution.py:271
  37.5 0.0 all-to-all-done
  37.5 1.5 %collective-permute-start.2 = (bf16[4,128,512]{2,1,0:T(8,128)(2,1)S(1)}, bf16[4,128,512]{2,1,0:T(8,128)(2,1)S(1)}, u32[]{:S(2)}, u32[]{:S(2)}) collective-permute-start(bf16[4,128,512]{2,1,0:T(8,128)(2,1)S(1)} %bitcast.6), channel_id=1, source_target_pairs={{0,3},{1,0},{2,1},{3,2},{4,7},{5,4},{6,5},{7,6},{8,11},{9,8},{10,9... | collective-permute-start | bytes 1572872 | tf_op jit(solution)/shard_map/ppermute | solution.py:271
  39.0 0.5 collective-permute-start.1
  39.5 0.0 collective-permute-done.6.in1
  39.5 0.9 collective-permute-start
  40.3 1.5 %collective-permute-done.7.in2 = bf16[4,96,128]{2,1,0:T(8,128)(2,1)S(1)} collective-permute-done((bf16[4,96,128]{2,1,0:T(8,128)(2,1)}, bf16[4,96,128]{2,1,0:T(8,128)(2,1)S(1)}, u32[]{:S(2)}, u32[]{:S(2)}) %collective-permute-start.7) | collective-permute-done | bytes 98336 | tf_op jit(solution)/shard_map/ppermute | solution.py:271
  41.9 3.1 %collective-permute-done.8.in3 = bf16[4,96,128]{2,1,0:T(8,128)(2,1)S(1)} collective-permute-done((bf16[4,96,128]{2,1,0:T(8,128)(2,1)}, bf16[4,96,128]{2,1,0:T(8,128)(2,1)S(1)}, u32[]{:S(2)}, u32[]{:S(2)}) %collective-permute-start.8) | collective-permute-done | bytes 98336 | tf_op jit(solution)/shard_map/ppermute | solution.py:271
  45.0 0.0 copy-done.1
  45.0 0.0 copy-done
  45.0 0.0 copy-start.3
  45.0 0.9 copy-done.3
  45.9 1.0 make_block.1
  46.9 12.2 %all_to_all.25.got_ref = bf16[16,64,128]{2,1,0:T(8,128)(2,1)S(1)} all-to-all(bf16[16,64,128]{2,1,0:T(8,128)(2,1)S(1)} %get-tuple-element.32), channel_id=1, replica_groups=mesh['x'=4,'zl'=2,'core'=2,'zh'=4,'y'=4] {'x','zl','core'}, dimensions={0} | all-to-all | bytes 524288 | tf_op jit(solution)/shard_map/all_to_all | solution.py:330
  59.1 0.0 collective-permute-done.2.fac3.far_ref
  59.1 0.0 collective-permute-done.1.fac2.last_ref
  59.1 6.5 %collective-permute-done.fac1.near_ref = bf16[4,128,512]{2,1,0:T(8,128)(2,1)S(1)} collective-permute-done((bf16[4,128,512]{2,1,0:T(8,128)(2,1)S(1)}, bf16[4,128,512]{2,1,0:T(8,128)(2,1)S(1)}, u32[]{:S(2)}, u32[]{:S(2)}) %collective-permute-start) | collective-permute-done | bytes 524320 | tf_op jit(solution)/shard_map/ppermute | solution.py:271
  65.6 0.0 copy-start.2
  65.6 0.0 copy-start.4
  65.6 1.0 symmetrize.1
  66.7 18.7 %all_to_all.26.own_ref = bf16[8,64,1024]{2,1,0:T(8,128)(2,1)S(1)} all-to-all(bf16[8,64,1024]{2,1,0:T(8,128)(2,1)S(1)} %get-tuple-element.34), channel_id=1, replica_groups=mesh['x'=4,'zl'=2,'core'=2,'zh'=4,'y'=4] {'x','zl'}, dimensions={0} | all-to-all | bytes 2097152 | tf_op jit(solution)/shard_map/all_to_all | solution.py:339
  85.3 1.9 %collective-permute-start.9 = (bf16[8,64,1024]{2,1,0:T(8,128)(2,1)S(1)}, bf16[8,64,1024]{2,1,0:T(8,128)(2,1)S(1)}, u32[]{:S(2)}, u32[]{:S(2)}) collective-permute-start(bf16[8,64,1024]{2,1,0:T(8,128)(2,1)S(1)} %all_to_all.26.own_ref), channel_id=1, source_target_pairs={{0,16},{16,0},{1,17},{17,1},{2,18},{18,2},{3,19},{19,3},{4,20},{20... | collective-permute-start | bytes 3145736 | tf_op jit(solution)/shard_map/ppermute | solution.py:275
  87.3 0.0 copy-done.2
  87.3 0.0 copy-done.4
  87.3 1.4 %prepare_factors.1 = (bf16[4,4,64,1024]{3,2,1,0:T(8,128)(2,1)S(1)}, bf16[8,2,64,1024]{3,2,1,0:T(8,128)(2,1)S(1)}) custom-call(bf16[4,128,512]{2,1,0:T(8,128)(2,1)S(1)} %bitcast.9, bf16[4,128,512]{2,1,0:T(8,128)(2,1)S(1)} %collective-permute-done.fac1.near_ref, bf16[4,128,512]{2,1,0:T(8,128)(2,1)S(1)} %collective-permute-done.1.fac2.last_ref, ...), custom_call_target="tpu_custom_call" | custom-call | tf_op jit(solution)/shard_map/prepare_factors/pallas_call | solution.py:341
  88.7 1.3 ladder_own.1.part_ref
  90.0 0.0 collective-permute-done.9.other_ref
  90.0 2.4 %ladder.1 = (bf16[1024,1024]{1,0:T(8,128)(2,1)S(1)}, bf16[8,64,1024]{2,1,0:T(8,128)(2,1)S(1)}) custom-call(bf16[8,64,1024]{2,1,0:T(8,128)(2,1)S(1)} %collective-permute-done.9.other_ref, bf16[4,4,64,1024]{3,2,1,0:T(8,128)(2,1)S(1)} %get-tuple-element.35.right_ref, bf16[8,2,64,1024]{3,2,1,0:T(8,128)(2,1)S(1)} %get-tuple-element.23.left_ref, ...), custom_call_target="tpu_custom_call" | custom-call | tf_op jit(solution)/shard_map/ladder/pallas_call | solution.py:357
  92.4 0.1 collective-permute-start.10
  92.5 1.2 ladder_rest.1
  93.8 1.4 %collective-permute-done.10 = bf16[8,64,1024]{2,1,0:T(8,128)(2,1)S(1)} collective-permute-done((bf16[8,64,1024]{2,1,0:T(8,128)(2,1)S(1)}, bf16[8,64,1024]{2,1,0:T(8,128)(2,1)S(1)}, u32[]{:S(2)}, u32[]{:S(2)}) %collective-permute-start.10) | collective-permute-done | bytes 1048608 | tf_op jit(solution)/shard_map/ppermute | solution.py:275
  95.2 0.4 add_convert_fusion
  95.6 18.1 %all_to_all.27.part_ref = bf16[8,64,1024]{2,1,0:T(8,128)(2,1)S(1)} all-to-all(bf16[8,64,1024]{2,1,0:T(8,128)(2,1)S(1)} %add_convert_fusion), channel_id=1, replica_groups=mesh['x'=4,'zl'=2,'core'=2,'zh'=4,'y'=4] {'x','zl'}, dimensions={0} | all-to-all | bytes 2097152 | tf_op jit(solution)/shard_map/all_to_all | solution.py:375
  113.7 0.4 sum_parts.1
  114.1 12.5 %all_to_all.28.resid_ref = bf16[16,32,128]{2,1,0:T(8,128)(2,1)} all-to-all(bf16[16,32,128]{2,1,0:T(8,128)(2,1)S(1)} %sum_parts.1), channel_id=1, replica_groups=mesh['x'=4,'zl'=2,'core'=2,'zh'=4,'y'=4] {'zh','y'}, dimensions={0} | all-to-all | bytes 262144 | tf_op jit(solution)/shard_map/all_to_all | solution.py:384
  126.6 2.1 %update.1 = bf16[16,4096]{1,0:T(8,128)(2,1)} custom-call(f32[4]{0:T(128)} %occ_ref.1, bf16[16,32,128]{2,1,0:T(8,128)(2,1)} %all_to_all.28.resid_ref, bf16[16,64,128]{2,1,0:T(8,128)(2,1)} %get-tuple-element.39.held_ref, f32[16,128]{1,0:T(8,128)} %get-tuple-element.40.mask_ref, f32[8,128]{1,0:T(8,128)} %bitcast.13), custom_call_target="tpu_custom_call" | custom-call | tf_op jit(solution)/shard_map/update/pallas_call | solution.py:385
Async XLA Ops:
  0.0 45.0 %copy-start.1 = (bf16[3,64,64]{2,1,0:T(8,128)(2,1)S(1)}, bf16[3,64,64]{2,1,0:T(8,128)(2,1)}, u32[]{:S(2)}) copy-start(bf16[3,64,64]{2,1,0:T(8,128)(2,1)} %constant.8.clone.small_ref) | copy-start | bytes 73732
  0.0 45.0 %copy-start = (bf16[1024,1024]{1,0:T(8,128)(2,1)S(1)}, bf16[1024,1024]{1,0:T(8,128)(2,1)}, u32[]{:S(2)}) copy-start(bf16[1024,1024]{1,0:T(8,128)(2,1)} %constant.9.clone.wide_ref) | copy-start | bytes 6291460
  1.9 35.5 %all-to-all-start = ((bf16[64,8,512]{2,1,0:T(8,128)(2,1)}), bf16[64,8,512]{2,1,0:T(8,128)(2,1)S(1)}, u32[]{:S(2)}, u32[]{:S(2)}) async-start(bf16[64,8,512]{2,1,0:T(8,128)(2,1)} %spread_factors.1), calls=%async_computation | async-start | bytes 1048576 | tf_op jit(solution)/shard_map/all_to_all | solution.py:300
  17.2 5.5 %collective-permute-start.3 = (bf16[4,96,128]{2,1,0:T(8,128)(2,1)}, bf16[4,96,128]{2,1,0:T(8,128)(2,1)S(1)}, u32[]{:S(2)}, u32[]{:S(2)}) collective-permute-start(bf16[4,96,128]{2,1,0:T(8,128)(2,1)} %get-tuple-element.25), channel_id=1, source_target_pairs={{0,1},{1,2},{2,3},{3,0},{4,5},{5,6},{6,7},{7,4},{8,9},{9,10},{10,1... | collective-permute-start | bytes 294920 | tf_op jit(solution)/shard_map/ppermute | solution.py:271
  18.5 7.4 %collective-permute-start.4 = (bf16[4,96,128]{2,1,0:T(8,128)(2,1)}, bf16[4,96,128]{2,1,0:T(8,128)(2,1)S(1)}, u32[]{:S(2)}, u32[]{:S(2)}) collective-permute-start(bf16[4,96,128]{2,1,0:T(8,128)(2,1)} %get-tuple-element.26), channel_id=1, source_target_pairs={{0,2},{1,3},{2,0},{3,1},{4,6},{5,7},{6,4},{7,5},{8,10},{9,11},{10,... | collective-permute-start | bytes 294920 | tf_op jit(solution)/shard_map/ppermute | solution.py:271
  21.1 4.8 %collective-permute-start.5 = (bf16[4,96,128]{2,1,0:T(8,128)(2,1)}, bf16[4,96,128]{2,1,0:T(8,128)(2,1)S(1)}, u32[]{:S(2)}, u32[]{:S(2)}) collective-permute-start(bf16[4,96,128]{2,1,0:T(8,128)(2,1)} %get-tuple-element.27), channel_id=1, source_target_pairs={{0,3},{1,0},{2,1},{3,2},{4,7},{5,4},{6,5},{7,6},{8,11},{9,8},{10,9... | collective-permute-start | bytes 294920 | tf_op jit(solution)/shard_map/ppermute | solution.py:271
  22.7 3.2 %copy-start.5 = (bf16[4,96,128]{2,1,0:T(8,128)(2,1)}, bf16[4,96,128]{2,1,0:T(8,128)(2,1)S(1)}, u32[]{:S(2)}) copy-start(bf16[4,96,128]{2,1,0:T(8,128)(2,1)S(1)} %collective-permute-done.3.in1) | copy-start | bytes 294916
  25.9 0.6 copy-start.6
  25.9 0.7 copy-start.7
  28.4 11.1 %collective-permute-start.6 = (bf16[4,96,128]{2,1,0:T(8,128)(2,1)}, bf16[4,96,128]{2,1,0:T(8,128)(2,1)S(1)}, u32[]{:S(2)}, u32[]{:S(2)}) collective-permute-start(bf16[4,96,128]{2,1,0:T(8,128)(2,1)} %get-tuple-element.29), channel_id=1, source_target_pairs={{0,4},{4,8},{8,12},{12,0},{1,5},{5,9},{9,13},{13,1},{2,6},{6,10},{... | collective-permute-start | bytes 294920 | tf_op jit(solution)/shard_map/ppermute | solution.py:271
  30.8 11.0 %collective-permute-start.7 = (bf16[4,96,128]{2,1,0:T(8,128)(2,1)}, bf16[4,96,128]{2,1,0:T(8,128)(2,1)S(1)}, u32[]{:S(2)}, u32[]{:S(2)}) collective-permute-start(bf16[4,96,128]{2,1,0:T(8,128)(2,1)} %get-tuple-element.30), channel_id=1, source_target_pairs={{0,8},{4,12},{8,0},{12,4},{1,9},{5,13},{9,1},{13,5},{2,10},{6,14},... | collective-permute-start | bytes 294920 | tf_op jit(solution)/shard_map/ppermute | solution.py:271
  34.3 10.7 %collective-permute-start.8 = (bf16[4,96,128]{2,1,0:T(8,128)(2,1)}, bf16[4,96,128]{2,1,0:T(8,128)(2,1)S(1)}, u32[]{:S(2)}, u32[]{:S(2)}) collective-permute-start(bf16[4,96,128]{2,1,0:T(8,128)(2,1)} %get-tuple-element.31), channel_id=1, source_target_pairs={{0,12},{4,0},{8,4},{12,8},{1,13},{5,1},{9,5},{13,9},{2,14},{6,2},{... | collective-permute-start | bytes 294920 | tf_op jit(solution)/shard_map/ppermute | solution.py:271
  37.5 21.6 %collective-permute-start.2 = (bf16[4,128,512]{2,1,0:T(8,128)(2,1)S(1)}, bf16[4,128,512]{2,1,0:T(8,128)(2,1)S(1)}, u32[]{:S(2)}, u32[]{:S(2)}) collective-permute-start(bf16[4,128,512]{2,1,0:T(8,128)(2,1)S(1)} %bitcast.6), channel_id=1, source_target_pairs={{0,3},{1,0},{2,1},{3,2},{4,7},{5,4},{6,5},{7,6},{8,11},{9,8},{10,9... | collective-permute-start | bytes 1572872 | tf_op jit(solution)/shard_map/ppermute | solution.py:271
  39.0 20.0 %collective-permute-start.1 = (bf16[4,128,512]{2,1,0:T(8,128)(2,1)S(1)}, bf16[4,128,512]{2,1,0:T(8,128)(2,1)S(1)}, u32[]{:S(2)}, u32[]{:S(2)}) collective-permute-start(bf16[4,128,512]{2,1,0:T(8,128)(2,1)S(1)} %bitcast.7), channel_id=1, source_target_pairs={{0,2},{1,3},{2,0},{3,1},{4,6},{5,7},{6,4},{7,5},{8,10},{9,11},{10,... | collective-permute-start | bytes 1572872 | tf_op jit(solution)/shard_map/ppermute | solution.py:271
  39.5 26.1 %collective-permute-start = (bf16[4,128,512]{2,1,0:T(8,128)(2,1)S(1)}, bf16[4,128,512]{2,1,0:T(8,128)(2,1)S(1)}, u32[]{:S(2)}, u32[]{:S(2)}) collective-permute-start(bf16[4,128,512]{2,1,0:T(8,128)(2,1)S(1)} %bitcast.8), channel_id=1, source_target_pairs={{0,1},{1,2},{2,3},{3,0},{4,5},{5,6},{6,7},{7,4},{8,9},{9,10},{10,1... | collective-permute-start | bytes 1572872 | tf_op jit(solution)/shard_map/ppermute | solution.py:271
  45.0 0.9 copy-start.3
  65.6 21.7 %copy-start.2 = (bf16[256,256]{1,0:T(8,128)(2,1)S(1)}, bf16[256,256]{1,0:T(8,128)(2,1)}, u32[]{:S(2)}) copy-start(bf16[256,256]{1,0:T(8,128)(2,1)} %constant.11.clone.rows_ref) | copy-start | bytes 393220
  65.6 21.7 %copy-start.4 = (bf16[128,128]{1,0:T(8,128)(2,1)S(1)}, bf16[128,128]{1,0:T(8,128)(2,1)}, u32[]{:S(2)}) copy-start(bf16[128,128]{1,0:T(8,128)(2,1)} %constant.10.clone.halves_ref) | copy-start | bytes 98308
  85.3 4.6 %collective-permute-start.9 = (bf16[8,64,1024]{2,1,0:T(8,128)(2,1)S(1)}, bf16[8,64,1024]{2,1,0:T(8,128)(2,1)S(1)}, u32[]{:S(2)}, u32[]{:S(2)}) collective-permute-start(bf16[8,64,1024]{2,1,0:T(8,128)(2,1)S(1)} %all_to_all.26.own_ref), channel_id=1, source_target_pairs={{0,16},{16,0},{1,17},{17,1},{2,18},{18,2},{3,19},{19,3},{4,20},{20... | collective-permute-start | bytes 3145736 | tf_op jit(solution)/shard_map/ppermute | solution.py:275
  92.4 2.7 %collective-permute-start.10 = (bf16[8,64,1024]{2,1,0:T(8,128)(2,1)S(1)}, bf16[8,64,1024]{2,1,0:T(8,128)(2,1)S(1)}, u32[]{:S(2)}, u32[]{:S(2)}) collective-permute-start(bf16[8,64,1024]{2,1,0:T(8,128)(2,1)S(1)} %get-tuple-element.37), channel_id=1, source_target_pairs={{0,16},{16,0},{1,17},{17,1},{2,18},{18,2},{3,19},{19,3},{4,20},{20... | collective-permute-start | bytes 3145736 | tf_op jit(solution)/shard_map/ppermute | solution.py:275

commit v7 on v6

--- a/solution.py
+++ b/solution.py
@@ -149,10 +149,6 @@
     kept_ref[...] = lax.dot_general(source, wide_ref[...], NT, preferred_element_type=F32).astype(BF16)
 
 
-def _gate_kernel(value_ref, small_ref, out_ref):
-    del value_ref, small_ref, out_ref
-
-
 def _factor_kernel(fac0, fac1, fac2, fac3, halves_ref, rows_ref, right_ref, left_ref):
     y = lax.axis_index("y")
     for k, ref in enumerate((fac0, fac1, fac2, fac3)):
@@ -275,17 +271,6 @@
     return lax.ppermute(value, "core", [(0, 1), (1, 0)])
 
 
-def _after(value, small):
-    return pl.pallas_call(
-        _gate_kernel,
-        out_shape=jax.ShapeDtypeStruct(value.shape, value.dtype),
-        in_specs=[_vmem(), ANY],
-        out_specs=_vmem(),
-        input_output_aliases={0: 0},
-        name="gate",
-    )(value, small)
-
-
 def _shards(tables, amps, source, factors, screen, occ_energy, vir_energy):
     small, wide, rows_b, halves = tables
     spread = pl.pallas_call(
@@ -304,7 +289,7 @@
         out_shape=(_sds(16, 64, 128), _sds(16, 128, dtype=F32)) + (four,) * 4,
         in_specs=[_vmem()] * 3,
         out_specs=(_vmem(),) * 6,
-        scratch_shapes=[pltpu.VMEM((512, 128), F32)] * 2,
+        scratch_shapes=[pltpu.VMEM((544, 128), F32)] * 2,
         name="mask_amps",
     )(amps.reshape(16, 4096), source.reshape(16, 4096), screen.transpose(1, 2, 0))
     outs = [_turn(out, "y", k) for k, out in enumerate(outs)]
@@ -387,7 +372,7 @@
         out_shape=_sds(16, 4096),
         in_specs=[SMEM, _vmem(), _vmem(), _vmem(), _vmem()],
         out_specs=_vmem(),
-        scratch_shapes=[pltpu.VMEM((512, 128), F32)],
+        scratch_shapes=[pltpu.VMEM((544, 128), F32)],
         name="update",
     )(occ_energy, back, held, mask, vir_energy.reshape(8, 128))
     return out.reshape(1, 1, 16, 4096)

time: 129 us -> 129 us (level)
  no operation moved by 1% of the time
where the time goes in v7:
time: 129 us
  blocking collectives  61.5 us (48%)
  starting transfers between devices  31.9 us (25%)
  Pallas kernels  16.9 us (13%)
  waiting for transfers between devices  16.3 us (13%)
  local copies, waits for them, and re-layouts  1.58 us (1%)
    all_to_all x1, blocking collectives, _shards(): own = lax.all_to_all(block, CHIPS, 0, 0, tiled=True)  18.7 us
    all_to_all x1, blocking collectives, _shards(): parts = lax.all_to_all(partial, CHIPS, 0, 0, tiled=True)  18.1 us
    ppermute x9, starting transfers between devices, _turn(): return lax.ppermute(value, axis, [(i, (i + step) % 4) for i in range(4)])  16.9 us
    ppermute x9, waiting for transfers between devices, _turn(): return lax.ppermute(value, axis, [(i, (i + step) % 4) for i in range(4)])  14.9 us
    all_to_all x1, starting transfers between devices, _shards(): lax.all_to_all(spread, ('zh',) + ROWS, 0, 0, tiled=True)  13 us
    all_to_all x1, blocking collectives, _shards(): back = lax.all_to_all(last, COLS, 0, 0, tiled=True)  12.5 us
    all_to_all x1, blocking collectives, _shards(): turn = lax.all_to_all(turn, ROWS, 0, 0, tiled=True)  12.2 us
  transfers between devices with their start and end apart: 12, of which 6 were waited for; matrix products, arithmetic and copies ran while one was open for 0% of the time, Pallas kernels for 7%

profile of v7, /device:TPU:1, one launch (start us, length us, event | category | flops | bytes accessed | tf_op | source)
XLA Modules:
  0.0 128.7 jit_solution(8248177562142298420)
XLA Ops:
  0.0 0.0 copy-start.1
  0.0 0.0 copy-start
  0.0 1.9 %spread_factors.1 = bf16[64,8,512]{2,1,0:T(8,128)(2,1)} custom-call(bf16[16,4,1024]{2,1,0:T(4,128)(2,1)} %fac_ref.1), custom_call_target="tpu_custom_call" | custom-call | tf_op jit(solution)/shard_map/spread_factors/pallas_call | solution.py:276
  1.9 13.0 %all-to-all-start = ((bf16[64,8,512]{2,1,0:T(8,128)(2,1)}), bf16[64,8,512]{2,1,0:T(8,128)(2,1)S(1)}, u32[]{:S(2)}, u32[]{:S(2)}) async-start(bf16[64,8,512]{2,1,0:T(8,128)(2,1)} %spread_factors.1), calls=%async_computation | async-start | bytes 1048576 | tf_op jit(solution)/shard_map/all_to_all | solution.py:285
  15.0 2.3 %mask_amps.1 = (bf16[16,64,128]{2,1,0:T(8,128)(2,1)}, f32[16,128]{1,0:T(8,128)}, bf16[4,96,128]{2,1,0:T(8,128)(2,1)}, bf16[4,96,128]{2,1,0:T(8,128)(2,1)}, bf16[...) custom-call(bf16[16,4096]{1,0:T(8,128)(2,1)} %bitcast.10, bf16[16,4096]{1,0:T(8,128)(2,1)} %bitcast.11, ...), custom_call_target="tpu_custom_call" | custom-call | tf_op jit(solution)/shard_map/mask_amps/pallas_call | solution.py:287
  17.2 1.3 %collective-permute-start.3 = (bf16[4,96,128]{2,1,0:T(8,128)(2,1)}, bf16[4,96,128]{2,1,0:T(8,128)(2,1)S(1)}, u32[]{:S(2)}, u32[]{:S(2)}) collective-permute-start(bf16[4,96,128]{2,1,0:T(8,128)(2,1)} %get-tuple-element.25), channel_id=1, source_target_pairs={{0,1},{1,2},{2,3},{3,0},{4,5},{5,6},{6,7},{7,4},{8,9},{9,10},{10,1... | collective-permute-start | bytes 294920 | tf_op jit(solution)/shard_map/ppermute | solution.py:267
  18.5 2.6 %collective-permute-start.4 = (bf16[4,96,128]{2,1,0:T(8,128)(2,1)}, bf16[4,96,128]{2,1,0:T(8,128)(2,1)S(1)}, u32[]{:S(2)}, u32[]{:S(2)}) collective-permute-start(bf16[4,96,128]{2,1,0:T(8,128)(2,1)} %get-tuple-element.26), channel_id=1, source_target_pairs={{0,2},{1,3},{2,0},{3,1},{4,6},{5,7},{6,4},{7,5},{8,10},{9,11},{10,... | collective-permute-start | bytes 294920 | tf_op jit(solution)/shard_map/ppermute | solution.py:267
  21.1 1.1 collective-permute-start.5
  22.2 0.5 collective-permute-done.3.in1
  22.7 0.0 copy-start.5
  22.7 3.2 %collective-permute-done.4.in2 = bf16[4,96,128]{2,1,0:T(8,128)(2,1)S(1)} collective-permute-done((bf16[4,96,128]{2,1,0:T(8,128)(2,1)}, bf16[4,96,128]{2,1,0:T(8,128)(2,1)S(1)}, u32[]{:S(2)}, u32[]{:S(2)}) %collective-permute-start.4) | collective-permute-done | bytes 98336 | tf_op jit(solution)/shard_map/ppermute | solution.py:267
  25.9 0.0 copy-start.6
  25.9 0.0 collective-permute-done.5.in3
  25.9 0.0 copy-start.7
  25.9 0.0 copy-done.5
  25.9 0.6 copy-done.6
  26.6 0.0 copy-done.7
  26.6 1.8 %relay.1 = (bf16[4,96,128]{2,1,0:T(8,128)(2,1)}, bf16[4,96,128]{2,1,0:T(8,128)(2,1)}, bf16[4,96,128]{2,1,0:T(8,128)(2,1)}, bf16[4,96,128]{2,1,0:T(8,128)(2,1)}) custom-call(bf16[4,96,128]{2,1,0:T(8,128)(2,1)} %get-tuple-element.24.in0, bf16[4,96,128]{2,1,0:T(8,128)(2,1)} %copy-done.5, bf16[4,96,128]{2,1,0:T(8,128)(2,1)} %copy-done.6, ...), custom_call_target="tpu_custom_call" | custom-call | tf_op jit(solution)/shard_map/relay/pallas_call | solution.py:296
  28.4 2.4 %collective-permute-start.6 = (bf16[4,96,128]{2,1,0:T(8,128)(2,1)}, bf16[4,96,128]{2,1,0:T(8,128)(2,1)S(1)}, u32[]{:S(2)}, u32[]{:S(2)}) collective-permute-start(bf16[4,96,128]{2,1,0:T(8,128)(2,1)} %get-tuple-element.29), channel_id=1, source_target_pairs={{0,4},{4,8},{8,12},{12,0},{1,5},{5,9},{9,13},{13,1},{2,6},{6,10},{... | collective-permute-start | bytes 294920 | tf_op jit(solution)/shard_map/ppermute | solution.py:267
  30.8 3.5 %collective-permute-start.7 = (bf16[4,96,128]{2,1,0:T(8,128)(2,1)}, bf16[4,96,128]{2,1,0:T(8,128)(2,1)S(1)}, u32[]{:S(2)}, u32[]{:S(2)}) collective-permute-start(bf16[4,96,128]{2,1,0:T(8,128)(2,1)} %get-tuple-element.30), channel_id=1, source_target_pairs={{0,8},{4,12},{8,0},{12,4},{1,9},{5,13},{9,1},{13,5},{2,10},{6,14},... | collective-permute-start | bytes 294920 | tf_op jit(solution)/shard_map/ppermute | solution.py:267
  34.3 3.2 %collective-permute-start.8 = (bf16[4,96,128]{2,1,0:T(8,128)(2,1)}, bf16[4,96,128]{2,1,0:T(8,128)(2,1)S(1)}, u32[]{:S(2)}, u32[]{:S(2)}) collective-permute-start(bf16[4,96,128]{2,1,0:T(8,128)(2,1)} %get-tuple-element.31), channel_id=1, source_target_pairs={{0,12},{4,0},{8,4},{12,8},{1,13},{5,1},{9,5},{13,9},{2,14},{6,2},{... | collective-permute-start | bytes 294920 | tf_op jit(solution)/shard_map/ppermute | solution.py:267
  37.5 0.0 all-to-all-done
  37.5 1.5 %collective-permute-start.2 = (bf16[4,128,512]{2,1,0:T(8,128)(2,1)S(1)}, bf16[4,128,512]{2,1,0:T(8,128)(2,1)S(1)}, u32[]{:S(2)}, u32[]{:S(2)}) collective-permute-start(bf16[4,128,512]{2,1,0:T(8,128)(2,1)S(1)} %bitcast.6), channel_id=1, source_target_pairs={{0,3},{1,0},{2,1},{3,2},{4,7},{5,4},{6,5},{7,6},{8,11},{9,8},{10,9... | collective-permute-start | bytes 1572872 | tf_op jit(solution)/shard_map/ppermute | solution.py:267
  39.0 0.5 collective-permute-start.1
  39.5 0.0 collective-permute-done.6.in1
  39.5 0.9 collective-permute-start
  40.3 1.5 %collective-permute-done.7.in2 = bf16[4,96,128]{2,1,0:T(8,128)(2,1)S(1)} collective-permute-done((bf16[4,96,128]{2,1,0:T(8,128)(2,1)}, bf16[4,96,128]{2,1,0:T(8,128)(2,1)S(1)}, u32[]{:S(2)}, u32[]{:S(2)}) %collective-permute-start.7) | collective-permute-done | bytes 98336 | tf_op jit(solution)/shard_map/ppermute | solution.py:267
  41.9 3.1 %collective-permute-done.8.in3 = bf16[4,96,128]{2,1,0:T(8,128)(2,1)S(1)} collective-permute-done((bf16[4,96,128]{2,1,0:T(8,128)(2,1)}, bf16[4,96,128]{2,1,0:T(8,128)(2,1)S(1)}, u32[]{:S(2)}, u32[]{:S(2)}) %collective-permute-start.8) | collective-permute-done | bytes 98336 | tf_op jit(solution)/shard_map/ppermute | solution.py:267
  45.0 0.0 copy-done.1
  45.0 0.0 copy-done
  45.0 0.0 copy-start.3
  45.0 0.9 copy-done.3
  45.9 1.0 make_block.1
  46.9 12.2 %all_to_all.25.got_ref = bf16[16,64,128]{2,1,0:T(8,128)(2,1)S(1)} all-to-all(bf16[16,64,128]{2,1,0:T(8,128)(2,1)S(1)} %get-tuple-element.32), channel_id=1, replica_groups=mesh['x'=4,'zl'=2,'core'=2,'zh'=4,'y'=4] {'x','zl','core'}, dimensions={0} | all-to-all | bytes 524288 | tf_op jit(solution)/shard_map/all_to_all | solution.py:315
  59.1 0.0 collective-permute-done.2.fac3.far_ref
  59.1 0.0 collective-permute-done.1.fac2.last_ref
  59.1 6.5 %collective-permute-done.fac1.near_ref = bf16[4,128,512]{2,1,0:T(8,128)(2,1)S(1)} collective-permute-done((bf16[4,128,512]{2,1,0:T(8,128)(2,1)S(1)}, bf16[4,128,512]{2,1,0:T(8,128)(2,1)S(1)}, u32[]{:S(2)}, u32[]{:S(2)}) %collective-permute-start) | collective-permute-done | bytes 524320 | tf_op jit(solution)/shard_map/ppermute | solution.py:267
  65.6 0.0 copy-start.2
  65.6 0.0 copy-start.4
  65.6 1.0 symmetrize.1
  66.7 18.7 %all_to_all.26.own_ref = bf16[8,64,1024]{2,1,0:T(8,128)(2,1)S(1)} all-to-all(bf16[8,64,1024]{2,1,0:T(8,128)(2,1)S(1)} %get-tuple-element.34), channel_id=1, replica_groups=mesh['x'=4,'zl'=2,'core'=2,'zh'=4,'y'=4] {'x','zl'}, dimensions={0} | all-to-all | bytes 2097152 | tf_op jit(solution)/shard_map/all_to_all | solution.py:324
  85.3 1.9 %collective-permute-start.9 = (bf16[8,64,1024]{2,1,0:T(8,128)(2,1)S(1)}, bf16[8,64,1024]{2,1,0:T(8,128)(2,1)S(1)}, u32[]{:S(2)}, u32[]{:S(2)}) collective-permute-start(bf16[8,64,1024]{2,1,0:T(8,128)(2,1)S(1)} %all_to_all.26.own_ref), channel_id=1, source_target_pairs={{0,16},{16,0},{1,17},{17,1},{2,18},{18,2},{3,19},{19,3},{4,20},{20... | collective-permute-start | bytes 3145736 | tf_op jit(solution)/shard_map/ppermute | solution.py:271
  87.3 0.0 copy-done.2
  87.3 0.0 copy-done.4
  87.3 1.4 %prepare_factors.1 = (bf16[4,4,64,1024]{3,2,1,0:T(8,128)(2,1)S(1)}, bf16[8,2,64,1024]{3,2,1,0:T(8,128)(2,1)S(1)}) custom-call(bf16[4,128,512]{2,1,0:T(8,128)(2,1)S(1)} %bitcast.9, bf16[4,128,512]{2,1,0:T(8,128)(2,1)S(1)} %collective-permute-done.fac1.near_ref, bf16[4,128,512]{2,1,0:T(8,128)(2,1)S(1)} %collective-permute-done.1.fac2.last_ref, ...), custom_call_target="tpu_custom_call" | custom-call | tf_op jit(solution)/shard_map/prepare_factors/pallas_call | solution.py:326
  88.7 1.3 ladder_own.1.part_ref
  90.0 0.0 collective-permute-done.9.other_ref
  90.0 2.4 %ladder.1 = (bf16[1024,1024]{1,0:T(8,128)(2,1)S(1)}, bf16[8,64,1024]{2,1,0:T(8,128)(2,1)S(1)}) custom-call(bf16[8,64,1024]{2,1,0:T(8,128)(2,1)S(1)} %collective-permute-done.9.other_ref, bf16[4,4,64,1024]{3,2,1,0:T(8,128)(2,1)S(1)} %get-tuple-element.35.right_ref, bf16[8,2,64,1024]{3,2,1,0:T(8,128)(2,1)S(1)} %get-tuple-element.23.left_ref, ...), custom_call_target="tpu_custom_call" | custom-call | tf_op jit(solution)/shard_map/ladder/pallas_call | solution.py:342
  92.4 0.1 collective-permute-start.10
  92.5 1.2 ladder_rest.1
  93.8 1.4 %collective-permute-done.10 = bf16[8,64,1024]{2,1,0:T(8,128)(2,1)S(1)} collective-permute-done((bf16[8,64,1024]{2,1,0:T(8,128)(2,1)S(1)}, bf16[8,64,1024]{2,1,0:T(8,128)(2,1)S(1)}, u32[]{:S(2)}, u32[]{:S(2)}) %collective-permute-start.10) | collective-permute-done | bytes 1048608 | tf_op jit(solution)/shard_map/ppermute | solution.py:271
  95.2 0.4 add_convert_fusion
  95.6 18.1 %all_to_all.27.part_ref = bf16[8,64,1024]{2,1,0:T(8,128)(2,1)S(1)} all-to-all(bf16[8,64,1024]{2,1,0:T(8,128)(2,1)S(1)} %add_convert_fusion), channel_id=1, replica_groups=mesh['x'=4,'zl'=2,'core'=2,'zh'=4,'y'=4] {'x','zl'}, dimensions={0} | all-to-all | bytes 2097152 | tf_op jit(solution)/shard_map/all_to_all | solution.py:360
  113.7 0.4 sum_parts.1
  114.1 12.5 %all_to_all.28.resid_ref = bf16[16,32,128]{2,1,0:T(8,128)(2,1)} all-to-all(bf16[16,32,128]{2,1,0:T(8,128)(2,1)S(1)} %sum_parts.1), channel_id=1, replica_groups=mesh['x'=4,'zl'=2,'core'=2,'zh'=4,'y'=4] {'zh','y'}, dimensions={0} | all-to-all | bytes 262144 | tf_op jit(solution)/shard_map/all_to_all | solution.py:369
  126.6 2.1 %update.1 = bf16[16,4096]{1,0:T(8,128)(2,1)} custom-call(f32[4]{0:T(128)} %occ_ref.1, bf16[16,32,128]{2,1,0:T(8,128)(2,1)} %all_to_all.28.resid_ref, bf16[16,64,128]{2,1,0:T(8,128)(2,1)} %get-tuple-element.39.held_ref, f32[16,128]{1,0:T(8,128)} %get-tuple-element.40.mask_ref, f32[8,128]{1,0:T(8,128)} %bitcast.13), custom_call_target="tpu_custom_call" | custom-call | tf_op jit(solution)/shard_map/update/pallas_call | solution.py:370
Async XLA Ops:
  0.0 45.0 %copy-start.1 = (bf16[3,64,64]{2,1,0:T(8,128)(2,1)S(1)}, bf16[3,64,64]{2,1,0:T(8,128)(2,1)}, u32[]{:S(2)}) copy-start(bf16[3,64,64]{2,1,0:T(8,128)(2,1)} %constant.8.clone.small_ref) | copy-start | bytes 73732
  0.0 45.0 %copy-start = (bf16[1024,1024]{1,0:T(8,128)(2,1)S(1)}, bf16[1024,1024]{1,0:T(8,128)(2,1)}, u32[]{:S(2)}) copy-start(bf16[1024,1024]{1,0:T(8,128)(2,1)} %constant.9.clone.wide_ref) | copy-start | bytes 6291460
  1.9 35.5 %all-to-all-start = ((bf16[64,8,512]{2,1,0:T(8,128)(2,1)}), bf16[64,8,512]{2,1,0:T(8,128)(2,1)S(1)}, u32[]{:S(2)}, u32[]{:S(2)}) async-start(bf16[64,8,512]{2,1,0:T(8,128)(2,1)} %spread_factors.1), calls=%async_computation | async-start | bytes 1048576 | tf_op jit(solution)/shard_map/all_to_all | solution.py:285
  17.2 5.5 %collective-permute-start.3 = (bf16[4,96,128]{2,1,0:T(8,128)(2,1)}, bf16[4,96,128]{2,1,0:T(8,128)(2,1)S(1)}, u32[]{:S(2)}, u32[]{:S(2)}) collective-permute-start(bf16[4,96,128]{2,1,0:T(8,128)(2,1)} %get-tuple-element.25), channel_id=1, source_target_pairs={{0,1},{1,2},{2,3},{3,0},{4,5},{5,6},{6,7},{7,4},{8,9},{9,10},{10,1... | collective-permute-start | bytes 294920 | tf_op jit(solution)/shard_map/ppermute | solution.py:267
  18.5 7.4 %collective-permute-start.4 = (bf16[4,96,128]{2,1,0:T(8,128)(2,1)}, bf16[4,96,128]{2,1,0:T(8,128)(2,1)S(1)}, u32[]{:S(2)}, u32[]{:S(2)}) collective-permute-start(bf16[4,96,128]{2,1,0:T(8,128)(2,1)} %get-tuple-element.26), channel_id=1, source_target_pairs={{0,2},{1,3},{2,0},{3,1},{4,6},{5,7},{6,4},{7,5},{8,10},{9,11},{10,... | collective-permute-start | bytes 294920 | tf_op jit(solution)/shard_map/ppermute | solution.py:267
  21.1 4.8 %collective-permute-start.5 = (bf16[4,96,128]{2,1,0:T(8,128)(2,1)}, bf16[4,96,128]{2,1,0:T(8,128)(2,1)S(1)}, u32[]{:S(2)}, u32[]{:S(2)}) collective-permute-start(bf16[4,96,128]{2,1,0:T(8,128)(2,1)} %get-tuple-element.27), channel_id=1, source_target_pairs={{0,3},{1,0},{2,1},{3,2},{4,7},{5,4},{6,5},{7,6},{8,11},{9,8},{10,9... | collective-permute-start | bytes 294920 | tf_op jit(solution)/shard_map/ppermute | solution.py:267
  22.7 3.2 %copy-start.5 = (bf16[4,96,128]{2,1,0:T(8,128)(2,1)}, bf16[4,96,128]{2,1,0:T(8,128)(2,1)S(1)}, u32[]{:S(2)}) copy-start(bf16[4,96,128]{2,1,0:T(8,128)(2,1)S(1)} %collective-permute-done.3.in1) | copy-start | bytes 294916
  25.9 0.6 copy-start.6
  25.9 0.7 copy-start.7
  28.4 11.1 %collective-permute-start.6 = (bf16[4,96,128]{2,1,0:T(8,128)(2,1)}, bf16[4,96,128]{2,1,0:T(8,128)(2,1)S(1)}, u32[]{:S(2)}, u32[]{:S(2)}) collective-permute-start(bf16[4,96,128]{2,1,0:T(8,128)(2,1)} %get-tuple-element.29), channel_id=1, source_target_pairs={{0,4},{4,8},{8,12},{12,0},{1,5},{5,9},{9,13},{13,1},{2,6},{6,10},{... | collective-permute-start | bytes 294920 | tf_op jit(solution)/shard_map/ppermute | solution.py:267
  30.8 11.0 %collective-permute-start.7 = (bf16[4,96,128]{2,1,0:T(8,128)(2,1)}, bf16[4,96,128]{2,1,0:T(8,128)(2,1)S(1)}, u32[]{:S(2)}, u32[]{:S(2)}) collective-permute-start(bf16[4,96,128]{2,1,0:T(8,128)(2,1)} %get-tuple-element.30), channel_id=1, source_target_pairs={{0,8},{4,12},{8,0},{12,4},{1,9},{5,13},{9,1},{13,5},{2,10},{6,14},... | collective-permute-start | bytes 294920 | tf_op jit(solution)/shard_map/ppermute | solution.py:267
  34.3 10.7 %collective-permute-start.8 = (bf16[4,96,128]{2,1,0:T(8,128)(2,1)}, bf16[4,96,128]{2,1,0:T(8,128)(2,1)S(1)}, u32[]{:S(2)}, u32[]{:S(2)}) collective-permute-start(bf16[4,96,128]{2,1,0:T(8,128)(2,1)} %get-tuple-element.31), channel_id=1, source_target_pairs={{0,12},{4,0},{8,4},{12,8},{1,13},{5,1},{9,5},{13,9},{2,14},{6,2},{... | collective-permute-start | bytes 294920 | tf_op jit(solution)/shard_map/ppermute | solution.py:267
  37.5 21.6 %collective-permute-start.2 = (bf16[4,128,512]{2,1,0:T(8,128)(2,1)S(1)}, bf16[4,128,512]{2,1,0:T(8,128)(2,1)S(1)}, u32[]{:S(2)}, u32[]{:S(2)}) collective-permute-start(bf16[4,128,512]{2,1,0:T(8,128)(2,1)S(1)} %bitcast.6), channel_id=1, source_target_pairs={{0,3},{1,0},{2,1},{3,2},{4,7},{5,4},{6,5},{7,6},{8,11},{9,8},{10,9... | collective-permute-start | bytes 1572872 | tf_op jit(solution)/shard_map/ppermute | solution.py:267
  39.0 20.0 %collective-permute-start.1 = (bf16[4,128,512]{2,1,0:T(8,128)(2,1)S(1)}, bf16[4,128,512]{2,1,0:T(8,128)(2,1)S(1)}, u32[]{:S(2)}, u32[]{:S(2)}) collective-permute-start(bf16[4,128,512]{2,1,0:T(8,128)(2,1)S(1)} %bitcast.7), channel_id=1, source_target_pairs={{0,2},{1,3},{2,0},{3,1},{4,6},{5,7},{6,4},{7,5},{8,10},{9,11},{10,... | collective-permute-start | bytes 1572872 | tf_op jit(solution)/shard_map/ppermute | solution.py:267
  39.5 26.1 %collective-permute-start = (bf16[4,128,512]{2,1,0:T(8,128)(2,1)S(1)}, bf16[4,128,512]{2,1,0:T(8,128)(2,1)S(1)}, u32[]{:S(2)}, u32[]{:S(2)}) collective-permute-start(bf16[4,128,512]{2,1,0:T(8,128)(2,1)S(1)} %bitcast.8), channel_id=1, source_target_pairs={{0,1},{1,2},{2,3},{3,0},{4,5},{5,6},{6,7},{7,4},{8,9},{9,10},{10,1... | collective-permute-start | bytes 1572872 | tf_op jit(solution)/shard_map/ppermute | solution.py:267
  45.0 0.9 copy-start.3
  65.6 21.7 %copy-start.2 = (bf16[256,256]{1,0:T(8,128)(2,1)S(1)}, bf16[256,256]{1,0:T(8,128)(2,1)}, u32[]{:S(2)}) copy-start(bf16[256,256]{1,0:T(8,128)(2,1)} %constant.11.clone.rows_ref) | copy-start | bytes 393220
  65.6 21.7 %copy-start.4 = (bf16[128,128]{1,0:T(8,128)(2,1)S(1)}, bf16[128,128]{1,0:T(8,128)(2,1)}, u32[]{:S(2)}) copy-start(bf16[128,128]{1,0:T(8,128)(2,1)} %constant.10.clone.halves_ref) | copy-start | bytes 98308
  85.3 4.6 %collective-permute-start.9 = (bf16[8,64,1024]{2,1,0:T(8,128)(2,1)S(1)}, bf16[8,64,1024]{2,1,0:T(8,128)(2,1)S(1)}, u32[]{:S(2)}, u32[]{:S(2)}) collective-permute-start(bf16[8,64,1024]{2,1,0:T(8,128)(2,1)S(1)} %all_to_all.26.own_ref), channel_id=1, source_target_pairs={{0,16},{16,0},{1,17},{17,1},{2,18},{18,2},{3,19},{19,3},{4,20},{20... | collective-permute-start | bytes 3145736 | tf_op jit(solution)/shard_map/ppermute | solution.py:271
  92.4 2.7 %collective-permute-start.10 = (bf16[8,64,1024]{2,1,0:T(8,128)(2,1)S(1)}, bf16[8,64,1024]{2,1,0:T(8,128)(2,1)S(1)}, u32[]{:S(2)}, u32[]{:S(2)}) collective-permute-start(bf16[8,64,1024]{2,1,0:T(8,128)(2,1)S(1)} %get-tuple-element.37), channel_id=1, source_target_pairs={{0,16},{16,0},{1,17},{17,1},{2,18},{18,2},{3,19},{19,3},{4,20},{20... | collective-permute-start | bytes 3145736 | tf_op jit(solution)/shard_map/ppermute | solution.py:271

commit v8 on v7

--- a/solution.py
+++ b/solution.py
@@ -133,10 +133,7 @@
         sent_ref[row, 32:, :] = _pack(whole[128:, cols])
 
 
-def _symmetric_kernel(
-    got_ref, amp_ref, small_ref, wide_ref, near_ref, far_ref, last_ref, sent_ref, kept_ref
-):
-    del near_ref, far_ref, last_ref
+def _symmetric_kernel(got_ref, amp_ref, small_ref, wide_ref, sent_ref, kept_ref):
 
     def turned(offset):
         tall = jnp.concatenate([_unpack(got_ref[row, offset : offset + 32, :]) for row in range(16)], axis=0)
@@ -147,6 +144,10 @@
         sent_ref[to] = block
     source = turned(32).astype(BF16)
     kept_ref[...] = lax.dot_general(source, wide_ref[...], NT, preferred_element_type=F32).astype(BF16)
+
+
+def _gate_kernel(*refs):
+    del refs
 
 
 def _factor_kernel(fac0, fac1, fac2, fac3, halves_ref, rows_ref, right_ref, left_ref):
@@ -316,11 +317,20 @@
     block, kept = pl.pallas_call(
         _symmetric_kernel,
         out_shape=(_sds(8, 64, 1024), _sds(64, 1024)),
-        in_specs=[_vmem()] * 4 + [ANY] * 3,
+        in_specs=[_vmem()] * 4,
         out_specs=(_vmem(), _vmem()),
         compiler_params=VMEM,
         name="symmetrize",
-    )(turn, block, small, wide, near, far, opposite)
+    )(turn, block, small, wide)
+    block = pl.pallas_call(
+        _gate_kernel,
+        out_shape=_sds(8, 64, 1024),
+        in_specs=[_vmem()] + [ANY] * 3,
+        out_specs=_vmem(),
+        input_output_aliases={0: 0},
+        compiler_params=VMEM,
+        name="gate",
+    )(block, near, far, opposite)
     own = lax.all_to_all(block, CHIPS, 0, 0, tiled=True)
     other = _swap_cores(own)
     right, left = pl.pallas_call(

time: 129 us -> 128 us (level)
  transfers between devices with their start and end apart: 12 -> 12, of which waited for: 6 -> 6; matrix products, arithmetic and copies ran while one was open for 0% -> 0% of each run, Pallas kernels for 7% -> 8%
where the time goes in v8:
time: 128 us
  blocking collectives  61.6 us (48%)
  starting transfers between devices  31.9 us (25%)
  Pallas kernels  16.9 us (13%)
  waiting for transfers between devices  15.2 us (12%)
  local copies, waits for them, and re-layouts  1.58 us (1%)
    all_to_all x1, blocking collectives, _shards(): own = lax.all_to_all(block, CHIPS, 0, 0, tiled=True)  18.8 us
    all_to_all x1, blocking collectives, _shards(): parts = lax.all_to_all(partial, CHIPS, 0, 0, tiled=True)  18.1 us
    ppermute x9, starting transfers between devices, _turn(): return lax.ppermute(value, axis, [(i, (i + step) % 4) for i in range(4)])  16.9 us
    ppermute x9, waiting for transfers between devices, _turn(): return lax.ppermute(value, axis, [(i, (i + step) % 4) for i in range(4)])  13.8 us
    all_to_all x1, starting transfers between devices, _shards(): lax.all_to_all(spread, ('zh',) + ROWS, 0, 0, tiled=True)  13 us
    all_to_all x1, blocking collectives, _shards(): back = lax.all_to_all(last, COLS, 0, 0, tiled=True)  12.5 us
    all_to_all x1, blocking collectives, _shards(): turn = lax.all_to_all(turn, ROWS, 0, 0, tiled=True)  12.2 us
  transfers between devices with their start and end apart: 12, of which 6 were waited for; matrix products, arithmetic and copies ran while one was open for 0% of the time, Pallas kernels for 8%

profile of v8, /device:TPU:1, one launch (start us, length us, event | category | flops | bytes accessed | tf_op | source)
XLA Modules:
  0.0 127.8 jit_solution(16388467222903187630)
XLA Ops:
  0.0 0.0 copy-start.1
  0.0 0.0 copy-start
  0.0 1.9 %spread_factors.1 = bf16[64,8,512]{2,1,0:T(8,128)(2,1)} custom-call(bf16[16,4,1024]{2,1,0:T(4,128)(2,1)} %fac_ref.1), custom_call_target="tpu_custom_call" | custom-call | tf_op jit(solution)/shard_map/spread_factors/pallas_call | solution.py:277
  1.9 13.0 %all-to-all-start = ((bf16[64,8,512]{2,1,0:T(8,128)(2,1)}), bf16[64,8,512]{2,1,0:T(8,128)(2,1)S(1)}, u32[]{:S(2)}, u32[]{:S(2)}) async-start(bf16[64,8,512]{2,1,0:T(8,128)(2,1)} %spread_factors.1), calls=%async_computation | async-start | bytes 1048576 | tf_op jit(solution)/shard_map/all_to_all | solution.py:286
  15.0 2.3 %mask_amps.1 = (bf16[16,64,128]{2,1,0:T(8,128)(2,1)}, f32[16,128]{1,0:T(8,128)}, bf16[4,96,128]{2,1,0:T(8,128)(2,1)}, bf16[4,96,128]{2,1,0:T(8,128)(2,1)}, bf16[...) custom-call(bf16[16,4096]{1,0:T(8,128)(2,1)} %bitcast.10, bf16[16,4096]{1,0:T(8,128)(2,1)} %bitcast.11, ...), custom_call_target="tpu_custom_call" | custom-call | tf_op jit(solution)/shard_map/mask_amps/pallas_call | solution.py:288
  17.2 1.3 %collective-permute-start.3 = (bf16[4,96,128]{2,1,0:T(8,128)(2,1)}, bf16[4,96,128]{2,1,0:T(8,128)(2,1)S(1)}, u32[]{:S(2)}, u32[]{:S(2)}) collective-permute-start(bf16[4,96,128]{2,1,0:T(8,128)(2,1)} %get-tuple-element.25), channel_id=1, source_target_pairs={{0,1},{1,2},{2,3},{3,0},{4,5},{5,6},{6,7},{7,4},{8,9},{9,10},{10,1... | collective-permute-start | bytes 294920 | tf_op jit(solution)/shard_map/ppermute | solution.py:268
  18.5 2.6 %collective-permute-start.4 = (bf16[4,96,128]{2,1,0:T(8,128)(2,1)}, bf16[4,96,128]{2,1,0:T(8,128)(2,1)S(1)}, u32[]{:S(2)}, u32[]{:S(2)}) collective-permute-start(bf16[4,96,128]{2,1,0:T(8,128)(2,1)} %get-tuple-element.26), channel_id=1, source_target_pairs={{0,2},{1,3},{2,0},{3,1},{4,6},{5,7},{6,4},{7,5},{8,10},{9,11},{10,... | collective-permute-start | bytes 294920 | tf_op jit(solution)/shard_map/ppermute | solution.py:268
  21.1 1.1 collective-permute-start.5
  22.2 0.5 collective-permute-done.3.in1
  22.7 0.0 copy-start.5
  22.7 3.2 %collective-permute-done.4.in2 = bf16[4,96,128]{2,1,0:T(8,128)(2,1)S(1)} collective-permute-done((bf16[4,96,128]{2,1,0:T(8,128)(2,1)}, bf16[4,96,128]{2,1,0:T(8,128)(2,1)S(1)}, u32[]{:S(2)}, u32[]{:S(2)}) %collective-permute-start.4) | collective-permute-done | bytes 98336 | tf_op jit(solution)/shard_map/ppermute | solution.py:268
  25.9 0.0 copy-start.6
  25.9 0.0 collective-permute-done.5.in3
  25.9 0.0 copy-start.7
  25.9 0.0 copy-done.5
  25.9 0.6 copy-done.6
  26.6 0.0 copy-done.7
  26.6 1.8 %relay.1 = (bf16[4,96,128]{2,1,0:T(8,128)(2,1)}, bf16[4,96,128]{2,1,0:T(8,128)(2,1)}, bf16[4,96,128]{2,1,0:T(8,128)(2,1)}, bf16[4,96,128]{2,1,0:T(8,128)(2,1)}) custom-call(bf16[4,96,128]{2,1,0:T(8,128)(2,1)} %get-tuple-element.24.in0, bf16[4,96,128]{2,1,0:T(8,128)(2,1)} %copy-done.5, bf16[4,96,128]{2,1,0:T(8,128)(2,1)} %copy-done.6, ...), custom_call_target="tpu_custom_call" | custom-call | tf_op jit(solution)/shard_map/relay/pallas_call | solution.py:297
  28.4 2.4 %collective-permute-start.6 = (bf16[4,96,128]{2,1,0:T(8,128)(2,1)}, bf16[4,96,128]{2,1,0:T(8,128)(2,1)S(1)}, u32[]{:S(2)}, u32[]{:S(2)}) collective-permute-start(bf16[4,96,128]{2,1,0:T(8,128)(2,1)} %get-tuple-element.29), channel_id=1, source_target_pairs={{0,4},{4,8},{8,12},{12,0},{1,5},{5,9},{9,13},{13,1},{2,6},{6,10},{... | collective-permute-start | bytes 294920 | tf_op jit(solution)/shard_map/ppermute | solution.py:268
  30.8 3.5 %collective-permute-start.7 = (bf16[4,96,128]{2,1,0:T(8,128)(2,1)}, bf16[4,96,128]{2,1,0:T(8,128)(2,1)S(1)}, u32[]{:S(2)}, u32[]{:S(2)}) collective-permute-start(bf16[4,96,128]{2,1,0:T(8,128)(2,1)} %get-tuple-element.30), channel_id=1, source_target_pairs={{0,8},{4,12},{8,0},{12,4},{1,9},{5,13},{9,1},{13,5},{2,10},{6,14},... | collective-permute-start | bytes 294920 | tf_op jit(solution)/shard_map/ppermute | solution.py:268
  34.3 3.2 %collective-permute-start.8 = (bf16[4,96,128]{2,1,0:T(8,128)(2,1)}, bf16[4,96,128]{2,1,0:T(8,128)(2,1)S(1)}, u32[]{:S(2)}, u32[]{:S(2)}) collective-permute-start(bf16[4,96,128]{2,1,0:T(8,128)(2,1)} %get-tuple-element.31), channel_id=1, source_target_pairs={{0,12},{4,0},{8,4},{12,8},{1,13},{5,1},{9,5},{13,9},{2,14},{6,2},{... | collective-permute-start | bytes 294920 | tf_op jit(solution)/shard_map/ppermute | solution.py:268
  37.5 0.0 all-to-all-done
  37.5 1.5 %collective-permute-start.2 = (bf16[4,128,512]{2,1,0:T(8,128)(2,1)S(1)}, bf16[4,128,512]{2,1,0:T(8,128)(2,1)S(1)}, u32[]{:S(2)}, u32[]{:S(2)}) collective-permute-start(bf16[4,128,512]{2,1,0:T(8,128)(2,1)S(1)} %bitcast.6), channel_id=1, source_target_pairs={{0,3},{1,0},{2,1},{3,2},{4,7},{5,4},{6,5},{7,6},{8,11},{9,8},{10,9... | collective-permute-start | bytes 1572872 | tf_op jit(solution)/shard_map/ppermute | solution.py:268
  39.0 0.5 collective-permute-start.1
  39.5 0.0 collective-permute-done.6.in1
  39.5 0.9 collective-permute-start
  40.3 1.5 %collective-permute-done.7.in2 = bf16[4,96,128]{2,1,0:T(8,128)(2,1)S(1)} collective-permute-done((bf16[4,96,128]{2,1,0:T(8,128)(2,1)}, bf16[4,96,128]{2,1,0:T(8,128)(2,1)S(1)}, u32[]{:S(2)}, u32[]{:S(2)}) %collective-permute-start.7) | collective-permute-done | bytes 98336 | tf_op jit(solution)/shard_map/ppermute | solution.py:268
  41.9 3.1 %collective-permute-done.8.in3 = bf16[4,96,128]{2,1,0:T(8,128)(2,1)S(1)} collective-permute-done((bf16[4,96,128]{2,1,0:T(8,128)(2,1)}, bf16[4,96,128]{2,1,0:T(8,128)(2,1)S(1)}, u32[]{:S(2)}, u32[]{:S(2)}) %collective-permute-start.8) | collective-permute-done | bytes 98336 | tf_op jit(solution)/shard_map/ppermute | solution.py:268
  45.0 0.0 copy-done.1
  45.0 0.0 copy-done
  45.0 0.0 copy-start.3
  45.0 0.9 copy-done.3
  45.9 1.0 make_block.1
  46.9 12.2 %all_to_all.25.got_ref = bf16[16,64,128]{2,1,0:T(8,128)(2,1)S(1)} all-to-all(bf16[16,64,128]{2,1,0:T(8,128)(2,1)S(1)} %get-tuple-element.32), channel_id=1, replica_groups=mesh['x'=4,'zl'=2,'core'=2,'zh'=4,'y'=4] {'x','zl','core'}, dimensions={0} | all-to-all | bytes 524288 | tf_op jit(solution)/shard_map/all_to_all | solution.py:316
  59.1 1.0 symmetrize.1
  60.1 0.0 collective-permute-done.2.fac3.refs_2_
  60.1 0.0 collective-permute-done.1.fac2.refs_3_
  60.1 5.5 %collective-permute-done.fac1.refs_1_ = bf16[4,128,512]{2,1,0:T(8,128)(2,1)S(1)} collective-permute-done((bf16[4,128,512]{2,1,0:T(8,128)(2,1)S(1)}, bf16[4,128,512]{2,1,0:T(8,128)(2,1)S(1)}, u32[]{:S(2)}, u32[]{:S(2)}) %collective-permute-start) | collective-permute-done | bytes 524320 | tf_op jit(solution)/shard_map/ppermute | solution.py:268
  65.6 0.0 copy-start.2
  65.6 0.0 copy-start.4
  65.6 18.8 %all_to_all.26.own_ref = bf16[8,64,1024]{2,1,0:T(8,128)(2,1)S(1)} all-to-all(bf16[8,64,1024]{2,1,0:T(8,128)(2,1)S(1)} %gate.1), channel_id=1, replica_groups=mesh['x'=4,'zl'=2,'core'=2,'zh'=4,'y'=4] {'x','zl'}, dimensions={0} | all-to-all | bytes 2097152 | tf_op jit(solution)/shard_map/all_to_all | solution.py:334
  84.4 1.9 %collective-permute-start.9 = (bf16[8,64,1024]{2,1,0:T(8,128)(2,1)S(1)}, bf16[8,64,1024]{2,1,0:T(8,128)(2,1)S(1)}, u32[]{:S(2)}, u32[]{:S(2)}) collective-permute-start(bf16[8,64,1024]{2,1,0:T(8,128)(2,1)S(1)} %all_to_all.26.own_ref), channel_id=1, source_target_pairs={{0,16},{16,0},{1,17},{17,1},{2,18},{18,2},{3,19},{19,3},{4,20},{20... | collective-permute-start | bytes 3145736 | tf_op jit(solution)/shard_map/ppermute | solution.py:272
  86.3 0.0 copy-done.2
  86.3 0.0 copy-done.4
  86.4 1.4 %prepare_factors.1 = (bf16[4,4,64,1024]{3,2,1,0:T(8,128)(2,1)S(1)}, bf16[8,2,64,1024]{3,2,1,0:T(8,128)(2,1)S(1)}) custom-call(bf16[4,128,512]{2,1,0:T(8,128)(2,1)S(1)} %bitcast.9, bf16[4,128,512]{2,1,0:T(8,128)(2,1)S(1)} %collective-permute-done.fac1.refs_1_, bf16[4,128,512]{2,1,0:T(8,128)(2,1)S(1)} %collective-permute-done.1.fac2.refs_3_, ...), custom_call_target="tpu_custom_call" | custom-call | tf_op jit(solution)/shard_map/prepare_factors/pallas_call | solution.py:336
  87.8 1.3 %ladder_own.1.part_ref = bf16[8,64,1024]{2,1,0:T(8,128)(2,1)S(1)} custom-call(bf16[8,64,1024]{2,1,0:T(8,128)(2,1)S(1)} %all_to_all.26.own_ref, bf16[4,4,64,1024]{3,2,1,0:T(8,128)(2,1)S(1)} %get-tuple-element.35.right_ref), custom_call_target="tpu_custom_call" | custom-call | tf_op jit(solution)/shard_map/ladder_own/pallas_call | solution.py:344
  89.1 0.0 collective-permute-done.9.other_ref
  89.1 2.4 %ladder.1 = (bf16[1024,1024]{1,0:T(8,128)(2,1)S(1)}, bf16[8,64,1024]{2,1,0:T(8,128)(2,1)S(1)}) custom-call(bf16[8,64,1024]{2,1,0:T(8,128)(2,1)S(1)} %collective-permute-done.9.other_ref, bf16[4,4,64,1024]{3,2,1,0:T(8,128)(2,1)S(1)} %get-tuple-element.35.right_ref, bf16[8,2,64,1024]{3,2,1,0:T(8,128)(2,1)S(1)} %get-tuple-element.23.left_ref, ...), custom_call_target="tpu_custom_call" | custom-call | tf_op jit(solution)/shard_map/ladder/pallas_call | solution.py:352
  91.5 0.1 collective-permute-start.10
  91.6 1.2 ladder_rest.1
  92.8 1.4 %collective-permute-done.10 = bf16[8,64,1024]{2,1,0:T(8,128)(2,1)S(1)} collective-permute-done((bf16[8,64,1024]{2,1,0:T(8,128)(2,1)S(1)}, bf16[8,64,1024]{2,1,0:T(8,128)(2,1)S(1)}, u32[]{:S(2)}, u32[]{:S(2)}) %collective-permute-start.10) | collective-permute-done | bytes 1048608 | tf_op jit(solution)/shard_map/ppermute | solution.py:272
  94.2 0.4 add_convert_fusion
  94.7 18.1 %all_to_all.27.part_ref = bf16[8,64,1024]{2,1,0:T(8,128)(2,1)S(1)} all-to-all(bf16[8,64,1024]{2,1,0:T(8,128)(2,1)S(1)} %add_convert_fusion), channel_id=1, replica_groups=mesh['x'=4,'zl'=2,'core'=2,'zh'=4,'y'=4] {'x','zl'}, dimensions={0} | all-to-all | bytes 2097152 | tf_op jit(solution)/shard_map/all_to_all | solution.py:370
  112.8 0.4 sum_parts.1
  113.2 12.5 %all_to_all.28.resid_ref = bf16[16,32,128]{2,1,0:T(8,128)(2,1)} all-to-all(bf16[16,32,128]{2,1,0:T(8,128)(2,1)S(1)} %sum_parts.1), channel_id=1, replica_groups=mesh['x'=4,'zl'=2,'core'=2,'zh'=4,'y'=4] {'zh','y'}, dimensions={0} | all-to-all | bytes 262144 | tf_op jit(solution)/shard_map/all_to_all | solution.py:379
  125.7 2.1 %update.1 = bf16[16,4096]{1,0:T(8,128)(2,1)} custom-call(f32[4]{0:T(128)} %occ_ref.1, bf16[16,32,128]{2,1,0:T(8,128)(2,1)} %all_to_all.28.resid_ref, bf16[16,64,128]{2,1,0:T(8,128)(2,1)} %get-tuple-element.39.held_ref, f32[16,128]{1,0:T(8,128)} %get-tuple-element.40.mask_ref, f32[8,128]{1,0:T(8,128)} %bitcast.13), custom_call_target="tpu_custom_call" | custom-call | tf_op jit(solution)/shard_map/update/pallas_call | solution.py:380
  (1 shorter events, 0.0 us)
Async XLA Ops:
  0.0 45.0 %copy-start.1 = (bf16[3,64,64]{2,1,0:T(8,128)(2,1)S(1)}, bf16[3,64,64]{2,1,0:T(8,128)(2,1)}, u32[]{:S(2)}) copy-start(bf16[3,64,64]{2,1,0:T(8,128)(2,1)} %constant.8.clone.small_ref) | copy-start | bytes 73732
  0.0 45.0 %copy-start = (bf16[1024,1024]{1,0:T(8,128)(2,1)S(1)}, bf16[1024,1024]{1,0:T(8,128)(2,1)}, u32[]{:S(2)}) copy-start(bf16[1024,1024]{1,0:T(8,128)(2,1)} %constant.9.clone.wide_ref) | copy-start | bytes 6291460
  1.9 35.5 %all-to-all-start = ((bf16[64,8,512]{2,1,0:T(8,128)(2,1)}), bf16[64,8,512]{2,1,0:T(8,128)(2,1)S(1)}, u32[]{:S(2)}, u32[]{:S(2)}) async-start(bf16[64,8,512]{2,1,0:T(8,128)(2,1)} %spread_factors.1), calls=%async_computation | async-start | bytes 1048576 | tf_op jit(solution)/shard_map/all_to_all | solution.py:286
  17.2 5.5 %collective-permute-start.3 = (bf16[4,96,128]{2,1,0:T(8,128)(2,1)}, bf16[4,96,128]{2,1,0:T(8,128)(2,1)S(1)}, u32[]{:S(2)}, u32[]{:S(2)}) collective-permute-start(bf16[4,96,128]{2,1,0:T(8,128)(2,1)} %get-tuple-element.25), channel_id=1, source_target_pairs={{0,1},{1,2},{2,3},{3,0},{4,5},{5,6},{6,7},{7,4},{8,9},{9,10},{10,1... | collective-permute-start | bytes 294920 | tf_op jit(solution)/shard_map/ppermute | solution.py:268
  18.5 7.4 %collective-permute-start.4 = (bf16[4,96,128]{2,1,0:T(8,128)(2,1)}, bf16[4,96,128]{2,1,0:T(8,128)(2,1)S(1)}, u32[]{:S(2)}, u32[]{:S(2)}) collective-permute-start(bf16[4,96,128]{2,1,0:T(8,128)(2,1)} %get-tuple-element.26), channel_id=1, source_target_pairs={{0,2},{1,3},{2,0},{3,1},{4,6},{5,7},{6,4},{7,5},{8,10},{9,11},{10,... | collective-permute-start | bytes 294920 | tf_op jit(solution)/shard_map/ppermute | solution.py:268
  21.1 4.8 %collective-permute-start.5 = (bf16[4,96,128]{2,1,0:T(8,128)(2,1)}, bf16[4,96,128]{2,1,0:T(8,128)(2,1)S(1)}, u32[]{:S(2)}, u32[]{:S(2)}) collective-permute-start(bf16[4,96,128]{2,1,0:T(8,128)(2,1)} %get-tuple-element.27), channel_id=1, source_target_pairs={{0,3},{1,0},{2,1},{3,2},{4,7},{5,4},{6,5},{7,6},{8,11},{9,8},{10,9... | collective-permute-start | bytes 294920 | tf_op jit(solution)/shard_map/ppermute | solution.py:268
  22.7 3.2 %copy-start.5 = (bf16[4,96,128]{2,1,0:T(8,128)(2,1)}, bf16[4,96,128]{2,1,0:T(8,128)(2,1)S(1)}, u32[]{:S(2)}) copy-start(bf16[4,96,128]{2,1,0:T(8,128)(2,1)S(1)} %collective-permute-done.3.in1) | copy-start | bytes 294916
  25.9 0.6 copy-start.6
  25.9 0.7 copy-start.7
  28.4 11.1 %collective-permute-start.6 = (bf16[4,96,128]{2,1,0:T(8,128)(2,1)}, bf16[4,96,128]{2,1,0:T(8,128)(2,1)S(1)}, u32[]{:S(2)}, u32[]{:S(2)}) collective-permute-start(bf16[4,96,128]{2,1,0:T(8,128)(2,1)} %get-tuple-element.29), channel_id=1, source_target_pairs={{0,4},{4,8},{8,12},{12,0},{1,5},{5,9},{9,13},{13,1},{2,6},{6,10},{... | collective-permute-start | bytes 294920 | tf_op jit(solution)/shard_map/ppermute | solution.py:268
  30.8 11.0 %collective-permute-start.7 = (bf16[4,96,128]{2,1,0:T(8,128)(2,1)}, bf16[4,96,128]{2,1,0:T(8,128)(2,1)S(1)}, u32[]{:S(2)}, u32[]{:S(2)}) collective-permute-start(bf16[4,96,128]{2,1,0:T(8,128)(2,1)} %get-tuple-element.30), channel_id=1, source_target_pairs={{0,8},{4,12},{8,0},{12,4},{1,9},{5,13},{9,1},{13,5},{2,10},{6,14},... | collective-permute-start | bytes 294920 | tf_op jit(solution)/shard_map/ppermute | solution.py:268
  34.3 10.7 %collective-permute-start.8 = (bf16[4,96,128]{2,1,0:T(8,128)(2,1)}, bf16[4,96,128]{2,1,0:T(8,128)(2,1)S(1)}, u32[]{:S(2)}, u32[]{:S(2)}) collective-permute-start(bf16[4,96,128]{2,1,0:T(8,128)(2,1)} %get-tuple-element.31), channel_id=1, source_target_pairs={{0,12},{4,0},{8,4},{12,8},{1,13},{5,1},{9,5},{13,9},{2,14},{6,2},{... | collective-permute-start | bytes 294920 | tf_op jit(solution)/shard_map/ppermute | solution.py:268
  37.5 22.6 %collective-permute-start.2 = (bf16[4,128,512]{2,1,0:T(8,128)(2,1)S(1)}, bf16[4,128,512]{2,1,0:T(8,128)(2,1)S(1)}, u32[]{:S(2)}, u32[]{:S(2)}) collective-permute-start(bf16[4,128,512]{2,1,0:T(8,128)(2,1)S(1)} %bitcast.6), channel_id=1, source_target_pairs={{0,3},{1,0},{2,1},{3,2},{4,7},{5,4},{6,5},{7,6},{8,11},{9,8},{10,9... | collective-permute-start | bytes 1572872 | tf_op jit(solution)/shard_map/ppermute | solution.py:268
  39.0 21.1 %collective-permute-start.1 = (bf16[4,128,512]{2,1,0:T(8,128)(2,1)S(1)}, bf16[4,128,512]{2,1,0:T(8,128)(2,1)S(1)}, u32[]{:S(2)}, u32[]{:S(2)}) collective-permute-start(bf16[4,128,512]{2,1,0:T(8,128)(2,1)S(1)} %bitcast.7), channel_id=1, source_target_pairs={{0,2},{1,3},{2,0},{3,1},{4,6},{5,7},{6,4},{7,5},{8,10},{9,11},{10,... | collective-permute-start | bytes 1572872 | tf_op jit(solution)/shard_map/ppermute | solution.py:268
  39.5 26.1 %collective-permute-start = (bf16[4,128,512]{2,1,0:T(8,128)(2,1)S(1)}, bf16[4,128,512]{2,1,0:T(8,128)(2,1)S(1)}, u32[]{:S(2)}, u32[]{:S(2)}) collective-permute-start(bf16[4,128,512]{2,1,0:T(8,128)(2,1)S(1)} %bitcast.8), channel_id=1, source_target_pairs={{0,1},{1,2},{2,3},{3,0},{4,5},{5,6},{6,7},{7,4},{8,9},{9,10},{10,1... | collective-permute-start | bytes 1572872 | tf_op jit(solution)/shard_map/ppermute | solution.py:268
  45.0 0.9 copy-start.3
  65.6 20.7 %copy-start.2 = (bf16[256,256]{1,0:T(8,128)(2,1)S(1)}, bf16[256,256]{1,0:T(8,128)(2,1)}, u32[]{:S(2)}) copy-start(bf16[256,256]{1,0:T(8,128)(2,1)} %constant.11.clone.rows_ref) | copy-start | bytes 393220
  65.6 20.7 %copy-start.4 = (bf16[128,128]{1,0:T(8,128)(2,1)S(1)}, bf16[128,128]{1,0:T(8,128)(2,1)}, u32[]{:S(2)}) copy-start(bf16[128,128]{1,0:T(8,128)(2,1)} %constant.10.clone.halves_ref) | copy-start | bytes 98308
  84.4 4.7 %collective-permute-start.9 = (bf16[8,64,1024]{2,1,0:T(8,128)(2,1)S(1)}, bf16[8,64,1024]{2,1,0:T(8,128)(2,1)S(1)}, u32[]{:S(2)}, u32[]{:S(2)}) collective-permute-start(bf16[8,64,1024]{2,1,0:T(8,128)(2,1)S(1)} %all_to_all.26.own_ref), channel_id=1, source_target_pairs={{0,16},{16,0},{1,17},{17,1},{2,18},{18,2},{3,19},{19,3},{4,20},{20... | collective-permute-start | bytes 3145736 | tf_op jit(solution)/shard_map/ppermute | solution.py:272
  91.5 2.7 %collective-permute-start.10 = (bf16[8,64,1024]{2,1,0:T(8,128)(2,1)S(1)}, bf16[8,64,1024]{2,1,0:T(8,128)(2,1)S(1)}, u32[]{:S(2)}, u32[]{:S(2)}) collective-permute-start(bf16[8,64,1024]{2,1,0:T(8,128)(2,1)S(1)} %get-tuple-element.37), channel_id=1, source_target_pairs={{0,16},{16,0},{1,17},{17,1},{2,18},{18,2},{3,19},{19,3},{4,20},{20... | collective-permute-start | bytes 3145736 | tf_op jit(solution)/shard_map/ppermute | solution.py:272

commit v9 on v8

--- a/solution.py
+++ b/solution.py
@@ -72,12 +72,35 @@
         copy.wait()
 
 
+def _virtuals(vir_ref):
+    row = _chip() * 2 + lax.axis_index("core")
+    col = lax.axis_index("zh") * 4 + lax.axis_index("y")
+    exact = lax.Precision.HIGHEST
+
+    def iota(shape, dim):
+        return lax.broadcasted_iota(jnp.int32, shape, dim)
+
+    mine = vir_ref[pl.ds(row // 2, 1), :]
+    l_row = iota((32, 128), 1) - (row % 2) * 64
+    in_row = (l_row // 2 == iota((32, 128), 0)) & (l_row >= 0)
+    picked = jnp.where(in_row, jnp.broadcast_to(mine, (32, 128)), 0.0)
+    same_half = (iota((128, 128), 0) % 2 == iota((128, 128), 1) // 64).astype(F32)
+    vir_a = jnp.dot(picked, same_half, precision=exact, preferred_element_type=F32)
+    lane = iota((128, 128), 1)
+    want = ((lane // 4) % 2) * 64 + col * 4 + lane % 4
+    choose = (iota((128, 128), 0) == want).astype(F32)
+    by_block = jnp.dot(vir_ref[...], choose, precision=exact, preferred_element_type=F32)
+    own_block = iota((8, 128), 0) == (iota((8, 128), 1) % 64) // 8
+    vir_b = jnp.sum(jnp.where(own_block, by_block, 0.0), axis=0, keepdims=True)
+    return vir_a + vir_b
+
+
 def _mask_kernel(
     amps_ref,
     source_ref,
-    screen_ref,
+    screen_ref, vir_ref,
     held_ref,
-    mask_ref,
+    mask_ref, table_ref,
     out0,
     out1,
     out2,
@@ -85,6 +108,7 @@
     flat_ref,
     flat2_ref,
 ):
+    table_ref[...] = _virtuals(vir_ref)
     block = screen_ref[_chip()].astype(F32)
     lane_block = (lax.broadcasted_iota(jnp.int32, (8, 128), 1) % 64) // 8
     spread = (lax.broadcasted_iota(jnp.int32, (8, 128), 0) == lane_block).astype(F32)
@@ -165,14 +189,14 @@
                 left_ref[x * 2 + zl, core] = part[at : at + 64]
 
 
-def _second_step(left_ref, core, inner_ref, out_ref):
-    for x in range(2):
+def _second_step(left_ref, core, inner_ref, out_ref, halves):
+    for at, x in enumerate(halves):
         rows = jnp.concatenate([left_ref[x * 4 + chip, core] for chip in range(4)], axis=0)
         for j in range(4):
             cols = slice(j * 256, j * 256 + 256)
             part = _perm(rows, inner_ref[:, cols])
             for chip in range(4):
-                out_ref[x * 4 + chip, :, cols] = part[chip * 64 : chip * 64 + 64]
+                out_ref[at * 4 + chip, :, cols] = part[chip * 64 : chip * 64 + 64]
 
 
 def _first_step(amp_ref, right_ref, put):
@@ -202,11 +226,15 @@
             inner_ref[at + 64 : at + 128, cols] = jnp.where(first, other, own)
 
     _first_step(other_ref, right_ref, put)
-    _second_step(left_ref, 1 - core, inner_ref, give_ref)
+    _second_step(left_ref, 1 - core, inner_ref, give_ref, (0,))
+
+
+def _more_kernel(left_ref, inner_ref, give_ref):
+    _second_step(left_ref, 1 - lax.axis_index("core"), inner_ref, give_ref, (1,))
 
 
 def _rest_kernel(left_ref, inner_ref, keep_ref):
-    _second_step(left_ref, lax.axis_index("core"), inner_ref, keep_ref)
+    _second_step(left_ref, lax.axis_index("core"), inner_ref, keep_ref, (0, 1))
 
 
 def _sum_kernel(part_ref, kept_ref, small_ref, sent_ref):
@@ -219,29 +247,9 @@
 
 
 def _update_kernel(occ_ref, resid_ref, held_ref, mask_ref, vir_ref, out_ref, flat_ref):
-    row = _chip() * 2 + lax.axis_index("core")
-    col = lax.axis_index("zh") * 4 + lax.axis_index("y")
-    exact = lax.Precision.HIGHEST
-
-    def iota(shape, dim):
-        return lax.broadcasted_iota(jnp.int32, shape, dim)
-
-    mine = vir_ref[pl.ds(row // 2, 1), :]
-    l_row = iota((32, 128), 1) - (row % 2) * 64
-    in_row = (l_row // 2 == iota((32, 128), 0)) & (l_row >= 0)
-    picked = jnp.where(in_row, jnp.broadcast_to(mine, (32, 128)), 0.0)
-    same_half = (iota((128, 128), 0) % 2 == iota((128, 128), 1) // 64).astype(F32)
-    vir_a = jnp.dot(picked, same_half, precision=exact, preferred_element_type=F32)
-    lane = iota((128, 128), 1)
-    want = ((lane // 4) % 2) * 64 + col * 4 + lane % 4
-    choose = (iota((128, 128), 0) == want).astype(F32)
-    by_block = jnp.dot(vir_ref[...], choose, precision=exact, preferred_element_type=F32)
-    own_block = iota((8, 128), 0) == (iota((8, 128), 1) % 64) // 8
-    vir_b = jnp.sum(jnp.where(own_block, by_block, 0.0), axis=0, keepdims=True)
-    vir = vir_a + vir_b
     for pair in range(16):
         i, j = pair // 4, pair % 4
-        denom = (occ_ref[i] + occ_ref[j]) - vir
+        denom = (occ_ref[i] + occ_ref[j]) - vir_ref[...]
         rsym = resid_ref[pair].astype(F32) + held_ref[pair, 32:].astype(F32)
         old = held_ref[pair, :32].astype(F32)
         flat_ref[pair * 32 : pair * 32 + 32, :] = old + mask_ref[pair : pair + 1, :] * (rsym / denom)
@@ -285,14 +293,14 @@
     )(factors)
     fac = lax.all_to_all(spread, ("zh",) + ROWS, 0, 0, tiled=True).reshape(4, 128, 512)
     four = _sds(4, 96, 128)
-    held, mask, *outs = pl.pallas_call(
+    held, mask, table, *outs = pl.pallas_call(
         _mask_kernel,
-        out_shape=(_sds(16, 64, 128), _sds(16, 128, dtype=F32)) + (four,) * 4,
-        in_specs=[_vmem()] * 3,
-        out_specs=(_vmem(),) * 6,
+        out_shape=(_sds(16, 64, 128), _sds(16, 128, dtype=F32), _sds(32, 128, dtype=F32)) + (four,) * 4,
+        in_specs=[_vmem()] * 4,
+        out_specs=(_vmem(),) * 7,
         scratch_shapes=[pltpu.VMEM((544, 128), F32)] * 2,
         name="mask_amps",
-    )(amps.reshape(16, 4096), source.reshape(16, 4096), screen.transpose(1, 2, 0))
+    )(amps.reshape(16, 4096), source.reshape(16, 4096), screen.transpose(1, 2, 0), vir_energy.reshape(8, 128))
     outs = [_turn(out, "y", k) for k, out in enumerate(outs)]
     outs = pl.pallas_call(
         _relay_kernel,
@@ -351,12 +359,20 @@
     )(own, right)
     inner, give = pl.pallas_call(
         _ladder_kernel,
-        out_shape=(_sds(1024, 1024), _sds(8, 64, 1024)),
+        out_shape=(_sds(1024, 1024), _sds(4, 64, 1024)),
         in_specs=[_vmem()] * 4,
         out_specs=(_vmem(), _vmem()),
         compiler_params=VMEM,
         name="ladder",
     )(other, right, left, part)
+    more = pl.pallas_call(
+        _more_kernel,
+        out_shape=_sds(4, 64, 1024),
+        in_specs=[_vmem()] * 2,
+        out_specs=_vmem(),
+        compiler_params=VMEM,
+        name="ladder_more",
+    )(left, inner)
     keep = pl.pallas_call(
         _rest_kernel,
         out_shape=_sds(8, 64, 1024),
@@ -365,7 +381,7 @@
         compiler_params=VMEM,
         name="ladder_rest",
     )(left, inner)
-    taken = _swap_cores(give)
+    taken = jnp.concatenate([_swap_cores(give), _swap_cores(more)], axis=0)
     partial = (keep.astype(F32) + taken.astype(F32)).astype(BF16)
     parts = lax.all_to_all(partial, CHIPS, 0, 0, tiled=True)
     last = pl.pallas_call(
@@ -384,7 +400,7 @@
         out_specs=_vmem(),
         scratch_shapes=[pltpu.VMEM((544, 128), F32)],
         name="update",
-    )(occ_energy, back, held, mask, vir_energy.reshape(8, 128))
+    )(occ_energy, back, held, mask, table)
     return out.reshape(1, 1, 16, 4096)
 
 

time: 128 us -> 128 us (level)
    pallas_call x1 -> x2, Pallas kernels: 2.41 us -> 2.57 us  [the longest x1 1.86 us: _shards(): pl.pallas_call(_ladder_kernel, out_shape=(_sds(1024, 1024), _sds(4, 64, 1...]
  transfers between devices with their start and end apart: 12 -> 13, of which waited for: 6 -> 7; matrix products, arithmetic and copies ran while one was open for 0% -> 0% of each run, Pallas kernels for 8% -> 8%
where the time goes in v9:
time: 128 us
  blocking collectives  61.6 us (48%)
  starting transfers between devices  32.4 us (25%)
  Pallas kernels  16.9 us (13%)
  waiting for transfers between devices  14.8 us (12%)
  local copies, waits for them, and re-layouts  1.57 us (1%)
    all_to_all x1, blocking collectives, _shards(): own = lax.all_to_all(block, CHIPS, 0, 0, tiled=True)  18.8 us
    all_to_all x1, blocking collectives, _shards(): parts = lax.all_to_all(partial, CHIPS, 0, 0, tiled=True)  18.1 us
    ppermute x9, starting transfers between devices, _turn(): return lax.ppermute(value, axis, [(i, (i + step) % 4) for i in range(4)])  16.9 us
    ppermute x9, waiting for transfers between devices, _turn(): return lax.ppermute(value, axis, [(i, (i + step) % 4) for i in range(4)])  13.9 us
    all_to_all x1, starting transfers between devices, _shards(): lax.all_to_all(spread, ('zh',) + ROWS, 0, 0, tiled=True)  13 us
    all_to_all x1, blocking collectives, _shards(): back = lax.all_to_all(last, COLS, 0, 0, tiled=True)  12.5 us
    all_to_all x1, blocking collectives, _shards(): turn = lax.all_to_all(turn, ROWS, 0, 0, tiled=True)  12.2 us
  transfers between devices with their start and end apart: 13, of which 7 were waited for; matrix products, arithmetic and copies ran while one was open for 0% of the time, Pallas kernels for 8%

profile of v9, /device:TPU:1, one launch (start us, length us, event | category | flops | bytes accessed | tf_op | source)
XLA Modules:
  0.0 127.8 jit_solution(1701349028871351429)
XLA Ops:
  0.0 0.0 copy-start.1
  0.0 0.0 copy-start
  0.0 1.9 %spread_factors.1 = bf16[64,8,512]{2,1,0:T(8,128)(2,1)} custom-call(bf16[16,4,1024]{2,1,0:T(4,128)(2,1)} %fac_ref.1), custom_call_target="tpu_custom_call" | custom-call | tf_op jit(solution)/shard_map/spread_factors/pallas_call | solution.py:285
  2.0 13.0 %all-to-all-start = ((bf16[64,8,512]{2,1,0:T(8,128)(2,1)}), bf16[64,8,512]{2,1,0:T(8,128)(2,1)S(1)}, u32[]{:S(2)}, u32[]{:S(2)}) async-start(bf16[64,8,512]{2,1,0:T(8,128)(2,1)} %spread_factors.1), calls=%async_computation | async-start | bytes 1048576 | tf_op jit(solution)/shard_map/all_to_all | solution.py:294
  15.0 2.3 %mask_amps.1 = (bf16[16,64,128]{2,1,0:T(8,128)(2,1)}, f32[16,128]{1,0:T(8,128)}, f32[32,128]{1,0:T(8,128)}, bf16[4,96,128]{2,1,0:T(8,128)(2,1)}, bf16[4,96,128]{...) custom-call(bf16[16,4096]{1,0:T(8,128)(2,1)} %bitcast.10, bf16[16,4096]{1,0:T(8,128)(2,1)} %bitcast.11, ...), custom_call_target="tpu_custom_call" | custom-call | tf_op jit(solution)/shard_map/mask_amps/pallas_call | solution.py:296
  17.3 1.3 %collective-permute-start.3 = (bf16[4,96,128]{2,1,0:T(8,128)(2,1)}, bf16[4,96,128]{2,1,0:T(8,128)(2,1)S(1)}, u32[]{:S(2)}, u32[]{:S(2)}) collective-permute-start(bf16[4,96,128]{2,1,0:T(8,128)(2,1)} %get-tuple-element.26), channel_id=1, source_target_pairs={{0,1},{1,2},{2,3},{3,0},{4,5},{5,6},{6,7},{7,4},{8,9},{9,10},{10,1... | collective-permute-start | bytes 294920 | tf_op jit(solution)/shard_map/ppermute | solution.py:276
  18.6 2.6 %collective-permute-start.4 = (bf16[4,96,128]{2,1,0:T(8,128)(2,1)}, bf16[4,96,128]{2,1,0:T(8,128)(2,1)S(1)}, u32[]{:S(2)}, u32[]{:S(2)}) collective-permute-start(bf16[4,96,128]{2,1,0:T(8,128)(2,1)} %get-tuple-element.27), channel_id=1, source_target_pairs={{0,2},{1,3},{2,0},{3,1},{4,6},{5,7},{6,4},{7,5},{8,10},{9,11},{10,... | collective-permute-start | bytes 294920 | tf_op jit(solution)/shard_map/ppermute | solution.py:276
  21.2 1.1 collective-permute-start.5
  22.3 0.5 collective-permute-done.3.in1
  22.8 0.0 copy-start.5
  22.8 3.2 %collective-permute-done.4.in2 = bf16[4,96,128]{2,1,0:T(8,128)(2,1)S(1)} collective-permute-done((bf16[4,96,128]{2,1,0:T(8,128)(2,1)}, bf16[4,96,128]{2,1,0:T(8,128)(2,1)S(1)}, u32[]{:S(2)}, u32[]{:S(2)}) %collective-permute-start.4) | collective-permute-done | bytes 98336 | tf_op jit(solution)/shard_map/ppermute | solution.py:276
  26.0 0.0 copy-start.6
  26.0 0.0 collective-permute-done.5.in3
  26.0 0.0 copy-start.7
  26.0 0.0 copy-done.5
  26.0 0.6 copy-done.6
  26.6 0.0 copy-done.7
  26.7 1.8 %relay.1 = (bf16[4,96,128]{2,1,0:T(8,128)(2,1)}, bf16[4,96,128]{2,1,0:T(8,128)(2,1)}, bf16[4,96,128]{2,1,0:T(8,128)(2,1)}, bf16[4,96,128]{2,1,0:T(8,128)(2,1)}) custom-call(bf16[4,96,128]{2,1,0:T(8,128)(2,1)} %get-tuple-element.25.in0, bf16[4,96,128]{2,1,0:T(8,128)(2,1)} %copy-done.5, bf16[4,96,128]{2,1,0:T(8,128)(2,1)} %copy-done.6, ...), custom_call_target="tpu_custom_call" | custom-call | tf_op jit(solution)/shard_map/relay/pallas_call | solution.py:305
  28.5 2.4 %collective-permute-start.6 = (bf16[4,96,128]{2,1,0:T(8,128)(2,1)}, bf16[4,96,128]{2,1,0:T(8,128)(2,1)S(1)}, u32[]{:S(2)}, u32[]{:S(2)}) collective-permute-start(bf16[4,96,128]{2,1,0:T(8,128)(2,1)} %get-tuple-element.30), channel_id=1, source_target_pairs={{0,4},{4,8},{8,12},{12,0},{1,5},{5,9},{9,13},{13,1},{2,6},{6,10},{... | collective-permute-start | bytes 294920 | tf_op jit(solution)/shard_map/ppermute | solution.py:276
  30.9 3.5 %collective-permute-start.7 = (bf16[4,96,128]{2,1,0:T(8,128)(2,1)}, bf16[4,96,128]{2,1,0:T(8,128)(2,1)S(1)}, u32[]{:S(2)}, u32[]{:S(2)}) collective-permute-start(bf16[4,96,128]{2,1,0:T(8,128)(2,1)} %get-tuple-element.31), channel_id=1, source_target_pairs={{0,8},{4,12},{8,0},{12,4},{1,9},{5,13},{9,1},{13,5},{2,10},{6,14},... | collective-permute-start | bytes 294920 | tf_op jit(solution)/shard_map/ppermute | solution.py:276
  34.4 3.2 %collective-permute-start.8 = (bf16[4,96,128]{2,1,0:T(8,128)(2,1)}, bf16[4,96,128]{2,1,0:T(8,128)(2,1)S(1)}, u32[]{:S(2)}, u32[]{:S(2)}) collective-permute-start(bf16[4,96,128]{2,1,0:T(8,128)(2,1)} %get-tuple-element.32), channel_id=1, source_target_pairs={{0,12},{4,0},{8,4},{12,8},{1,13},{5,1},{9,5},{13,9},{2,14},{6,2},{... | collective-permute-start | bytes 294920 | tf_op jit(solution)/shard_map/ppermute | solution.py:276
  37.6 0.0 all-to-all-done
  37.6 1.5 %collective-permute-start.2 = (bf16[4,128,512]{2,1,0:T(8,128)(2,1)S(1)}, bf16[4,128,512]{2,1,0:T(8,128)(2,1)S(1)}, u32[]{:S(2)}, u32[]{:S(2)}) collective-permute-start(bf16[4,128,512]{2,1,0:T(8,128)(2,1)S(1)} %bitcast.6), channel_id=1, source_target_pairs={{0,3},{1,0},{2,1},{3,2},{4,7},{5,4},{6,5},{7,6},{8,11},{9,8},{10,9... | collective-permute-start | bytes 1572872 | tf_op jit(solution)/shard_map/ppermute | solution.py:276
  39.1 0.5 collective-permute-start.1
  39.6 0.0 collective-permute-done.6.in1
  39.6 0.8 collective-permute-start
  40.4 1.5 %collective-permute-done.7.in2 = bf16[4,96,128]{2,1,0:T(8,128)(2,1)S(1)} collective-permute-done((bf16[4,96,128]{2,1,0:T(8,128)(2,1)}, bf16[4,96,128]{2,1,0:T(8,128)(2,1)S(1)}, u32[]{:S(2)}, u32[]{:S(2)}) %collective-permute-start.7) | collective-permute-done | bytes 98336 | tf_op jit(solution)/shard_map/ppermute | solution.py:276
  41.9 3.1 %collective-permute-done.8.in3 = bf16[4,96,128]{2,1,0:T(8,128)(2,1)S(1)} collective-permute-done((bf16[4,96,128]{2,1,0:T(8,128)(2,1)}, bf16[4,96,128]{2,1,0:T(8,128)(2,1)S(1)}, u32[]{:S(2)}, u32[]{:S(2)}) %collective-permute-start.8) | collective-permute-done | bytes 98336 | tf_op jit(solution)/shard_map/ppermute | solution.py:276
  45.0 0.0 copy-done.1
  45.0 0.0 copy-done
  45.0 0.0 copy-start.3
  45.1 0.9 copy-done.3
  45.9 1.0 make_block.1
  46.9 12.2 %all_to_all.25.got_ref = bf16[16,64,128]{2,1,0:T(8,128)(2,1)S(1)} all-to-all(bf16[16,64,128]{2,1,0:T(8,128)(2,1)S(1)} %get-tuple-element.33), channel_id=1, replica_groups=mesh['x'=4,'zl'=2,'core'=2,'zh'=4,'y'=4] {'x','zl','core'}, dimensions={0} | all-to-all | bytes 524288 | tf_op jit(solution)/shard_map/all_to_all | solution.py:324
  59.1 1.0 symmetrize.1
  60.2 0.0 collective-permute-done.2.fac3.refs_2_
  60.2 0.0 collective-permute-done.1.fac2.refs_3_
  60.2 5.5 %collective-permute-done.fac1.refs_1_ = bf16[4,128,512]{2,1,0:T(8,128)(2,1)S(1)} collective-permute-done((bf16[4,128,512]{2,1,0:T(8,128)(2,1)S(1)}, bf16[4,128,512]{2,1,0:T(8,128)(2,1)S(1)}, u32[]{:S(2)}, u32[]{:S(2)}) %collective-permute-start) | collective-permute-done | bytes 524320 | tf_op jit(solution)/shard_map/ppermute | solution.py:276
  65.7 0.0 copy-start.2
  65.7 0.0 copy-start.4
  65.7 18.8 %all_to_all.26.own_ref = bf16[8,64,1024]{2,1,0:T(8,128)(2,1)S(1)} all-to-all(bf16[8,64,1024]{2,1,0:T(8,128)(2,1)S(1)} %gate.1), channel_id=1, replica_groups=mesh['x'=4,'zl'=2,'core'=2,'zh'=4,'y'=4] {'x','zl'}, dimensions={0} | all-to-all | bytes 2097152 | tf_op jit(solution)/shard_map/all_to_all | solution.py:342
  84.5 1.9 %collective-permute-start.9 = (bf16[8,64,1024]{2,1,0:T(8,128)(2,1)S(1)}, bf16[8,64,1024]{2,1,0:T(8,128)(2,1)S(1)}, u32[]{:S(2)}, u32[]{:S(2)}) collective-permute-start(bf16[8,64,1024]{2,1,0:T(8,128)(2,1)S(1)} %all_to_all.26.own_ref), channel_id=1, source_target_pairs={{0,16},{16,0},{1,17},{17,1},{2,18},{18,2},{3,19},{19,3},{4,20},{20... | collective-permute-start | bytes 3145736 | tf_op jit(solution)/shard_map/ppermute | solution.py:280
  86.4 0.0 copy-done.2
  86.4 0.0 copy-done.4
  86.4 1.4 %prepare_factors.1 = (bf16[4,4,64,1024]{3,2,1,0:T(8,128)(2,1)S(1)}, bf16[8,2,64,1024]{3,2,1,0:T(8,128)(2,1)S(1)}) custom-call(bf16[4,128,512]{2,1,0:T(8,128)(2,1)S(1)} %bitcast.9, bf16[4,128,512]{2,1,0:T(8,128)(2,1)S(1)} %collective-permute-done.fac1.refs_1_, bf16[4,128,512]{2,1,0:T(8,128)(2,1)S(1)} %collective-permute-done.1.fac2.refs_3_, ...), custom_call_target="tpu_custom_call" | custom-call | tf_op jit(solution)/shard_map/prepare_factors/pallas_call | solution.py:344
  87.8 1.3 %ladder_own.1.part_ref = bf16[8,64,1024]{2,1,0:T(8,128)(2,1)S(1)} custom-call(bf16[8,64,1024]{2,1,0:T(8,128)(2,1)S(1)} %all_to_all.26.own_ref, bf16[4,4,64,1024]{3,2,1,0:T(8,128)(2,1)S(1)} %get-tuple-element.36.right_ref), custom_call_target="tpu_custom_call" | custom-call | tf_op jit(solution)/shard_map/ladder_own/pallas_call | solution.py:352
  89.1 0.0 collective-permute-done.9.other_ref
  89.1 1.9 %ladder.1 = (bf16[1024,1024]{1,0:T(8,128)(2,1)S(1)}, bf16[4,64,1024]{2,1,0:T(8,128)(2,1)S(1)}) custom-call(bf16[8,64,1024]{2,1,0:T(8,128)(2,1)S(1)} %collective-permute-done.9.other_ref, bf16[4,4,64,1024]{3,2,1,0:T(8,128)(2,1)S(1)} %get-tuple-element.36.right_ref, bf16[8,2,64,1024]{3,2,1,0:T(8,128)(2,1)S(1)} %get-tuple-element.24.left_ref, ...), custom_call_target="tpu_custom_call" | custom-call | tf_op jit(solution)/shard_map/ladder/pallas_call | solution.py:360
  91.0 0.7 ladder_more.1
  91.7 0.1 collective-permute-start.11
  91.8 0.5 collective-permute-start.10
  92.3 1.2 ladder_rest.1
  93.6 0.1 collective-permute-done.11
  93.7 0.7 collective-permute-done.10
  94.5 0.4 add_convert_fusion
  94.9 18.1 %all_to_all.27.part_ref = bf16[8,64,1024]{2,1,0:T(8,128)(2,1)S(1)} all-to-all(bf16[8,64,1024]{2,1,0:T(8,128)(2,1)S(1)} %add_convert_fusion), channel_id=1, replica_groups=mesh['x'=4,'zl'=2,'core'=2,'zh'=4,'y'=4] {'x','zl'}, dimensions={0} | all-to-all | bytes 2097152 | tf_op jit(solution)/shard_map/all_to_all | solution.py:386
  113.0 0.4 sum_parts.1
  113.4 12.5 %all_to_all.28.resid_ref = bf16[16,32,128]{2,1,0:T(8,128)(2,1)} all-to-all(bf16[16,32,128]{2,1,0:T(8,128)(2,1)S(1)} %sum_parts.1), channel_id=1, replica_groups=mesh['x'=4,'zl'=2,'core'=2,'zh'=4,'y'=4] {'zh','y'}, dimensions={0} | all-to-all | bytes 262144 | tf_op jit(solution)/shard_map/all_to_all | solution.py:395
  125.9 1.9 %update.1 = bf16[16,4096]{1,0:T(8,128)(2,1)} custom-call(f32[4]{0:T(128)} %occ_ref.1, bf16[16,32,128]{2,1,0:T(8,128)(2,1)} %all_to_all.28.resid_ref, bf16[16,64,128]{2,1,0:T(8,128)(2,1)} %get-tuple-element.40.held_ref, f32[16,128]{1,0:T(8,128)} %get-tuple-element.41.mask_ref, f32[32,128]{1,0:T(8,128)} %get-tuple-element.42.vir_ref), custom_call_target="tpu_custom_call" | custom-call | tf_op jit(solution)/shard_map/update/pallas_call | solution.py:396
  (1 shorter events, 0.0 us)
Async XLA Ops:
  0.0 45.0 %copy-start.1 = (bf16[3,64,64]{2,1,0:T(8,128)(2,1)S(1)}, bf16[3,64,64]{2,1,0:T(8,128)(2,1)}, u32[]{:S(2)}) copy-start(bf16[3,64,64]{2,1,0:T(8,128)(2,1)} %constant.8.clone.small_ref) | copy-start | bytes 73732
  0.0 45.0 %copy-start = (bf16[1024,1024]{1,0:T(8,128)(2,1)S(1)}, bf16[1024,1024]{1,0:T(8,128)(2,1)}, u32[]{:S(2)}) copy-start(bf16[1024,1024]{1,0:T(8,128)(2,1)} %constant.9.clone.wide_ref) | copy-start | bytes 6291460
  2.0 35.6 %all-to-all-start = ((bf16[64,8,512]{2,1,0:T(8,128)(2,1)}), bf16[64,8,512]{2,1,0:T(8,128)(2,1)S(1)}, u32[]{:S(2)}, u32[]{:S(2)}) async-start(bf16[64,8,512]{2,1,0:T(8,128)(2,1)} %spread_factors.1), calls=%async_computation | async-start | bytes 1048576 | tf_op jit(solution)/shard_map/all_to_all | solution.py:294
  17.3 5.5 %collective-permute-start.3 = (bf16[4,96,128]{2,1,0:T(8,128)(2,1)}, bf16[4,96,128]{2,1,0:T(8,128)(2,1)S(1)}, u32[]{:S(2)}, u32[]{:S(2)}) collective-permute-start(bf16[4,96,128]{2,1,0:T(8,128)(2,1)} %get-tuple-element.26), channel_id=1, source_target_pairs={{0,1},{1,2},{2,3},{3,0},{4,5},{5,6},{6,7},{7,4},{8,9},{9,10},{10,1... | collective-permute-start | bytes 294920 | tf_op jit(solution)/shard_map/ppermute | solution.py:276
  18.6 7.4 %collective-permute-start.4 = (bf16[4,96,128]{2,1,0:T(8,128)(2,1)}, bf16[4,96,128]{2,1,0:T(8,128)(2,1)S(1)}, u32[]{:S(2)}, u32[]{:S(2)}) collective-permute-start(bf16[4,96,128]{2,1,0:T(8,128)(2,1)} %get-tuple-element.27), channel_id=1, source_target_pairs={{0,2},{1,3},{2,0},{3,1},{4,6},{5,7},{6,4},{7,5},{8,10},{9,11},{10,... | collective-permute-start | bytes 294920 | tf_op jit(solution)/shard_map/ppermute | solution.py:276
  21.2 4.8 %collective-permute-start.5 = (bf16[4,96,128]{2,1,0:T(8,128)(2,1)}, bf16[4,96,128]{2,1,0:T(8,128)(2,1)S(1)}, u32[]{:S(2)}, u32[]{:S(2)}) collective-permute-start(bf16[4,96,128]{2,1,0:T(8,128)(2,1)} %get-tuple-element.28), channel_id=1, source_target_pairs={{0,3},{1,0},{2,1},{3,2},{4,7},{5,4},{6,5},{7,6},{8,11},{9,8},{10,9... | collective-permute-start | bytes 294920 | tf_op jit(solution)/shard_map/ppermute | solution.py:276
  22.8 3.2 %copy-start.5 = (bf16[4,96,128]{2,1,0:T(8,128)(2,1)}, bf16[4,96,128]{2,1,0:T(8,128)(2,1)S(1)}, u32[]{:S(2)}) copy-start(bf16[4,96,128]{2,1,0:T(8,128)(2,1)S(1)} %collective-permute-done.3.in1) | copy-start | bytes 294916
  26.0 0.6 copy-start.6
  26.0 0.7 copy-start.7
  28.5 11.1 %collective-permute-start.6 = (bf16[4,96,128]{2,1,0:T(8,128)(2,1)}, bf16[4,96,128]{2,1,0:T(8,128)(2,1)S(1)}, u32[]{:S(2)}, u32[]{:S(2)}) collective-permute-start(bf16[4,96,128]{2,1,0:T(8,128)(2,1)} %get-tuple-element.30), channel_id=1, source_target_pairs={{0,4},{4,8},{8,12},{12,0},{1,5},{5,9},{9,13},{13,1},{2,6},{6,10},{... | collective-permute-start | bytes 294920 | tf_op jit(solution)/shard_map/ppermute | solution.py:276
  30.9 11.0 %collective-permute-start.7 = (bf16[4,96,128]{2,1,0:T(8,128)(2,1)}, bf16[4,96,128]{2,1,0:T(8,128)(2,1)S(1)}, u32[]{:S(2)}, u32[]{:S(2)}) collective-permute-start(bf16[4,96,128]{2,1,0:T(8,128)(2,1)} %get-tuple-element.31), channel_id=1, source_target_pairs={{0,8},{4,12},{8,0},{12,4},{1,9},{5,13},{9,1},{13,5},{2,10},{6,14},... | collective-permute-start | bytes 294920 | tf_op jit(solution)/shard_map/ppermute | solution.py:276
  34.4 10.7 %collective-permute-start.8 = (bf16[4,96,128]{2,1,0:T(8,128)(2,1)}, bf16[4,96,128]{2,1,0:T(8,128)(2,1)S(1)}, u32[]{:S(2)}, u32[]{:S(2)}) collective-permute-start(bf16[4,96,128]{2,1,0:T(8,128)(2,1)} %get-tuple-element.32), channel_id=1, source_target_pairs={{0,12},{4,0},{8,4},{12,8},{1,13},{5,1},{9,5},{13,9},{2,14},{6,2},{... | collective-permute-start | bytes 294920 | tf_op jit(solution)/shard_map/ppermute | solution.py:276
  37.6 22.6 %collective-permute-start.2 = (bf16[4,128,512]{2,1,0:T(8,128)(2,1)S(1)}, bf16[4,128,512]{2,1,0:T(8,128)(2,1)S(1)}, u32[]{:S(2)}, u32[]{:S(2)}) collective-permute-start(bf16[4,128,512]{2,1,0:T(8,128)(2,1)S(1)} %bitcast.6), channel_id=1, source_target_pairs={{0,3},{1,0},{2,1},{3,2},{4,7},{5,4},{6,5},{7,6},{8,11},{9,8},{10,9... | collective-permute-start | bytes 1572872 | tf_op jit(solution)/shard_map/ppermute | solution.py:276
  39.1 21.1 %collective-permute-start.1 = (bf16[4,128,512]{2,1,0:T(8,128)(2,1)S(1)}, bf16[4,128,512]{2,1,0:T(8,128)(2,1)S(1)}, u32[]{:S(2)}, u32[]{:S(2)}) collective-permute-start(bf16[4,128,512]{2,1,0:T(8,128)(2,1)S(1)} %bitcast.7), channel_id=1, source_target_pairs={{0,2},{1,3},{2,0},{3,1},{4,6},{5,7},{6,4},{7,5},{8,10},{9,11},{10,... | collective-permute-start | bytes 1572872 | tf_op jit(solution)/shard_map/ppermute | solution.py:276
  39.6 26.1 %collective-permute-start = (bf16[4,128,512]{2,1,0:T(8,128)(2,1)S(1)}, bf16[4,128,512]{2,1,0:T(8,128)(2,1)S(1)}, u32[]{:S(2)}, u32[]{:S(2)}) collective-permute-start(bf16[4,128,512]{2,1,0:T(8,128)(2,1)S(1)} %bitcast.8), channel_id=1, source_target_pairs={{0,1},{1,2},{2,3},{3,0},{4,5},{5,6},{6,7},{7,4},{8,9},{9,10},{10,1... | collective-permute-start | bytes 1572872 | tf_op jit(solution)/shard_map/ppermute | solution.py:276
  45.0 0.9 copy-start.3
  65.7 20.7 %copy-start.2 = (bf16[256,256]{1,0:T(8,128)(2,1)S(1)}, bf16[256,256]{1,0:T(8,128)(2,1)}, u32[]{:S(2)}) copy-start(bf16[256,256]{1,0:T(8,128)(2,1)} %constant.11.clone.rows_ref) | copy-start | bytes 393220
  65.7 20.7 %copy-start.4 = (bf16[128,128]{1,0:T(8,128)(2,1)S(1)}, bf16[128,128]{1,0:T(8,128)(2,1)}, u32[]{:S(2)}) copy-start(bf16[128,128]{1,0:T(8,128)(2,1)} %constant.10.clone.halves_ref) | copy-start | bytes 98308
  84.5 4.7 %collective-permute-start.9 = (bf16[8,64,1024]{2,1,0:T(8,128)(2,1)S(1)}, bf16[8,64,1024]{2,1,0:T(8,128)(2,1)S(1)}, u32[]{:S(2)}, u32[]{:S(2)}) collective-permute-start(bf16[8,64,1024]{2,1,0:T(8,128)(2,1)S(1)} %all_to_all.26.own_ref), channel_id=1, source_target_pairs={{0,16},{16,0},{1,17},{17,1},{2,18},{18,2},{3,19},{19,3},{4,20},{20... | collective-permute-start | bytes 3145736 | tf_op jit(solution)/shard_map/ppermute | solution.py:280
  91.7 2.0 %collective-permute-start.11 = (bf16[4,64,1024]{2,1,0:T(8,128)(2,1)S(1)}, bf16[4,64,1024]{2,1,0:T(8,128)(2,1)S(1)}, u32[]{:S(2)}, u32[]{:S(2)}) collective-permute-start(bf16[4,64,1024]{2,1,0:T(8,128)(2,1)S(1)} %ladder_more.1), channel_id=1, source_target_pairs={{0,16},{16,0},{1,17},{17,1},{2,18},{18,2},{3,19},{19,3},{4,20},{20... | collective-permute-start | bytes 1572872 | tf_op jit(solution)/shard_map/ppermute | solution.py:280
  91.8 2.6 %collective-permute-start.10 = (bf16[4,64,1024]{2,1,0:T(8,128)(2,1)S(1)}, bf16[4,64,1024]{2,1,0:T(8,128)(2,1)S(1)}, u32[]{:S(2)}, u32[]{:S(2)}) collective-permute-start(bf16[4,64,1024]{2,1,0:T(8,128)(2,1)S(1)} %get-tuple-element.38), channel_id=1, source_target_pairs={{0,16},{16,0},{1,17},{17,1},{2,18},{18,2},{3,19},{19,3},{4,20},{20... | collective-permute-start | bytes 1572872 | tf_op jit(solution)/shard_map/ppermute | solution.py:280

commit v10 on v9

--- a/solution.py
+++ b/solution.py
@@ -189,14 +189,14 @@
                 left_ref[x * 2 + zl, core] = part[at : at + 64]
 
 
-def _second_step(left_ref, core, inner_ref, out_ref, halves):
-    for at, x in enumerate(halves):
+def _second_step(left_ref, core, inner_ref, out_ref):
+    for x in range(2):
         rows = jnp.concatenate([left_ref[x * 4 + chip, core] for chip in range(4)], axis=0)
         for j in range(4):
             cols = slice(j * 256, j * 256 + 256)
             part = _perm(rows, inner_ref[:, cols])
             for chip in range(4):
-                out_ref[at * 4 + chip, :, cols] = part[chip * 64 : chip * 64 + 64]
+                out_ref[x * 4 + chip, :, cols] = part[chip * 64 : chip * 64 + 64]
 
 
 def _first_step(amp_ref, right_ref, put):
@@ -226,15 +226,11 @@
             inner_ref[at + 64 : at + 128, cols] = jnp.where(first, other, own)
 
     _first_step(other_ref, right_ref, put)
-    _second_step(left_ref, 1 - core, inner_ref, give_ref, (0,))
-
-
-def _more_kernel(left_ref, inner_ref, give_ref):
-    _second_step(left_ref, 1 - lax.axis_index("core"), inner_ref, give_ref, (1,))
+    _second_step(left_ref, 1 - core, inner_ref, give_ref)
 
 
 def _rest_kernel(left_ref, inner_ref, keep_ref):
-    _second_step(left_ref, lax.axis_index("core"), inner_ref, keep_ref, (0, 1))
+    _second_step(left_ref, lax.axis_index("core"), inner_ref, keep_ref)
 
 
 def _sum_kernel(part_ref, kept_ref, small_ref, sent_ref):
@@ -359,20 +355,12 @@
     )(own, right)
     inner, give = pl.pallas_call(
         _ladder_kernel,
-        out_shape=(_sds(1024, 1024), _sds(4, 64, 1024)),
+        out_shape=(_sds(1024, 1024), _sds(8, 64, 1024)),
         in_specs=[_vmem()] * 4,
         out_specs=(_vmem(), _vmem()),
         compiler_params=VMEM,
         name="ladder",
     )(other, right, left, part)
-    more = pl.pallas_call(
-        _more_kernel,
-        out_shape=_sds(4, 64, 1024),
-        in_specs=[_vmem()] * 2,
-        out_specs=_vmem(),
-        compiler_params=VMEM,
-        name="ladder_more",
-    )(left, inner)
     keep = pl.pallas_call(
         _rest_kernel,
         out_shape=_sds(8, 64, 1024),
@@ -381,7 +369,7 @@
         compiler_params=VMEM,
         name="ladder_rest",
     )(left, inner)
-    taken = jnp.concatenate([_swap_cores(give), _swap_cores(more)], axis=0)
+    taken = _swap_cores(give)
     partial = (keep.astype(F32) + taken.astype(F32)).astype(BF16)
     parts = lax.all_to_all(partial, CHIPS, 0, 0, tiled=True)
     last = pl.pallas_call(

time: 128 us -> 128 us (level)
    pallas_call x2 -> x1, Pallas kernels: 2.57 us -> 2.41 us  [_shards(): pl.pallas_call(_ladder_kernel, out_shape=(_sds(1024, 1024), _sds(8, 64, 1...]
  transfers between devices with their start and end apart: 13 -> 12, of which waited for: 7 -> 6; matrix products, arithmetic and copies ran while one was open for 0% -> 0% of each run, Pallas kernels for 8% -> 8%
where the time goes in v10:
time: 128 us
  blocking collectives  61.6 us (48%)
  starting transfers between devices  31.9 us (25%)
  Pallas kernels  16.7 us (13%)
  waiting for transfers between devices  15.3 us (12%)
  local copies, waits for them, and re-layouts  1.58 us (1%)
    all_to_all x1, blocking collectives, _shards(): own = lax.all_to_all(block, CHIPS, 0, 0, tiled=True)  18.8 us
    all_to_all x1, blocking collectives, _shards(): parts = lax.all_to_all(partial, CHIPS, 0, 0, tiled=True)  18.1 us
    ppermute x9, starting transfers between devices, _turn(): return lax.ppermute(value, axis, [(i, (i + step) % 4) for i in range(4)])  16.9 us
    ppermute x9, waiting for transfers between devices, _turn(): return lax.ppermute(value, axis, [(i, (i + step) % 4) for i in range(4)])  13.9 us
    all_to_all x1, starting transfers between devices, _shards(): lax.all_to_all(spread, ('zh',) + ROWS, 0, 0, tiled=True)  13 us
    all_to_all x1, blocking collectives, _shards(): back = lax.all_to_all(last, COLS, 0, 0, tiled=True)  12.5 us
    all_to_all x1, blocking collectives, _shards(): turn = lax.all_to_all(turn, ROWS, 0, 0, tiled=True)  12.2 us
  transfers between devices with their start and end apart: 12, of which 6 were waited for; matrix products, arithmetic and copies ran while one was open for 0% of the time, Pallas kernels for 8%

profile of v10, /device:TPU:1, one launch (start us, length us, event | category | flops | bytes accessed | tf_op | source)
XLA Modules:
  0.0 127.6 jit_solution(14191375224070911750)
XLA Ops:
  0.0 0.0 copy-start.1
  0.0 0.0 copy-start
  0.0 1.9 %spread_factors.1 = bf16[64,8,512]{2,1,0:T(8,128)(2,1)} custom-call(bf16[16,4,1024]{2,1,0:T(4,128)(2,1)} %fac_ref.1), custom_call_target="tpu_custom_call" | custom-call | tf_op jit(solution)/shard_map/spread_factors/pallas_call | solution.py:281
  1.9 13.0 %all-to-all-start = ((bf16[64,8,512]{2,1,0:T(8,128)(2,1)}), bf16[64,8,512]{2,1,0:T(8,128)(2,1)S(1)}, u32[]{:S(2)}, u32[]{:S(2)}) async-start(bf16[64,8,512]{2,1,0:T(8,128)(2,1)} %spread_factors.1), calls=%async_computation | async-start | bytes 1048576 | tf_op jit(solution)/shard_map/all_to_all | solution.py:290
  15.0 2.3 %mask_amps.1 = (bf16[16,64,128]{2,1,0:T(8,128)(2,1)}, f32[16,128]{1,0:T(8,128)}, f32[32,128]{1,0:T(8,128)}, bf16[4,96,128]{2,1,0:T(8,128)(2,1)}, bf16[4,96,128]{...) custom-call(bf16[16,4096]{1,0:T(8,128)(2,1)} %bitcast.10, bf16[16,4096]{1,0:T(8,128)(2,1)} %bitcast.11, ...), custom_call_target="tpu_custom_call" | custom-call | tf_op jit(solution)/shard_map/mask_amps/pallas_call | solution.py:292
  17.3 1.3 %collective-permute-start.3 = (bf16[4,96,128]{2,1,0:T(8,128)(2,1)}, bf16[4,96,128]{2,1,0:T(8,128)(2,1)S(1)}, u32[]{:S(2)}, u32[]{:S(2)}) collective-permute-start(bf16[4,96,128]{2,1,0:T(8,128)(2,1)} %get-tuple-element.26), channel_id=1, source_target_pairs={{0,1},{1,2},{2,3},{3,0},{4,5},{5,6},{6,7},{7,4},{8,9},{9,10},{10,1... | collective-permute-start | bytes 294920 | tf_op jit(solution)/shard_map/ppermute | solution.py:272
  18.6 2.6 %collective-permute-start.4 = (bf16[4,96,128]{2,1,0:T(8,128)(2,1)}, bf16[4,96,128]{2,1,0:T(8,128)(2,1)S(1)}, u32[]{:S(2)}, u32[]{:S(2)}) collective-permute-start(bf16[4,96,128]{2,1,0:T(8,128)(2,1)} %get-tuple-element.27), channel_id=1, source_target_pairs={{0,2},{1,3},{2,0},{3,1},{4,6},{5,7},{6,4},{7,5},{8,10},{9,11},{10,... | collective-permute-start | bytes 294920 | tf_op jit(solution)/shard_map/ppermute | solution.py:272
  21.2 1.1 collective-permute-start.5
  22.3 0.5 collective-permute-done.3.in1
  22.8 0.0 copy-start.5
  22.8 3.2 %collective-permute-done.4.in2 = bf16[4,96,128]{2,1,0:T(8,128)(2,1)S(1)} collective-permute-done((bf16[4,96,128]{2,1,0:T(8,128)(2,1)}, bf16[4,96,128]{2,1,0:T(8,128)(2,1)S(1)}, u32[]{:S(2)}, u32[]{:S(2)}) %collective-permute-start.4) | collective-permute-done | bytes 98336 | tf_op jit(solution)/shard_map/ppermute | solution.py:272
  26.0 0.0 copy-start.6
  26.0 0.0 collective-permute-done.5.in3
  26.0 0.0 copy-start.7
  26.0 0.0 copy-done.5
  26.0 0.6 copy-done.6
  26.6 0.0 copy-done.7
  26.7 1.8 %relay.1 = (bf16[4,96,128]{2,1,0:T(8,128)(2,1)}, bf16[4,96,128]{2,1,0:T(8,128)(2,1)}, bf16[4,96,128]{2,1,0:T(8,128)(2,1)}, bf16[4,96,128]{2,1,0:T(8,128)(2,1)}) custom-call(bf16[4,96,128]{2,1,0:T(8,128)(2,1)} %get-tuple-element.25.in0, bf16[4,96,128]{2,1,0:T(8,128)(2,1)} %copy-done.5, bf16[4,96,128]{2,1,0:T(8,128)(2,1)} %copy-done.6, ...), custom_call_target="tpu_custom_call" | custom-call | tf_op jit(solution)/shard_map/relay/pallas_call | solution.py:301
  28.5 2.4 %collective-permute-start.6 = (bf16[4,96,128]{2,1,0:T(8,128)(2,1)}, bf16[4,96,128]{2,1,0:T(8,128)(2,1)S(1)}, u32[]{:S(2)}, u32[]{:S(2)}) collective-permute-start(bf16[4,96,128]{2,1,0:T(8,128)(2,1)} %get-tuple-element.30), channel_id=1, source_target_pairs={{0,4},{4,8},{8,12},{12,0},{1,5},{5,9},{9,13},{13,1},{2,6},{6,10},{... | collective-permute-start | bytes 294920 | tf_op jit(solution)/shard_map/ppermute | solution.py:272
  30.9 3.5 %collective-permute-start.7 = (bf16[4,96,128]{2,1,0:T(8,128)(2,1)}, bf16[4,96,128]{2,1,0:T(8,128)(2,1)S(1)}, u32[]{:S(2)}, u32[]{:S(2)}) collective-permute-start(bf16[4,96,128]{2,1,0:T(8,128)(2,1)} %get-tuple-element.31), channel_id=1, source_target_pairs={{0,8},{4,12},{8,0},{12,4},{1,9},{5,13},{9,1},{13,5},{2,10},{6,14},... | collective-permute-start | bytes 294920 | tf_op jit(solution)/shard_map/ppermute | solution.py:272
  34.4 3.2 %collective-permute-start.8 = (bf16[4,96,128]{2,1,0:T(8,128)(2,1)}, bf16[4,96,128]{2,1,0:T(8,128)(2,1)S(1)}, u32[]{:S(2)}, u32[]{:S(2)}) collective-permute-start(bf16[4,96,128]{2,1,0:T(8,128)(2,1)} %get-tuple-element.32), channel_id=1, source_target_pairs={{0,12},{4,0},{8,4},{12,8},{1,13},{5,1},{9,5},{13,9},{2,14},{6,2},{... | collective-permute-start | bytes 294920 | tf_op jit(solution)/shard_map/ppermute | solution.py:272
  37.6 0.0 all-to-all-done
  37.6 1.5 %collective-permute-start.2 = (bf16[4,128,512]{2,1,0:T(8,128)(2,1)S(1)}, bf16[4,128,512]{2,1,0:T(8,128)(2,1)S(1)}, u32[]{:S(2)}, u32[]{:S(2)}) collective-permute-start(bf16[4,128,512]{2,1,0:T(8,128)(2,1)S(1)} %bitcast.6), channel_id=1, source_target_pairs={{0,3},{1,0},{2,1},{3,2},{4,7},{5,4},{6,5},{7,6},{8,11},{9,8},{10,9... | collective-permute-start | bytes 1572872 | tf_op jit(solution)/shard_map/ppermute | solution.py:272
  39.1 0.5 collective-permute-start.1
  39.6 0.0 collective-permute-done.6.in1
  39.6 0.8 collective-permute-start
  40.4 1.5 %collective-permute-done.7.in2 = bf16[4,96,128]{2,1,0:T(8,128)(2,1)S(1)} collective-permute-done((bf16[4,96,128]{2,1,0:T(8,128)(2,1)}, bf16[4,96,128]{2,1,0:T(8,128)(2,1)S(1)}, u32[]{:S(2)}, u32[]{:S(2)}) %collective-permute-start.7) | collective-permute-done | bytes 98336 | tf_op jit(solution)/shard_map/ppermute | solution.py:272
  41.9 3.1 %collective-permute-done.8.in3 = bf16[4,96,128]{2,1,0:T(8,128)(2,1)S(1)} collective-permute-done((bf16[4,96,128]{2,1,0:T(8,128)(2,1)}, bf16[4,96,128]{2,1,0:T(8,128)(2,1)S(1)}, u32[]{:S(2)}, u32[]{:S(2)}) %collective-permute-start.8) | collective-permute-done | bytes 98336 | tf_op jit(solution)/shard_map/ppermute | solution.py:272
  45.1 0.0 copy-done.1
  45.1 0.0 copy-done
  45.1 0.0 copy-start.3
  45.1 0.9 copy-done.3
  46.0 1.0 make_block.1
  47.0 12.2 %all_to_all.25.got_ref = bf16[16,64,128]{2,1,0:T(8,128)(2,1)S(1)} all-to-all(bf16[16,64,128]{2,1,0:T(8,128)(2,1)S(1)} %get-tuple-element.33), channel_id=1, replica_groups=mesh['x'=4,'zl'=2,'core'=2,'zh'=4,'y'=4] {'x','zl','core'}, dimensions={0} | all-to-all | bytes 524288 | tf_op jit(solution)/shard_map/all_to_all | solution.py:320
  59.1 1.0 symmetrize.1
  60.2 0.0 collective-permute-done.2.fac3.refs_2_
  60.2 0.0 collective-permute-done.1.fac2.refs_3_
  60.2 5.5 %collective-permute-done.fac1.refs_1_ = bf16[4,128,512]{2,1,0:T(8,128)(2,1)S(1)} collective-permute-done((bf16[4,128,512]{2,1,0:T(8,128)(2,1)S(1)}, bf16[4,128,512]{2,1,0:T(8,128)(2,1)S(1)}, u32[]{:S(2)}, u32[]{:S(2)}) %collective-permute-start) | collective-permute-done | bytes 524320 | tf_op jit(solution)/shard_map/ppermute | solution.py:272
  65.7 0.0 copy-start.2
  65.7 0.0 copy-start.4
  65.7 18.8 %all_to_all.26.own_ref = bf16[8,64,1024]{2,1,0:T(8,128)(2,1)S(1)} all-to-all(bf16[8,64,1024]{2,1,0:T(8,128)(2,1)S(1)} %gate.1), channel_id=1, replica_groups=mesh['x'=4,'zl'=2,'core'=2,'zh'=4,'y'=4] {'x','zl'}, dimensions={0} | all-to-all | bytes 2097152 | tf_op jit(solution)/shard_map/all_to_all | solution.py:338
  84.5 1.9 %collective-permute-start.9 = (bf16[8,64,1024]{2,1,0:T(8,128)(2,1)S(1)}, bf16[8,64,1024]{2,1,0:T(8,128)(2,1)S(1)}, u32[]{:S(2)}, u32[]{:S(2)}) collective-permute-start(bf16[8,64,1024]{2,1,0:T(8,128)(2,1)S(1)} %all_to_all.26.own_ref), channel_id=1, source_target_pairs={{0,16},{16,0},{1,17},{17,1},{2,18},{18,2},{3,19},{19,3},{4,20},{20... | collective-permute-start | bytes 3145736 | tf_op jit(solution)/shard_map/ppermute | solution.py:276
  86.4 0.0 copy-done.2
  86.4 0.0 copy-done.4
  86.4 1.4 %prepare_factors.1 = (bf16[4,4,64,1024]{3,2,1,0:T(8,128)(2,1)S(1)}, bf16[8,2,64,1024]{3,2,1,0:T(8,128)(2,1)S(1)}) custom-call(bf16[4,128,512]{2,1,0:T(8,128)(2,1)S(1)} %bitcast.9, bf16[4,128,512]{2,1,0:T(8,128)(2,1)S(1)} %collective-permute-done.fac1.refs_1_, bf16[4,128,512]{2,1,0:T(8,128)(2,1)S(1)} %collective-permute-done.1.fac2.refs_3_, ...), custom_call_target="tpu_custom_call" | custom-call | tf_op jit(solution)/shard_map/prepare_factors/pallas_call | solution.py:340
  87.9 1.3 %ladder_own.1.part_ref = bf16[8,64,1024]{2,1,0:T(8,128)(2,1)S(1)} custom-call(bf16[8,64,1024]{2,1,0:T(8,128)(2,1)S(1)} %all_to_all.26.own_ref, bf16[4,4,64,1024]{3,2,1,0:T(8,128)(2,1)S(1)} %get-tuple-element.36.right_ref), custom_call_target="tpu_custom_call" | custom-call | tf_op jit(solution)/shard_map/ladder_own/pallas_call | solution.py:348
  89.1 0.0 collective-permute-done.9.other_ref
  89.2 2.4 %ladder.1 = (bf16[1024,1024]{1,0:T(8,128)(2,1)S(1)}, bf16[8,64,1024]{2,1,0:T(8,128)(2,1)S(1)}) custom-call(bf16[8,64,1024]{2,1,0:T(8,128)(2,1)S(1)} %collective-permute-done.9.other_ref, bf16[4,4,64,1024]{3,2,1,0:T(8,128)(2,1)S(1)} %get-tuple-element.36.right_ref, bf16[8,2,64,1024]{3,2,1,0:T(8,128)(2,1)S(1)} %get-tuple-element.24.left_ref, ...), custom_call_target="tpu_custom_call" | custom-call | tf_op jit(solution)/shard_map/ladder/pallas_call | solution.py:356
  91.6 0.1 collective-permute-start.10
  91.7 1.2 ladder_rest.1
  92.9 1.4 %collective-permute-done.10 = bf16[8,64,1024]{2,1,0:T(8,128)(2,1)S(1)} collective-permute-done((bf16[8,64,1024]{2,1,0:T(8,128)(2,1)S(1)}, bf16[8,64,1024]{2,1,0:T(8,128)(2,1)S(1)}, u32[]{:S(2)}, u32[]{:S(2)}) %collective-permute-start.10) | collective-permute-done | bytes 1048608 | tf_op jit(solution)/shard_map/ppermute | solution.py:276
  94.3 0.4 add_convert_fusion
  94.8 18.1 %all_to_all.27.part_ref = bf16[8,64,1024]{2,1,0:T(8,128)(2,1)S(1)} all-to-all(bf16[8,64,1024]{2,1,0:T(8,128)(2,1)S(1)} %add_convert_fusion), channel_id=1, replica_groups=mesh['x'=4,'zl'=2,'core'=2,'zh'=4,'y'=4] {'x','zl'}, dimensions={0} | all-to-all | bytes 2097152 | tf_op jit(solution)/shard_map/all_to_all | solution.py:374
  112.9 0.4 sum_parts.1
  113.3 12.5 %all_to_all.28.resid_ref = bf16[16,32,128]{2,1,0:T(8,128)(2,1)} all-to-all(bf16[16,32,128]{2,1,0:T(8,128)(2,1)S(1)} %sum_parts.1), channel_id=1, replica_groups=mesh['x'=4,'zl'=2,'core'=2,'zh'=4,'y'=4] {'zh','y'}, dimensions={0} | all-to-all | bytes 262144 | tf_op jit(solution)/shard_map/all_to_all | solution.py:383
  125.7 1.9 %update.1 = bf16[16,4096]{1,0:T(8,128)(2,1)} custom-call(f32[4]{0:T(128)} %occ_ref.1, bf16[16,32,128]{2,1,0:T(8,128)(2,1)} %all_to_all.28.resid_ref, bf16[16,64,128]{2,1,0:T(8,128)(2,1)} %get-tuple-element.40.held_ref, f32[16,128]{1,0:T(8,128)} %get-tuple-element.41.mask_ref, f32[32,128]{1,0:T(8,128)} %get-tuple-element.42.vir_ref), custom_call_target="tpu_custom_call" | custom-call | tf_op jit(solution)/shard_map/update/pallas_call | solution.py:384
  (1 shorter events, 0.0 us)
Async XLA Ops:
  0.0 45.1 %copy-start.1 = (bf16[3,64,64]{2,1,0:T(8,128)(2,1)S(1)}, bf16[3,64,64]{2,1,0:T(8,128)(2,1)}, u32[]{:S(2)}) copy-start(bf16[3,64,64]{2,1,0:T(8,128)(2,1)} %constant.8.clone.small_ref) | copy-start | bytes 73732
  0.0 45.1 %copy-start = (bf16[1024,1024]{1,0:T(8,128)(2,1)S(1)}, bf16[1024,1024]{1,0:T(8,128)(2,1)}, u32[]{:S(2)}) copy-start(bf16[1024,1024]{1,0:T(8,128)(2,1)} %constant.9.clone.wide_ref) | copy-start | bytes 6291460
  1.9 35.6 %all-to-all-start = ((bf16[64,8,512]{2,1,0:T(8,128)(2,1)}), bf16[64,8,512]{2,1,0:T(8,128)(2,1)S(1)}, u32[]{:S(2)}, u32[]{:S(2)}) async-start(bf16[64,8,512]{2,1,0:T(8,128)(2,1)} %spread_factors.1), calls=%async_computation | async-start | bytes 1048576 | tf_op jit(solution)/shard_map/all_to_all | solution.py:290
  17.3 5.5 %collective-permute-start.3 = (bf16[4,96,128]{2,1,0:T(8,128)(2,1)}, bf16[4,96,128]{2,1,0:T(8,128)(2,1)S(1)}, u32[]{:S(2)}, u32[]{:S(2)}) collective-permute-start(bf16[4,96,128]{2,1,0:T(8,128)(2,1)} %get-tuple-element.26), channel_id=1, source_target_pairs={{0,1},{1,2},{2,3},{3,0},{4,5},{5,6},{6,7},{7,4},{8,9},{9,10},{10,1... | collective-permute-start | bytes 294920 | tf_op jit(solution)/shard_map/ppermute | solution.py:272
  18.6 7.4 %collective-permute-start.4 = (bf16[4,96,128]{2,1,0:T(8,128)(2,1)}, bf16[4,96,128]{2,1,0:T(8,128)(2,1)S(1)}, u32[]{:S(2)}, u32[]{:S(2)}) collective-permute-start(bf16[4,96,128]{2,1,0:T(8,128)(2,1)} %get-tuple-element.27), channel_id=1, source_target_pairs={{0,2},{1,3},{2,0},{3,1},{4,6},{5,7},{6,4},{7,5},{8,10},{9,11},{10,... | collective-permute-start | bytes 294920 | tf_op jit(solution)/shard_map/ppermute | solution.py:272
  21.2 4.8 %collective-permute-start.5 = (bf16[4,96,128]{2,1,0:T(8,128)(2,1)}, bf16[4,96,128]{2,1,0:T(8,128)(2,1)S(1)}, u32[]{:S(2)}, u32[]{:S(2)}) collective-permute-start(bf16[4,96,128]{2,1,0:T(8,128)(2,1)} %get-tuple-element.28), channel_id=1, source_target_pairs={{0,3},{1,0},{2,1},{3,2},{4,7},{5,4},{6,5},{7,6},{8,11},{9,8},{10,9... | collective-permute-start | bytes 294920 | tf_op jit(solution)/shard_map/ppermute | solution.py:272
  22.8 3.2 %copy-start.5 = (bf16[4,96,128]{2,1,0:T(8,128)(2,1)}, bf16[4,96,128]{2,1,0:T(8,128)(2,1)S(1)}, u32[]{:S(2)}) copy-start(bf16[4,96,128]{2,1,0:T(8,128)(2,1)S(1)} %collective-permute-done.3.in1) | copy-start | bytes 294916
  26.0 0.6 copy-start.6
  26.0 0.7 copy-start.7
  28.5 11.1 %collective-permute-start.6 = (bf16[4,96,128]{2,1,0:T(8,128)(2,1)}, bf16[4,96,128]{2,1,0:T(8,128)(2,1)S(1)}, u32[]{:S(2)}, u32[]{:S(2)}) collective-permute-start(bf16[4,96,128]{2,1,0:T(8,128)(2,1)} %get-tuple-element.30), channel_id=1, source_target_pairs={{0,4},{4,8},{8,12},{12,0},{1,5},{5,9},{9,13},{13,1},{2,6},{6,10},{... | collective-permute-start | bytes 294920 | tf_op jit(solution)/shard_map/ppermute | solution.py:272
  30.9 11.0 %collective-permute-start.7 = (bf16[4,96,128]{2,1,0:T(8,128)(2,1)}, bf16[4,96,128]{2,1,0:T(8,128)(2,1)S(1)}, u32[]{:S(2)}, u32[]{:S(2)}) collective-permute-start(bf16[4,96,128]{2,1,0:T(8,128)(2,1)} %get-tuple-element.31), channel_id=1, source_target_pairs={{0,8},{4,12},{8,0},{12,4},{1,9},{5,13},{9,1},{13,5},{2,10},{6,14},... | collective-permute-start | bytes 294920 | tf_op jit(solution)/shard_map/ppermute | solution.py:272
  34.4 10.7 %collective-permute-start.8 = (bf16[4,96,128]{2,1,0:T(8,128)(2,1)}, bf16[4,96,128]{2,1,0:T(8,128)(2,1)S(1)}, u32[]{:S(2)}, u32[]{:S(2)}) collective-permute-start(bf16[4,96,128]{2,1,0:T(8,128)(2,1)} %get-tuple-element.32), channel_id=1, source_target_pairs={{0,12},{4,0},{8,4},{12,8},{1,13},{5,1},{9,5},{13,9},{2,14},{6,2},{... | collective-permute-start | bytes 294920 | tf_op jit(solution)/shard_map/ppermute | solution.py:272
  37.6 22.6 %collective-permute-start.2 = (bf16[4,128,512]{2,1,0:T(8,128)(2,1)S(1)}, bf16[4,128,512]{2,1,0:T(8,128)(2,1)S(1)}, u32[]{:S(2)}, u32[]{:S(2)}) collective-permute-start(bf16[4,128,512]{2,1,0:T(8,128)(2,1)S(1)} %bitcast.6), channel_id=1, source_target_pairs={{0,3},{1,0},{2,1},{3,2},{4,7},{5,4},{6,5},{7,6},{8,11},{9,8},{10,9... | collective-permute-start | bytes 1572872 | tf_op jit(solution)/shard_map/ppermute | solution.py:272
  39.1 21.1 %collective-permute-start.1 = (bf16[4,128,512]{2,1,0:T(8,128)(2,1)S(1)}, bf16[4,128,512]{2,1,0:T(8,128)(2,1)S(1)}, u32[]{:S(2)}, u32[]{:S(2)}) collective-permute-start(bf16[4,128,512]{2,1,0:T(8,128)(2,1)S(1)} %bitcast.7), channel_id=1, source_target_pairs={{0,2},{1,3},{2,0},{3,1},{4,6},{5,7},{6,4},{7,5},{8,10},{9,11},{10,... | collective-permute-start | bytes 1572872 | tf_op jit(solution)/shard_map/ppermute | solution.py:272
  39.6 26.1 %collective-permute-start = (bf16[4,128,512]{2,1,0:T(8,128)(2,1)S(1)}, bf16[4,128,512]{2,1,0:T(8,128)(2,1)S(1)}, u32[]{:S(2)}, u32[]{:S(2)}) collective-permute-start(bf16[4,128,512]{2,1,0:T(8,128)(2,1)S(1)} %bitcast.8), channel_id=1, source_target_pairs={{0,1},{1,2},{2,3},{3,0},{4,5},{5,6},{6,7},{7,4},{8,9},{9,10},{10,1... | collective-permute-start | bytes 1572872 | tf_op jit(solution)/shard_map/ppermute | solution.py:272
  45.1 0.9 copy-start.3
  65.7 20.7 %copy-start.2 = (bf16[256,256]{1,0:T(8,128)(2,1)S(1)}, bf16[256,256]{1,0:T(8,128)(2,1)}, u32[]{:S(2)}) copy-start(bf16[256,256]{1,0:T(8,128)(2,1)} %constant.11.clone.rows_ref) | copy-start | bytes 393220
  65.7 20.7 %copy-start.4 = (bf16[128,128]{1,0:T(8,128)(2,1)S(1)}, bf16[128,128]{1,0:T(8,128)(2,1)}, u32[]{:S(2)}) copy-start(bf16[128,128]{1,0:T(8,128)(2,1)} %constant.10.clone.halves_ref) | copy-start | bytes 98308
  84.5 4.7 %collective-permute-start.9 = (bf16[8,64,1024]{2,1,0:T(8,128)(2,1)S(1)}, bf16[8,64,1024]{2,1,0:T(8,128)(2,1)S(1)}, u32[]{:S(2)}, u32[]{:S(2)}) collective-permute-start(bf16[8,64,1024]{2,1,0:T(8,128)(2,1)S(1)} %all_to_all.26.own_ref), channel_id=1, source_target_pairs={{0,16},{16,0},{1,17},{17,1},{2,18},{18,2},{3,19},{19,3},{4,20},{20... | collective-permute-start | bytes 3145736 | tf_op jit(solution)/shard_map/ppermute | solution.py:276
  91.6 2.7 %collective-permute-start.10 = (bf16[8,64,1024]{2,1,0:T(8,128)(2,1)S(1)}, bf16[8,64,1024]{2,1,0:T(8,128)(2,1)S(1)}, u32[]{:S(2)}, u32[]{:S(2)}) collective-permute-start(bf16[8,64,1024]{2,1,0:T(8,128)(2,1)S(1)} %get-tuple-element.38), channel_id=1, source_target_pairs={{0,16},{16,0},{1,17},{17,1},{2,18},{18,2},{3,19},{19,3},{4,20},{20... | collective-permute-start | bytes 3145736 | tf_op jit(solution)/shard_map/ppermute | solution.py:276
